TPU v7x, 32 devices: a whole 2x2x4 slice. The times are simulated.
32 devices in a mesh: dp: 16 (over z, y, core), qry: 2 (over x).
Axes of the slice: x: 2, y: 2, z: 4, core: 2. Of those that a mesh axis runs over, the one named last changes fastest.
Arguments:
- queries: bfloat16 [16, 128, 768], P('dp', 'qry'), may hold values from -6 to 6
- latents: bfloat16 [16, 128, 768], P('dp', 'qry'), may hold values from -6 to 6
- positions: int32 [16, 128], P('dp', 'qry'), may hold values from 0 to 195
- visible_valid: int32 [16, 128], P('dp'), may hold values from 0 to 1, as said below
- masked_valid: int32 [16, 128], P('dp'), may hold values from 0 to 1, as said below
- w_query: bfloat16 [768, 768], replicated, may hold values from -0.3125 to 0.3125
- b_query: float32 [768], replicated, may hold values from -3 to 3
- w_key: bfloat16 [768, 768], replicated, may hold values from -0.21875 to 0.21875
- w_value: bfloat16 [768, 768], replicated, may hold values from -0.21875 to 0.21875
- b_value: float32 [768], replicated, may hold values from -3 to 3
- w_out: bfloat16 [768, 768], replicated, may hold values from -0.875 to 0.875
- b_out: float32 [768], replicated, may hold values from -3 to 3
- w_fc1: bfloat16 [768, 3072], replicated, may hold values from -0.21875 to 0.21875
- b_fc1: float32 [3072], replicated, may hold values from -3 to 3
- w_fc2: bfloat16 [3072, 768], replicated, may hold values from -0.109375 to 0.109375
- b_fc2: float32 [768], replicated, may hold values from -3 to 3
- gain_query: float32 [768], replicated, may hold values from 0.25 to 1.75
- shift_query: float32 [768], replicated, may hold values from -2 to 2
- gain_keys: float32 [768], replicated, may hold values from 0.25 to 1.75
- shift_keys: float32 [768], replicated, may hold values from -2 to 2
- gain_mlp: float32 [768], replicated, may hold values from 0.25 to 1.75
- shift_mlp: float32 [768], replicated, may hold values from -2 to 2
- scale_attn: float32 [768], replicated, may hold values from 0.25 to 1.75
- scale_mlp: float32 [768], replicated, may hold values from 0.25 to 1.75
- out_grad: bfloat16 [16, 128, 768], P('dp', 'qry'), may hold values from -6 to 6
Outputs:
- block_out: bfloat16 [16, 128, 768], P('dp', 'qry')
- grad_queries: float32 [16, 128, 768], P('dp', 'qry')
- grad_latents: float32 [16, 128, 768], P('dp', 'qry')
- grad_w_query: float32 [768, 768], P('dp', 'qry')
- grad_b_query: float32 [768], replicated
- grad_w_key: float32 [768, 768], P('dp', 'qry')
- grad_w_value: float32 [768, 768], P('dp', 'qry')
- grad_b_value: float32 [768], replicated
- grad_w_out: float32 [768, 768], P('dp', 'qry')
- grad_b_out: float32 [768], replicated
- grad_w_fc1: float32 [768, 3072], P('dp', 'qry')
- grad_b_fc1: float32 [3072], replicated
- grad_w_fc2: float32 [3072, 768], P('dp', 'qry')
- grad_b_fc2: float32 [768], replicated
- grad_gain_query: float32 [768], replicated
- grad_shift_query: float32 [768], replicated
- grad_gain_keys: float32 [768], replicated
- grad_shift_keys: float32 [768], replicated
- grad_gain_mlp: float32 [768], replicated
- grad_shift_mlp: float32 [768], replicated
- grad_scale_attn: float32 [768], replicated
- grad_scale_mlp: float32 [768], replicated
Inputs may be any that keep to these rules, and one draw needn't show every extreme that they name: `visible_valid`: in every image the valid visible slots form a leading run of more than 64 slots. `masked_valid`: in every image the valid masked slots form a leading run of more than 64 slots.
All inputs are finite; a program needn't handle non-finite values.
Results may differ from a plain program's by a relative error of at most 0.014.
The roundings to bfloat16 on the way count: a program that leaves them out, or rounds other values in their place, can miss the bound.
Values may be sent and summed in bfloat16 or wider, within the bound.
A program may use at most 128 MiB of HBM per device.

v0:
```python
import math

import jax
import jax.numpy as jnp
from jax import lax
from jax.sharding import PartitionSpec as P

HEAD_DIM = 64


def sinusoid(places, width):
    index = jnp.arange(width)
    freq = jnp.exp(-(2.0 * (index // 2).astype(jnp.float32) / width) * math.log(10000.0))
    angle = places.astype(jnp.float32)[..., None] * freq
    return jnp.where(index % 2 == 0, jnp.sin(angle), jnp.cos(angle))


def layer_norm(x, gain, shift):
    centre = x - jnp.mean(x, axis=-1, keepdims=True)
    spread = jnp.mean(centre * centre, axis=-1, keepdims=True)
    return centre * lax.rsqrt(spread + 1e-06) * gain + shift


def gelu_exact(v):
    return jax.nn.gelu(v, approximate=False)


def matmul(left, weight):
    return jnp.einsum("bnd,df->bnf", left, weight, preferred_element_type=jnp.float32)


def weight_grad(left, right):
    return jnp.einsum("bnd,bnf->df", left, right, preferred_element_type=jnp.float32)


def back_mul(grad, weight):
    return jnp.einsum("bnf,df->bnd", grad, weight, preferred_element_type=jnp.float32)


def row_total(grad):
    return jnp.sum(grad.astype(jnp.float32), axis=(0, 1))


def per_device(
    queries,
    latents,
    positions,
    visible_valid,
    masked_valid,
    w_query,
    b_query,
    w_key,
    w_value,
    b_value,
    w_out,
    b_out,
    w_fc1,
    b_fc1,
    w_fc2,
    b_fc2,
    gain_query,
    shift_query,
    gain_keys,
    shift_keys,
    gain_mlp,
    shift_mlp,
    scale_attn,
    scale_mlp,
    out_grad,
):
    images, half_msk, width = queries.shape
    half_vis = latents.shape[1]
    heads = width // HEAD_DIM
    parts = lax.axis_size("qry")
    scale = 1.0 / math.sqrt(HEAD_DIM)
    bfloat = jnp.bfloat16
    qin = queries.astype(jnp.float32) + sinusoid(positions, width)
    hq_full, pull_query = jax.vjp(layer_norm, qin, gain_query, shift_query)
    hq = hq_full.astype(bfloat)
    source = jnp.concatenate([latents.astype(jnp.float32), qin], axis=1)
    hk_full, pull_keys = jax.vjp(layer_norm, source, gain_keys, shift_keys)
    hk = hk_full.astype(bfloat)
    query = (matmul(hq, w_query) + b_query).astype(bfloat)
    kv_bias = jnp.concatenate([jnp.zeros_like(b_value), b_value])
    piece = lax.all_gather(hk, "qry", axis=1, tiled=True)
    both = jnp.concatenate([matmul(piece, w_key), matmul(piece, w_value)], axis=-1)
    keyval = (both + kv_bias).astype(bfloat)
    total_keys = keyval.shape[1]
    keymask = jnp.concatenate(
        [
            visible_valid.reshape(images, parts, half_vis),
            masked_valid.reshape(images, parts, half_msk),
        ],
        axis=2,
    )
    keymask = keymask.reshape(images, total_keys) > 0
    keys = keyval[..., :width].reshape(images, total_keys, heads, HEAD_DIM)
    values = keyval[..., width:].reshape(images, total_keys, heads, HEAD_DIM)
    qheads = query.reshape(images, half_msk, heads, HEAD_DIM)

    def scores_of():
        raw = (
            jnp.einsum("bmhe,bkhe->bhmk", qheads, keys, preferred_element_type=jnp.float32) * scale
        )
        return jnp.where(keymask[:, None, None, :], raw, -1e30)

    scores = scores_of()
    peak = jnp.max(scores, axis=-1, keepdims=True)
    lse = peak + jnp.log(jnp.sum(jnp.exp(scores - peak), axis=-1, keepdims=True))
    probs = jnp.exp(scores - lse).astype(bfloat)
    attended = jnp.einsum("bhmk,bkhe->bmhe", probs, values, preferred_element_type=jnp.float32)
    attended = attended.reshape(images, half_msk, width).astype(bfloat)
    branch = matmul(attended, w_out) + b_out
    resid = qin + scale_attn * branch
    h_full, pull_mlp = jax.vjp(layer_norm, resid, gain_mlp, shift_mlp)
    h_two = h_full.astype(bfloat)
    pre_act = matmul(h_two, w_fc1) + b_fc1
    act_full, pull_act = jax.vjp(gelu_exact, pre_act)
    act = act_full.astype(bfloat)
    mlp_out = matmul(act, w_fc2) + b_fc2
    block_out = (resid + scale_mlp * mlp_out).astype(bfloat)
    grad_y = out_grad.astype(jnp.float32)
    d_mlp = (scale_mlp * grad_y).astype(bfloat)
    g_scale_mlp = jnp.sum(grad_y * mlp_out, axis=(0, 1))
    g_b_fc2 = row_total(d_mlp)
    g_w_fc2 = weight_grad(act, d_mlp)
    d_pre = pull_act(back_mul(d_mlp, w_fc2))[0].astype(bfloat)
    g_b_fc1 = row_total(d_pre)
    g_w_fc1 = weight_grad(h_two, d_pre)
    d_resid_norm, g_gain_mlp, g_shift_mlp = pull_mlp(back_mul(d_pre, w_fc1))
    d_resid = grad_y + d_resid_norm
    d_branch = (scale_attn * d_resid).astype(bfloat)
    g_scale_attn = jnp.sum(d_resid * branch, axis=(0, 1))
    g_b_out = row_total(d_branch)
    g_w_out = weight_grad(attended, d_branch)
    d_att = back_mul(d_branch, w_out).astype(bfloat).reshape(images, half_msk, heads, HEAD_DIM)
    prob_full = jnp.exp(scores_of() - lse)
    d_prob = jnp.einsum("bmhe,bkhe->bhmk", d_att, values, preferred_element_type=jnp.float32)
    delta = jnp.sum(d_prob * prob_full, axis=-1, keepdims=True)
    d_scores = (prob_full * (d_prob - delta)).astype(bfloat)
    d_query = (
        jnp.einsum("bhmk,bkhe->bmhe", d_scores, keys, preferred_element_type=jnp.float32) * scale
    )
    d_query = d_query.reshape(images, half_msk, width).astype(bfloat)
    d_keys = (
        jnp.einsum("bhmk,bmhe->bkhe", d_scores, qheads, preferred_element_type=jnp.float32) * scale
    )
    d_values = jnp.einsum("bhmk,bmhe->bkhe", probs, d_att, preferred_element_type=jnp.float32)
    d_pair = jnp.concatenate(
        [d_keys.reshape(images, total_keys, width), d_values.reshape(images, total_keys, width)],
        axis=-1,
    )
    d_local = lax.psum_scatter(d_pair, "qry", scatter_dimension=1, tiled=True).astype(bfloat)
    d_key_rows = d_local[..., :width]
    d_value_rows = d_local[..., width:]
    g_b_value = row_total(d_value_rows)
    g_w_key = weight_grad(hk, d_key_rows)
    g_w_value = weight_grad(hk, d_value_rows)
    d_hk = back_mul(d_key_rows, w_key) + back_mul(d_value_rows, w_value)
    d_source, g_gain_keys, g_shift_keys = pull_keys(d_hk)
    g_b_query = row_total(d_query)
    g_w_query = weight_grad(hq, d_query)
    d_qnorm, g_gain_query, g_shift_query = pull_query(back_mul(d_query, w_query))
    grad_queries = d_resid + d_qnorm + d_source[:, half_vis:]
    grad_latents = d_source[:, :half_vis]
    matrices = (g_w_query, g_w_key, g_w_value, g_w_out, g_w_fc1, g_w_fc2)
    matrices = (
        lax.psum_scatter(matrices[0], "dp", scatter_dimension=0, tiled=True),
        lax.psum_scatter(matrices[1], "dp", scatter_dimension=0, tiled=True),
        lax.psum_scatter(matrices[2], "dp", scatter_dimension=0, tiled=True),
        lax.psum_scatter(matrices[3], "dp", scatter_dimension=0, tiled=True),
        lax.psum_scatter(matrices[4], "dp", scatter_dimension=0, tiled=True),
        lax.psum_scatter(matrices[5], "dp", scatter_dimension=0, tiled=True),
    )
    matrices = (
        lax.psum_scatter(matrices[0], "qry", scatter_dimension=1, tiled=True),
        lax.psum_scatter(matrices[1], "qry", scatter_dimension=1, tiled=True),
        lax.psum_scatter(matrices[2], "qry", scatter_dimension=1, tiled=True),
        lax.psum_scatter(matrices[3], "qry", scatter_dimension=1, tiled=True),
        lax.psum_scatter(matrices[4], "qry", scatter_dimension=1, tiled=True),
        lax.psum_scatter(matrices[5], "qry", scatter_dimension=1, tiled=True),
    )
    vectors = lax.psum(
        (
            g_b_query,
            g_b_value,
            g_b_out,
            g_b_fc1,
            g_b_fc2,
            g_gain_query,
            g_shift_query,
            g_gain_keys,
            g_shift_keys,
            g_gain_mlp,
            g_shift_mlp,
            g_scale_attn,
            g_scale_mlp,
        ),
        ("dp", "qry"),
    )
    return (
        block_out,
        grad_queries,
        grad_latents,
        matrices[0],
        vectors[0],
        matrices[1],
        matrices[2],
        vectors[1],
        matrices[3],
        vectors[2],
        matrices[4],
        vectors[3],
        matrices[5],
        vectors[4],
        vectors[5],
        vectors[6],
        vectors[7],
        vectors[8],
        vectors[9],
        vectors[10],
        vectors[11],
        vectors[12],
    )


def solution(mesh):
    return jax.shard_map(
        per_device,
        mesh=mesh,
        in_specs=(
            P("dp", "qry", None),
            P("dp", "qry", None),
            P("dp", "qry"),
            P("dp", None),
            P("dp", None),
            P(),
            P(),
            P(),
            P(),
            P(),
            P(),
            P(),
            P(),
            P(),
            P(),
            P(),
            P(),
            P(),
            P(),
            P(),
            P(),
            P(),
            P(),
            P(),
            P("dp", "qry", None),
        ),
        out_specs=(
            P("dp", "qry", None),
            P("dp", "qry", None),
            P("dp", "qry", None),
            P("dp", "qry"),
            P(),
            P("dp", "qry"),
            P("dp", "qry"),
            P(),
            P("dp", "qry"),
            P(),
            P("dp", "qry"),
            P(),
            P("dp", "qry"),
            P(),
            P(),
            P(),
            P(),
            P(),
            P(),
            P(),
            P(),
            P(),
        ),
        check_vma=False,
    )
```

profile of v0, /device:TPU:0, one launch (start us, length us, event | category | flops | bytes accessed | tf_op | source)
XLA Modules:
  0.0 673.8 jit_solution(2359068983958507255)
XLA Ops:
  7.3 0.7 convert_bitcast_fusion.1
  8.6 1.3 reduce.40
  9.9 1.3 reduce.39
  11.4 1.8 fusion.72
  13.2 1.8 multiply_reduce_fusion.5
  15.1 2.4 fusion.4
  17.5 0.8 copy.62
  19.7 8.8 %all_gather.3 = bf16[1,256,768]{2,1,0:T(8,128)(2,1)S(1)} all-gather(bf16[1,128,768]{2,1,0:T(8,128)(2,1)S(1)} %add_convert_fusion.2), channel_id=1, replica_groups=mesh['dp'=16,'qry'=2] {'qry'}, dimensions={1}, use_global_device_ids=true | all-gather | bytes 589824 | tf_op jit(solution)/shard_map/all_gather | solution.py:85
  29.9 0.9 copy.56
  30.8 0.9 copy.55
  31.8 1.5 fusion.79
  34.2 1.8 fusion.76
  36.2 3.5 convolution_add_fusion
  39.8 3.2 convert_reduce_fusion
  43.1 2.2 fusion.20
  48.1 1.1 convolution_convert_fusion.1
  49.3 1.7 copy.63
  51.0 1.5 multiply_reduce_fusion
  53.2 0.7 copy-done.5
  54.2 1.3 pad_maximum_fusion
  55.5 0.8 copy-done.16
  56.4 1.8 fusion.37
  58.3 0.9 copy-done.3
  59.4 0.9 convert_reduce_fusion.2
  60.5 3.7 fusion.65
  65.2 2.9 fusion.21
  68.7 2.1 fusion.74
  70.8 12.3 %reduce-scatter.14.cloned.1.call-done = f32[1,128,1536]{1,2,0:T(8,128)} async-done(((f32[1,256,1536]{1,2,0:T(8,128)}), f32[1,128,1536]{1,2,0:T(8,128)}) %reduce-scatter.14.cloned.1.call-update) | async-done | bytes 786448 | tf_op jit(solution)/shard_map/reduce_scatter | solution.py:153
  83.2 1.2 convert_element_type.177
  84.4 2.0 fusion.28
  86.5 2.0 fusion.22
  88.6 0.8 copy-done.33
  89.4 7.8 %fusion.40 = f32[3072,768]{1,0:T(8,128)} fusion(bf16[1,64,768]{2,1,0:T(8,128)(2,1)S(1)} %copy-done.33, f32[768]{0:T(1024)S(1)} %copy-done.79, f32[64,3072]{1,0:T(8,128)} %copy-done.22), kind=kOutput, calls=%fused_computation.102 | convolution fusion | flops 314916864 | bytes 10324992 | tf_op jit(solution)/shard_map/bnd,bnf->df/dot_general | solution.py:33
  97.9 6.1 fusion.62
  104.1 46.3 %reduce-scatter.28.cloned.1.call-done = f32[48,768]{1,0:T(8,128)} async-done(((f32[768,768]{1,0:T(8,128)}), f32[48,768]{1,0:T(8,128)}) %reduce-scatter.28.cloned.1.call-update) | async-done | bytes 147472 | tf_op jit(solution)/shard_map/reduce_scatter | solution.py:171
  150.5 65.7 %reduce-scatter.16.cloned.1.call-done = f32[48,768]{1,0:T(8,128)} async-done(((f32[768,768]{1,0:T(8,128)}), f32[48,768]{1,0:T(8,128)}) %reduce-scatter.16.cloned.1.call-update) | async-done | bytes 147472 | tf_op jit(solution)/shard_map/reduce_scatter | solution.py:168
  216.3 66.0 %reduce-scatter.20.cloned.1.call-done = f32[48,768]{1,0:T(8,128)} async-done(((f32[768,768]{1,0:T(8,128)}), f32[48,768]{1,0:T(8,128)}) %reduce-scatter.20.cloned.1.call-update) | async-done | bytes 147472 | tf_op jit(solution)/shard_map/reduce_scatter | solution.py:169
  282.3 65.5 %reduce-scatter.24.cloned.1.call-done = f32[48,768]{1,0:T(8,128)} async-done(((f32[768,768]{1,0:T(8,128)}), f32[48,768]{1,0:T(8,128)}) %reduce-scatter.24.cloned.1.call-update) | async-done | bytes 147472 | tf_op jit(solution)/shard_map/reduce_scatter | solution.py:170
  347.9 114.8 %reduce-scatter.36.cloned.1.call-done = f32[192,768]{1,0:T(8,128)} async-done(((f32[3072,768]{1,0:T(8,128)}), f32[192,768]{1,0:T(8,128)}) %reduce-scatter.36.cloned.1.call-update) | async-done | bytes 589840 | tf_op jit(solution)/shard_map/reduce_scatter | solution.py:173
  462.8 1.2 negate_multiply_fusion.2
  464.6 1.5 reduce_sum.314
  468.9 109.1 %reduce-scatter.32.cloned.1.call-done = f32[48,3072]{1,0:T(8,128)} async-done(((f32[768,3072]{1,0:T(8,128)}), f32[48,3072]{1,0:T(8,128)}) %reduce-scatter.32.cloned.1.call-update) | async-done | bytes 589840 | tf_op jit(solution)/shard_map/reduce_scatter | solution.py:172
  578.8 0.8 add_bitcast_fusion
  579.7 5.6 fusion.78
  585.4 42.2 %all-reduce.1 = (f32[768]{0:T(1024)}, f32[768]{0:T(1024)}, f32[768]{0:T(1024)}, f32[3072]{0:T(1024)}, f32[768]{0:T(1024)}, /*index=5*/f32[768]{0:T(1024)}, f32[7...) all-reduce(f32[768]{0:T(1024)S(1)} %copy-done.53, ...), channel_id=1, replica_groups=mesh['dp'=16,'qry'=2] {'dp','qry'}, use_global_device_ids=true, to_apply=%region_19.20 | all-reduce | flops 12288 | bytes 98304 | tf_op jit(solution)/shard_map/psum | solution.py:183
  627.6 3.5 reduce-scatter.26.cloned.1.call-done
  631.1 18.1 %reduce-scatter.38.cloned.1.call-done = f32[192,384]{1,0:T(8,128)} async-done(((f32[192,768]{1,0:T(8,128)}), f32[192,384]{1,0:T(8,128)}) %reduce-scatter.38.cloned.1.call-update) | async-done | bytes 294928 | tf_op jit(solution)/shard_map/reduce_scatter | solution.py:181
  649.1 18.1 %reduce-scatter.34.cloned.1.call-done = f32[48,1536]{1,0:T(8,128)} async-done(((f32[48,3072]{1,0:T(8,128)}), f32[48,1536]{1,0:T(8,128)}) %reduce-scatter.34.cloned.1.call-update) | async-done | bytes 294928 | tf_op jit(solution)/shard_map/reduce_scatter | solution.py:180
  (233 shorter events, 15.6 us)
Async XLA Ops:
  7.2 21.3 %copy-start = (bf16[768,768]{1,0:T(8,128)(2,1)S(1)}, bf16[768,768]{1,0:T(8,128)(2,1)}, u32[]{:S(2)}) copy-start(bf16[768,768]{1,0:T(8,128)(2,1)} %param.33) | copy-start | bytes 3538948
  7.2 11.1 %copy-start.34 = (bf16[1,64,768]{2,1,0:T(8,128)(2,1)S(1)}, bf16[1,64,768]{2,1,0:T(8,128)(2,1)}, u32[]{:S(2)}) copy-start(bf16[1,64,768]{2,1,0:T(8,128)(2,1)} %param.26) | copy-start | bytes 294916
  7.2 76.0 %reduce-scatter.14.cloned.1.call-start = ((), (), s32[]{:S(2)}) async-start(), calls=%async_computation.13 | async-start | bytes 2359296 | tf_op jit(solution)/shard_map/reduce_scatter | solution.py:153
  7.3 10.2 %copy-start.39 = (pred[768]{0:T(1024)(128)(4,1)}, pred[768]{0:T(1024)(128)(4,1)S(1)}, u32[]{:S(2)}) copy-start(pred[768]{0:T(1024)(128)(4,1)S(1)} %fusion.48) | copy-start | bytes 2308
  7.3 10.2 %copy-start.27 = (f32[768]{0:T(1024)}, f32[768]{0:T(1024)S(1)}, u32[]{:S(2)}) copy-start(f32[768]{0:T(1024)S(1)} %fusion.54) | copy-start | bytes 9220
  8.1 9.4 %copy-start.55 = (f32[64]{0:T(128)}, f32[64]{0:T(128)S(1)}, u32[]{:S(2)}) copy-start(f32[64]{0:T(128)S(1)} %convert_bitcast_fusion.1) | copy-start | bytes 772
  13.2 4.3 copy-start.65
  15.0 4.5 copy-start.26
  15.0 4.5 copy-start.36
  18.7 10.3 %copy-start.72 = (f32[128]{0:T(128)}, f32[128]{0:T(128)S(1)}, u32[]{:S(2)}) copy-start(f32[128]{0:T(128)S(1)} %multiply_reduce_fusion.3) | copy-start | bytes 1540
  19.7 9.3 %copy-start.2 = (bf16[768,768]{1,0:T(8,128)(2,1)S(1)}, bf16[768,768]{1,0:T(8,128)(2,1)}, u32[]{:S(2)}) copy-start(bf16[768,768]{1,0:T(8,128)(2,1)} %param.32) | copy-start | bytes 3538948
  33.7 6.0 copy-start.77
  36.0 9.3 %copy-start.45 = (f32[64]{0:T(128)}, f32[64]{0:T(128)S(1)}, u32[]{:S(2)}) copy-start(f32[64]{0:T(128)S(1)} %broadcast_multiply_fusion) | copy-start | bytes 772
  36.2 9.0 %copy-start.61 = (f32[64]{0:T(128)}, f32[64]{0:T(128)S(1)}, u32[]{:S(2)}) copy-start(f32[64]{0:T(128)S(1)} %fusion.61) | copy-start | bytes 772
  36.2 3.5 copy-start.32
  36.2 3.5 copy-start.78
  36.2 6.8 %slice-start = ((s8[4718592]{0:T(1024)(128)(4,1)}), s8[4194304]{0:T(1024)(128)(4,1)S(1)}, s32[]{:S(2)}) async-start(s8[4718592]{0:T(1024)(128)(4,1)} %bitcast.138), calls=%async_computation.26 | async-start | bytes 8388608
  55.5 95.0 %reduce-scatter.28.cloned.1.call-start = ((), (), s32[]{:S(2)}) async-start(), calls=%async_computation.20 | async-start | bytes 2506752 | tf_op jit(solution)/shard_map/reduce_scatter | solution.py:171
  58.3 157.9 %reduce-scatter.16.cloned.1.call-start = ((), (), s32[]{:S(2)}) async-start(), calls=%async_computation.14 | async-start | bytes 2506752 | tf_op jit(solution)/shard_map/reduce_scatter | solution.py:168
  64.3 3.7 copy-start.76
  64.3 20.0 %copy-start.37 = (f32[768]{0:T(1024)S(1)}, f32[768]{0:T(1024)}, u32[]{:S(2)}) copy-start(f32[768]{0:T(1024)} %param.44) | copy-start | bytes 9220
  64.3 20.0 %copy-start.43 = (f32[128]{0:T(128)S(1)}, f32[128]{0:T(128)}, u32[]{:S(2)}) copy-start(f32[128]{0:T(128)} %copy-done.42) | copy-start | bytes 1540
  64.3 20.0 %copy-start.59 = (f32[128]{0:T(128)S(1)}, f32[128]{0:T(128)}, u32[]{:S(2)}) copy-start(f32[128]{0:T(128)} %copy-done.58) | copy-start | bytes 1540
  64.4 217.9 %reduce-scatter.20.cloned.1.call-start = ((), (), s32[]{:S(2)}) async-start(), calls=%async_computation.16 | async-start | bytes 2506752 | tf_op jit(solution)/shard_map/reduce_scatter | solution.py:169
  86.5 261.4 %reduce-scatter.24.cloned.1.call-start = ((), (), s32[]{:S(2)}) async-start(), calls=%async_computation.18 | async-start | bytes 2506752 | tf_op jit(solution)/shard_map/reduce_scatter | solution.py:170
  88.5 374.2 %reduce-scatter.36.cloned.1.call-start = ((), (), s32[]{:S(2)}) async-start(), calls=%async_computation.24 | async-start | bytes 10027008 | tf_op jit(solution)/shard_map/reduce_scatter | solution.py:173
  97.2 480.8 %reduce-scatter.32.cloned.1.call-start = ((), (), s32[]{:S(2)}) async-start(), calls=%async_computation.22 | async-start | bytes 10027008 | tf_op jit(solution)/shard_map/reduce_scatter | solution.py:172
  104.0 360.0 %copy-start.10 = (f32[64,768]{1,0:T(8,128)S(1)}, f32[64,768]{1,0:T(8,128)}, u32[]{:S(2)}) copy-start(f32[64,768]{1,0:T(8,128)} %copy-done.9) | copy-start | bytes 589828
  104.0 362.1 %copy-start.38 = (f32[12,64]{1,0:T(8,128)S(1)}, f32[12,64]{1,0:T(8,128)}, u32[]{:S(2)}) copy-start(f32[12,64]{1,0:T(8,128)} %get-tuple-element.75) | copy-start | bytes 9220
  104.0 523.5 %reduce-scatter.30.cloned.1.call-start = ((), (), s32[]{:S(2)}) async-start(), calls=%async_computation.21 | async-start | bytes 221184 | tf_op jit(solution)/shard_map/reduce_scatter | solution.py:179
  150.4 477.1 %reduce-scatter.18.cloned.1.call-start = ((), (), s32[]{:S(2)}) async-start(), calls=%async_computation.15 | async-start | bytes 221184 | tf_op jit(solution)/shard_map/reduce_scatter | solution.py:176
  216.2 251.1 %copy-start.44 = (f32[128]{0:T(128)S(1)}, f32[128]{0:T(128)}, u32[]{:S(2)}) copy-start(f32[128]{0:T(128)} %copy-done.42) | copy-start | bytes 1540
  216.2 411.3 %reduce-scatter.22.cloned.1.call-start = ((), (), s32[]{:S(2)}) async-start(), calls=%async_computation.17 | async-start | bytes 221184 | tf_op jit(solution)/shard_map/reduce_scatter | solution.py:177
  282.3 348.8 %reduce-scatter.26.cloned.1.call-start = ((), (), s32[]{:S(2)}) async-start(), calls=%async_computation.19 | async-start | bytes 221184 | tf_op jit(solution)/shard_map/reduce_scatter | solution.py:178
  347.9 301.3 %reduce-scatter.38.cloned.1.call-start = ((), (), s32[]{:S(2)}) async-start(), calls=%async_computation.25 | async-start | bytes 884736 | tf_op jit(solution)/shard_map/reduce_scatter | solution.py:181
  462.8 204.5 %reduce-scatter.34.cloned.1.call-start = ((), (), s32[]{:S(2)}) async-start(), calls=%async_computation.23 | async-start | bytes 884736 | tf_op jit(solution)/shard_map/reduce_scatter | solution.py:180
  468.0 111.6 %copy-start.21 = (f32[1,64,768]{2,1,0:T(8,128)S(1)}, f32[1,64,768]{2,1,0:T(8,128)}, u32[]{:S(2)}) copy-start(f32[1,64,768]{2,1,0:T(8,128)} %copy-done.20) | copy-start | bytes 589828
  468.0 111.6 %copy-start.24 = (f32[1,64,768]{2,1,0:T(8,128)S(1)}, f32[1,64,768]{2,1,0:T(8,128)}, u32[]{:S(2)}) copy-start(f32[1,64,768]{2,1,0:T(8,128)} %get-tuple-element.49) | copy-start | bytes 589828
  468.0 111.6 %copy-start.25 = (f32[64,768]{1,0:T(8,128)S(1)}, f32[64,768]{1,0:T(8,128)}, u32[]{:S(2)}) copy-start(f32[64,768]{1,0:T(8,128)} %get-tuple-element.69) | copy-start | bytes 589828
  468.1 109.9 %copy-start.71 = (f32[128]{0:T(128)}, f32[128]{0:T(128)S(1)}, u32[]{:S(2)}) copy-start(f32[128]{0:T(128)S(1)} %multiply_multiply_fusion.5) | copy-start | bytes 1540
  579.6 5.7 copy-start.48
  579.6 5.7 copy-start.49
  579.7 5.7 copy-start.50
  579.7 5.7 copy-start.51
  579.7 5.7 copy-start.52
  579.7 5.7 copy-start.53
  579.7 5.6 copy-start.54
  579.7 5.6 copy-start.63
  (47 other events, 72.3 us)
Sparse Core Ops, SparseCore 0:
  55.6 27.5 reduce-scatter.13
  87.4 62.9 reduce-scatter.27
  154.2 61.9 reduce-scatter.15
  220.3 61.9 reduce-scatter.19
  285.9 61.9 reduce-scatter.23
  352.4 110.3 reduce-scatter.35
  466.8 111.1 reduce-scatter.31
  580.9 10.1 reduce-scatter.29
  594.0 10.5 reduce-scatter.17
  607.3 10.3 reduce-scatter.21
  620.6 10.4 reduce-scatter.25
  633.8 15.2 reduce-scatter.37
  652.0 15.2 reduce-scatter.33
where the time goes:
time: 675 us; the launch traced here: 674 us
  waiting for transfers between devices  520 us (77%)
  matrix products  53 us (8%)
  blocking collectives  51 us (8%)
  other arithmetic  19.6 us (3%)
  between operations  15 us (2%)
  local copies, waits for them, and re-layouts  14.7 us (2%)
    reduce_scatter x1, waiting for transfers between devices, per_device(): lax.psum_scatter(matrices[5], 'dp', scatter_dimension=0, tiled=True)  115 us
    reduce_scatter x1, waiting for transfers between devices, per_device(): lax.psum_scatter(matrices[4], 'dp', scatter_dimension=0, tiled=True)  109 us
    reduce_scatter x1, waiting for transfers between devices, per_device(): lax.psum_scatter(matrices[1], 'dp', scatter_dimension=0, tiled=True)  66 us
    reduce_scatter x1, waiting for transfers between devices, per_device(): lax.psum_scatter(matrices[0], 'dp', scatter_dimension=0, tiled=True)  65.7 us
    reduce_scatter x1, waiting for transfers between devices, per_device(): lax.psum_scatter(matrices[2], 'dp', scatter_dimension=0, tiled=True)  65.5 us
    reduce_scatter x1, waiting for transfers between devices, per_device(): lax.psum_scatter(matrices[3], 'dp', scatter_dimension=0, tiled=True)  46.3 us
    psum x1, blocking collectives, per_device(): lax.psum((g_b_query, g_b_value, g_b_out, g_b_fc1, g_b_fc2, g_gain_query,...  42.2 us
    dot_general x6, matrix products, weight_grad(): jnp.einsum('bnd,bnf->df', left, right, preferred_element_type=jnp.float32)  23.5 us
  transfers between devices with their start and end apart: 13, of which 10 were waited for; matrix products, arithmetic and copies ran while one was open for 7% of the time, Pallas kernels for 0%

commit v1 on v0

v1 whole, which is shorter than its diff:
```python
import functools
import math
import types

import jax
import jax.numpy as jnp
from jax import lax
from jax.experimental import pallas as pl
from jax.experimental.pallas import tpu as pltpu
from jax.sharding import PartitionSpec as P

HEAD_DIM = 64
MESH = pl.DeviceIdType.MESH
F32 = jnp.float32
BF16 = jnp.bfloat16
GROUPS = 16
Z_ORDER = (0, 2, 1, 3)


def dot(a, b):
    return lax.dot_general(a, b, (((1,), (0,)), ((), ())), preferred_element_type=F32)


def dot_t(a, b):
    return lax.dot_general(a, b, (((1,), (1,)), ((), ())), preferred_element_type=F32)


def col_sum(a):
    return jnp.sum(a, axis=0, keepdims=True)


def normalise(v):
    centre = v - jnp.mean(v, axis=-1, keepdims=True)
    spread = jnp.mean(centre * centre, axis=-1, keepdims=True)
    inv = lax.rsqrt(spread + 1e-06)
    return centre * inv, inv


def normalise_back(grad_hat, hat, inv):
    m1 = jnp.mean(grad_hat, axis=-1, keepdims=True)
    m2 = jnp.mean(grad_hat * hat, axis=-1, keepdims=True)
    return inv * (grad_hat - m1 - hat * m2)


def sinusoid(places, width):
    index = lax.broadcasted_iota(jnp.int32, (1, width), 1)
    half = index // 2
    freq = jnp.exp(-(2.0 * half.astype(F32) / width) * math.log(10000.0))
    odd = (index - 2 * half).astype(F32)
    angle = places * freq
    turns = jnp.floor(angle * (2.0 / math.pi) + 0.5)
    rest = angle - turns * 1.5703125
    rest = rest - turns * 4.8351287841796875e-4
    rest = rest - turns * 3.1385570764541626e-07
    sq = rest * rest
    sine = rest * (
        1.0 + sq * (-1.0 / 6 + sq * (1.0 / 120 + sq * (-1.0 / 5040 + sq * (1.0 / 362880))))
    )
    cosine = 1.0 + sq * (-0.5 + sq * (1.0 / 24 + sq * (-1.0 / 720 + sq * (1.0 / 40320))))
    quarter = turns + odd
    pairs = jnp.floor(quarter * 0.5)
    parity = quarter - 2.0 * pairs
    flips = pairs - 2.0 * jnp.floor(pairs * 0.5)
    value = jnp.where(parity > 0.5, cosine, sine)
    return jnp.where(flips > 0.5, -value, value)


def kernel(
    shape,
    queries, latents, positions, vis_ok, msk_ok, dy_in,
    w_query, w_key, w_value, w_out, w_fc1, w_fc2,
    b_query, b_value, b_out, b_fc1, b_fc2,
    gain_q, shift_q, gain_k, shift_k, gain_m, shift_m, scale_a, scale_m,
    out_block, out_dq, out_dl, out_wq, out_wk, out_wv, out_wo, out_w1, out_w2, out_vec,
    s,
):
    s = types.SimpleNamespace(**s)
    rows, width, ff, share = shape
    (b_query, b_value, b_out, b_fc1, b_fc2, gain_q, shift_q, gain_k, shift_k, gain_m, shift_m,
     scale_a, scale_m) = (
        ref[...].reshape(1, -1)
        for ref in (b_query, b_value, b_out, b_fc1, b_fc2, gain_q, shift_q, gain_k, shift_k, gain_m,
                    shift_m, scale_a, scale_m)
    )
    half = width // 2
    heads = half // HEAD_DIM
    blk = width // GROUPS
    fblk = ff // GROUPS
    nb = ff // half
    scale = 1.0 / math.sqrt(HEAD_DIM)

    x = lax.axis_index("qry")
    place = lax.axis_index("dp")
    n = place // share
    low = place - n * share
    z = n // 4
    y = (n // 2) % 2
    c = n % 2
    zs = (z, z + 1 - 2 * (z % 2), (z + 2) % 4, 3 - z)

    def dev(zz, yy, cc, xx):
        return (((zz * 2 + yy) * 2 + cc) * share + low, xx)

    PX = dev(z, y, c, 1 - x)
    PY = dev(z, 1 - y, c, x)
    PXY = dev(z, 1 - y, c, 1 - x)
    PC = dev(z, y, 1 - c, x)
    PZ = {t: dev(zs[t], y, c, x) for t in (1, 2, 3)}

    def remote(src, dst, i, peer):
        return pltpu.make_async_remote_copy(
            src_ref=src, dst_ref=dst, send_sem=s.send.at[i], recv_sem=s.recv.at[i],
            device_id=peer, device_id_type=MESH,
        )

    counter = [0]
    sent = []

    def new():
        counter[0] += 1
        return counter[0] - 1

    def push(src, dst, peer, landing=None):
        i = new()
        copy = remote(src, dst, i, peer)
        copy.start()
        sent.append(copy)
        arrival = copy if landing is None else remote(src, landing, i, peer)
        return arrival.wait_recv

    loads = []

    def load(src, dst):
        copy = pltpu.make_async_copy(src, dst, s.load.at[len(loads)])
        copy.start()
        loads.append(copy)
        return copy.wait

    own = pl.ds(pl.multiple_of(x * rows, rows), rows)
    other = pl.ds(pl.multiple_of((1 - x) * rows, rows), rows)
    mine = pl.ds(pl.multiple_of(x * half, half), half)
    theirs = pl.ds(pl.multiple_of((1 - x) * half, half), half)
    load_dy = load(dy_in.at[0], s.dy)
    load_q = load(queries.at[0], s.qraw.at[own])
    load_l = load(latents.at[0], s.lraw.at[own])
    load_w2 = load(w_fc2, s.w2)
    load_wk = load(w_key.at[:, mine], s.wk)
    load_wv = load(w_value.at[:, mine], s.wv)
    load_wq = load(w_query.at[:, mine], s.wq)
    load_wo = load(w_out, s.wo)
    load_w1 = load(w_fc1, s.w1)

    barrier = pltpu.get_barrier_semaphore()
    peers = [PX, PY, PXY, PC, PZ[1], PZ[2], PZ[3]]
    for peer in peers:
        pl.semaphore_signal(barrier, inc=1, device_id=peer, device_id_type=MESH)
    pl.semaphore_wait(barrier, len(peers))

    got_q = push(queries.at[0], s.qraw.at[own], PX, s.qraw.at[other])
    got_p = push(positions, s.ppos, PX)
    got_l = push(latents.at[0], s.lraw.at[own], PX, s.lraw.at[other])

    load_dy()
    dy = s.dy[...].astype(F32)
    d_mlp = (scale_m * dy).astype(BF16)
    s.vec[4:5, :] = col_sum(d_mlp.astype(F32))
    for xx in range(2):
        s.dm_s[xx] = d_mlp[:, xx * half:(xx + 1) * half]
    got_dm = [
        push(s.dm_s.at[x], s.dm_g.at[1], PY),
        push(s.dm_s.at[1 - x], s.dm_g.at[2], PX),
        push(s.dm_s.at[1 - x], s.dm_g.at[3], PXY),
    ]
    s.dm_g[0] = s.dm_s[x]

    eye = lax.broadcasted_iota(jnp.int32, (rows, rows), 0) == lax.broadcasted_iota(
        jnp.int32, (rows, rows), 1
    )

    def own_half(pos_ref, at, low_at):
        row = jnp.broadcast_to(pos_ref[...].astype(F32), (rows, rows))
        places = jnp.sum(jnp.where(eye, row, 0.0), axis=1, keepdims=True)
        qin = s.qraw[at, :].astype(F32) + sinusoid(places, width)
        hat, inv = normalise(qin)
        s.hat[low_at, :] = hat
        hq = (hat * gain_q + shift_q).astype(BF16)
        hkq = (hat * gain_k + shift_k).astype(BF16)
        s.hq[at, :] = hq
        s.hk[low_at, :] = hkq
        return qin, hat, inv, hq, hkq

    def lat_half(at):
        hat, inv = normalise(s.lraw[at, :].astype(F32))
        s.hat[at, :] = hat
        hkl = (hat * gain_k + shift_k).astype(BF16)
        s.hk[at, :] = hkl
        return hat, inv, hkl

    def project(hq, hkq, hkl, at, low_at):
        both = jnp.concatenate([hkl, hkq], axis=0)
        k = dot(both, s.wk[...]).astype(BF16)
        s.k[at, :] = k[:rows]
        s.k[low_at, :] = k[rows:]
        v = (dot(both, s.wv[...]) + jnp.where(x == 0, b_value[:, :half], b_value[:, half:])).astype(BF16)
        s.v[at, :] = v[:rows]
        s.v[low_at, :] = v[rows:]
        q = (dot(hq, s.wq[...]) + jnp.where(x == 0, b_query[:, :half], b_query[:, half:])).astype(BF16)
        s.q[at, :] = q

    low_own = pl.ds(pl.multiple_of((2 + x) * rows, rows), rows)
    low_other = pl.ds(pl.multiple_of((3 - x) * rows, rows), rows)
    load_q()
    load_l()
    qin, hat_q, inv_q, hq, hkq = own_half(positions, own, low_own)
    hat_l, inv_l, hkl = lat_half(own)

    load_w2()
    for b in range(nb):
        s.d_act[b] = dot_t(d_mlp, s.w2[b * half:(b + 1) * half, :])

    load_wk()
    load_wv()
    load_wq()
    project(hq, hkq, hkl, own, low_own)

    got_q()
    got_p()
    _, _, _, hq_o, hkq_o = own_half(s.ppos, other, low_other)
    got_l()
    _, _, hkl_o = lat_half(other)
    project(hq_o, hkq_o, hkl_o, other, low_other)

    ok = jnp.concatenate([vis_ok[...], msk_ok[...]], axis=1) > 0
    lane = lax.broadcasted_iota(jnp.int32, (2 * rows, 2 * HEAD_DIM), 1)
    first = lane < HEAD_DIM

    def stack(pair):
        zero = jnp.zeros_like(pair)
        return jnp.concatenate([jnp.where(first, pair, zero), jnp.where(first, zero, pair)], axis=0)

    def unstack(both):
        return jnp.where(first, both[:2 * rows], both[2 * rows:])

    def lanes(pair):
        return slice(pair * 2 * HEAD_DIM, (pair + 1) * 2 * HEAD_DIM)

    for pair in range(heads // 2):
        raw = dot_t(stack(s.q[:, lanes(pair)]), s.k[:, lanes(pair)]) * scale
        scores = jnp.where(ok, raw, -1e30)
        peak = jnp.max(scores, axis=-1, keepdims=True)
        weight = jnp.exp(scores - peak)
        prob = weight * (1.0 / jnp.sum(weight, axis=-1, keepdims=True))
        s.prob[pair] = prob
        s.att[x, :, lanes(pair)] = unstack(dot(prob.astype(BF16), s.v[:, lanes(pair)])).astype(
            BF16
        )
    got_att = push(s.att.at[x], s.att.at[x], PX, s.att.at[1 - x])

    s.hq_t[...] = s.hq[...].T
    s.hk_t[...] = s.hk[...].T
    load_wo()
    got_att()

    branch = (
        dot(s.att[0, own, :], s.wo[:half, :])
        + dot(s.att[1, own, :], s.wo[half:, :])
        + b_out
    )
    resid = qin + scale_a * branch
    hat_m, inv_m = normalise(resid)
    h_two = (hat_m * gain_m + shift_m).astype(BF16)
    s.h2_g[0] = h_two
    got_h2 = [
        push(s.h2_g.at[0], s.h2_g.at[1], PY),
        push(s.h2_g.at[0], s.h2_g.at[2], PX),
        push(s.h2_g.at[0], s.h2_g.at[3], PXY),
    ]
    load_w1()
    mlp = jnp.zeros((rows, width), F32)
    d_h2 = jnp.zeros((rows, width), F32)
    for b in range(nb):
        cols = slice(b * half, (b + 1) * half)
        pre = dot(h_two, s.w1[:, cols]) + b_fc1[:, cols]
        cdf = 0.5 * (1.0 + lax.erf(pre * math.sqrt(0.5)))
        act = (pre * cdf).astype(BF16)
        slope = cdf + pre * (jnp.exp(-0.5 * pre * pre) * (1.0 / math.sqrt(2 * math.pi)))
        d_pre = (s.d_act[b] * slope).astype(BF16)
        s.act_s[b % 2, b // 2] = act
        s.dp_s[b // (nb // 2), b % (nb // 2)] = d_pre
        s.vec[b // 2:b // 2 + 1, (b % 2) * half:(b % 2 + 1) * half] = col_sum(d_pre.astype(F32))
        mlp += dot(act, s.w2[cols, :])
        d_h2 += dot_t(d_pre, s.w1[:, cols])
    got_act = [push(s.act_s.at[1 - y], s.act_g.at[1], PY)]

    s.vec[6:7, :] = col_sum(d_h2 * hat_m)
    s.vec[7:8, :] = col_sum(d_h2)
    d_resid = dy + normalise_back(d_h2 * gain_m, hat_m, inv_m)
    d_branch = (scale_a * d_resid).astype(BF16)
    s.dbr[own, :] = d_branch
    got_dbr = push(s.dbr.at[own], s.dbr.at[own], PX, s.dbr.at[other])

    got_act += [
        push(s.act_s.at[y], s.act_g.at[2], PX),
        push(s.act_s.at[1 - y], s.act_g.at[3], PXY),
    ]
    got_dp = [
        push(s.dp_s.at[x], s.dp_g.at[1], PY),
        push(s.dp_s.at[1 - x], s.dp_g.at[2], PX),
        push(s.dp_s.at[1 - x], s.dp_g.at[3], PXY),
    ]
    s.act_g[0] = s.act_s[y]
    s.dp_g[0] = s.dp_s[x]
    mlp_out = mlp + b_fc2
    out_block[0] = (resid + scale_m * mlp_out).astype(BF16)
    s.vec[5:6, :] = col_sum(dy * mlp_out)
    s.vec2[0:1, :] = col_sum(d_branch.astype(F32))
    s.vec2[1:2, :] = col_sum(d_resid * branch)

    got_dbr()
    wo_mine = s.wo[mine, :]
    s.da[...] = dot_t(s.dbr[...], wo_mine).astype(BF16)
    for pair in range(heads // 2):
        q2 = stack(s.q[:, lanes(pair)])
        da2 = stack(s.da[:, lanes(pair)])
        prob = s.prob[pair]
        s.dv[:, lanes(pair)] = dot(prob.astype(BF16).T, da2).astype(BF16)
        d_prob = dot_t(da2, s.v[:, lanes(pair)])
        delta = jnp.sum(d_prob * prob, axis=-1, keepdims=True)
        ds = (prob * (d_prob - delta)).astype(BF16)
        s.dq[:, lanes(pair)] = (unstack(dot(ds, s.k[:, lanes(pair)])) * scale).astype(BF16)
        s.dk[:, lanes(pair)] = (dot(ds.T, q2) * scale).astype(BF16)

    def blocks(ref, cc, yy):
        return jnp.concatenate(
            [
                ref[pl.ds(pl.multiple_of(((zs[t] * 2 + yy) * 2 + cc) * blk, blk), blk), :]
                for t in Z_ORDER
            ],
            axis=0,
        )

    def square(i, left_t, right):
        for leave in (1, 0):
            cc = 1 - c if leave else c
            left = jnp.concatenate([blocks(left_t, cc, y), blocks(left_t, cc, 1 - y)], axis=0)
            total = dot(left, right)
            if leave:
                s.sq_cs[i] = total.astype(BF16)
                got = push(s.sq_cs.at[i], s.sq_cr.at[i], PC)
            else:
                s.sq[i] = total
        return got

    got_c = [None] * 4
    got_c[1] = square(1, s.hk_t, s.dv[...])
    got_c[2] = square(2, s.hk_t, s.dk[...])
    got_c[3] = square(3, s.hq_t, s.dq[...])

    dhk = dot_t(s.dk[...], s.wk[...]) + dot_t(s.dv[...], s.wv[...])
    dhq = dot_t(s.dq[...], s.wq[...])
    s.vec2[2:3, :] = jnp.zeros((1, width), F32)
    s.vec2[3:4, :] = jnp.zeros((1, width), F32)
    s.vec2[2:3, mine] = col_sum(s.dq[...].astype(F32))
    s.vec2[3:4, mine] = col_sum(s.dv[...].astype(F32))
    hat_low = s.hat[2 * rows:, :]
    s.vec2[4:5, :] = col_sum(dhq * hat_low)
    s.vec2[5:6, :] = col_sum(dhq)
    s.vec2[6:7, :] = col_sum(dhk * s.hat[...])
    s.vec2[7:8, :] = col_sum(dhk)
    s.dx[0] = dhk[:2 * rows] * gain_k
    s.dx[1] = dhk[2 * rows:] * gain_k + dhq * gain_q
    s.dx_s[...] = s.dx[:, other, :].astype(BF16)
    got_dx = push(s.dx_s, s.dx_r, PX)

    s.att_t[mine, :] = s.att[x].T
    s.att_t[theirs, :] = s.att[1 - x].T
    got_c[0] = square(0, s.att_t, s.dbr[:, mine])

    vectors = ((s.vec, s.vec_a, s.vec_b, s.vec_r), (s.vec2, s.vec2_a, s.vec2_b, s.vec2_r))
    got_vc = [push(s.vec, s.vec_r.at[0], PC), push(s.vec2, s.vec2_r.at[0], PC)]

    for got in got_dm:
        got()
    for got in got_act:
        got()
    d_mlp_all = s.dm_g[...].reshape(4 * rows, half)
    for k, t in enumerate(Z_ORDER):
        part = s.act_g[:, zs[t]].reshape(4 * rows, half)
        s.fc2[k] = dot(part.T, d_mlp_all)
        s.fc2_cs[k] = s.fc2[k, pl.ds(pl.multiple_of((1 - c) * fblk, fblk), fblk), :].astype(BF16)
    got_c2 = push(s.fc2_cs, s.fc2_cr, PC)

    for got in got_h2:
        got()
    s.h2_t[...] = s.h2_g[...].reshape(4 * rows, width).T
    for got in got_dp:
        got()
    leave = blocks(s.h2_t, 1 - c, y)
    stay = blocks(s.h2_t, c, y)
    for b in range(nb // 2):
        right = s.dp_g[:, b].reshape(4 * rows, half)
        s.fc1_cs[b] = dot(leave, right).astype(BF16)
        s.fc1[b] = dot(stay, right)
    got_c1 = push(s.fc1_cs, s.fc1_cr, PC)

    yrows = 4 * blk
    got_y = []
    for i in (1, 2, 3, 0):
        got_c[i]()
        s.sq_ys[i] = (s.sq[i, yrows:, :] + s.sq_cr[i, yrows:, :].astype(F32)).astype(BF16)
        got_y.append(push(s.sq_ys.at[i], s.sq_yr.at[i], PY))

    got_c2()
    keep = pl.ds(pl.multiple_of(c * fblk, fblk), fblk)
    s.fc2_zs[...] = (s.fc2[2:, keep, :] + s.fc2_cr[2:].astype(F32)).astype(BF16)
    got_z2 = push(s.fc2_zs, s.fc2_zr, PZ[1])
    got_c1()
    s.fc1_zs[...] = (s.fc1[:, 2 * blk:, :] + s.fc1_cr[:, 2 * blk:, :].astype(F32)).astype(BF16)
    got_z1 = push(s.fc1_zs, s.fc1_zr, PZ[1])

    got_vxy = []
    for group, got in enumerate(got_vc):
        got()
        ref, summed, _, landing = vectors[group]
        summed[...] = ref[...] + landing[0]
        got_vxy.append(
            [
                push(summed, landing.at[1], PX),
                push(summed, landing.at[2], PY),
                push(summed, landing.at[3], PXY),
            ]
        )

    for got in got_y:
        got()
    zrows = 2 * blk
    for i in range(4):
        s.sq[i, :yrows, :] = (
            s.sq[i, :yrows, :] + s.sq_cr[i, :yrows, :].astype(F32) + s.sq_yr[i].astype(F32)
        )
        s.sq_zs[i] = s.sq[i, zrows:yrows, :].astype(BF16)
    got_zsq = push(s.sq_zs, s.sq_zr, PZ[1])

    got_dx()
    dx_l = s.dx[0, own, :] + s.dx_r[0].astype(F32)
    dx_q = s.dx[1, own, :] + s.dx_r[1].astype(F32)
    out_dl[0] = normalise_back(dx_l, hat_l, inv_l)
    out_dq[0] = d_resid + normalise_back(dx_q, hat_q, inv_q)

    got_vz = []
    for group, gots in enumerate(got_vxy):
        for got in gots:
            got()
        _, summed, square_sum, landing = vectors[group]
        square_sum[...] = (summed[...] + landing[1]) + (landing[2] + landing[3])
        got_vz.append([push(square_sum, landing.at[3 + t], PZ[t]) for t in (1, 2, 3)])

    got_z2()
    s.fc2_ws[...] = (
        s.fc2[1, keep, :] + s.fc2_cr[1].astype(F32) + s.fc2_zr[1].astype(F32)
    ).astype(BF16)
    got_w2 = push(s.fc2_ws, s.fc2_wr, PZ[2])
    got_z1()
    s.fc1_ws[...] = (
        s.fc1[:, blk:2 * blk, :]
        + s.fc1_cr[:, blk:2 * blk, :].astype(F32)
        + s.fc1_zr[:, blk:, :].astype(F32)
    ).astype(BF16)
    got_w1 = push(s.fc1_ws, s.fc1_wr, PZ[2])
    got_zsq()
    s.sq_ws[...] = (s.sq[:, blk:zrows, :] + s.sq_zr[:, blk:, :].astype(F32)).astype(BF16)
    got_wsq = push(s.sq_ws, s.sq_wr, PZ[2])

    got_w2()
    out_w2[...] = (
        s.fc2[0, keep, :]
        + s.fc2_cr[0].astype(F32)
        + s.fc2_zr[0].astype(F32)
        + s.fc2_wr[...].astype(F32)
    )
    got_w1()
    for b in range(nb // 2):
        out_w1[:, b * half:(b + 1) * half] = (
            s.fc1[b, :blk, :]
            + s.fc1_cr[b, :blk, :].astype(F32)
            + s.fc1_zr[b, :blk, :].astype(F32)
            + s.fc1_wr[b].astype(F32)
        )
    for group, gots in enumerate(got_vz):
        for got in gots:
            got()
        _, _, square_sum, landing = vectors[group]
        out_vec[group * 8:group * 8 + 8, :] = (square_sum[...] + landing[4]) + (
            landing[5] + landing[6]
        )
    got_wsq()
    for i, out in enumerate((out_wo, out_wv, out_wk, out_wq)):
        out[...] = (
            s.sq[i, :blk, :] + s.sq_zr[i, :blk, :].astype(F32) + s.sq_wr[i].astype(F32)
        )
    for copy in sent:
        copy.wait_send()


def fused(share, args):
    (queries, latents, positions, vis_ok, msk_ok, dy, w_query, w_key, w_value, w_out, w_fc1, w_fc2) = args[:12]
    vectors = args[12:]
    _, rows, width = queries.shape
    ff = w_fc1.shape[1]
    half = width // 2
    blk, fblk, nb = width // GROUPS, ff // GROUPS, ff // half
    pairs = half // (2 * HEAD_DIM)
    vm = pltpu.VMEM
    scratch = dict(
        send=pltpu.SemaphoreType.DMA((64,)),
        recv=pltpu.SemaphoreType.DMA((64,)),
        load=pltpu.SemaphoreType.DMA((16,)),
        dy=vm((rows, width), BF16),
        qraw=vm((2 * rows, width), BF16),
        lraw=vm((2 * rows, width), BF16),
        ppos=vm((1, rows), jnp.int32),
        w2=vm((ff, width), BF16),
        w1=vm((width, ff), BF16),
        wo=vm((width, width), BF16),
        wk=vm((width, half), BF16),
        wv=vm((width, half), BF16),
        wq=vm((width, half), BF16),
        hat=vm((4 * rows, width), F32),
        hq=vm((2 * rows, width), BF16),
        hk=vm((4 * rows, width), BF16),
        hq_t=vm((width, 2 * rows), BF16),
        hk_t=vm((width, 4 * rows), BF16),
        att_t=vm((width, 2 * rows), BF16),
        h2_t=vm((width, 4 * rows), BF16),
        q=vm((2 * rows, half), BF16),
        k=vm((4 * rows, half), BF16),
        v=vm((4 * rows, half), BF16),
        prob=vm((pairs, 4 * rows, 4 * rows), F32),
        att=vm((2, 2 * rows, half), BF16),
        d_act=vm((nb, rows, half), F32),
        dm_s=vm((2, rows, half), BF16),
        dm_g=vm((4, rows, half), BF16),
        h2_g=vm((4, rows, width), BF16),
        act_s=vm((2, nb // 2, rows, half), BF16),
        act_g=vm((4, nb // 2, rows, half), BF16),
        dp_s=vm((2, nb // 2, rows, half), BF16),
        dp_g=vm((4, nb // 2, rows, half), BF16),
        dbr=vm((2 * rows, width), BF16),
        da=vm((2 * rows, half), BF16),
        dq=vm((2 * rows, half), BF16),
        dk=vm((4 * rows, half), BF16),
        dv=vm((4 * rows, half), BF16),
        dx=vm((2, 2 * rows, width), F32),
        dx_s=vm((2, rows, width), BF16),
        dx_r=vm((2, rows, width), BF16),
        sq=vm((4, 8 * blk, half), F32),
        sq_cs=vm((4, 8 * blk, half), BF16),
        sq_cr=vm((4, 8 * blk, half), BF16),
        sq_ys=vm((4, 4 * blk, half), BF16),
        sq_yr=vm((4, 4 * blk, half), BF16),
        sq_zs=vm((4, 2 * blk, half), BF16),
        sq_zr=vm((4, 2 * blk, half), BF16),
        sq_ws=vm((4, blk, half), BF16),
        sq_wr=vm((4, blk, half), BF16),
        fc2=vm((4, 2 * fblk, half), F32),
        fc2_cs=vm((4, fblk, half), BF16),
        fc2_cr=vm((4, fblk, half), BF16),
        fc2_zs=vm((2, fblk, half), BF16),
        fc2_zr=vm((2, fblk, half), BF16),
        fc2_ws=vm((fblk, half), BF16),
        fc2_wr=vm((fblk, half), BF16),
        fc1=vm((nb // 2, 4 * blk, half), F32),
        fc1_cs=vm((nb // 2, 4 * blk, half), BF16),
        fc1_cr=vm((nb // 2, 4 * blk, half), BF16),
        fc1_zs=vm((nb // 2, 2 * blk, half), BF16),
        fc1_zr=vm((nb // 2, 2 * blk, half), BF16),
        fc1_ws=vm((nb // 2, blk, half), BF16),
        fc1_wr=vm((nb // 2, blk, half), BF16),
        vec=vm((8, width), F32),
        vec_a=vm((8, width), F32),
        vec_b=vm((8, width), F32),
        vec_r=vm((7, 8, width), F32),
        vec2=vm((8, width), F32),
        vec2_a=vm((8, width), F32),
        vec2_b=vm((8, width), F32),
        vec2_r=vm((7, 8, width), F32),
    )
    ANY = pl.BlockSpec(memory_space=pl.ANY)
    VMEM = pl.BlockSpec(memory_space=pltpu.VMEM)
    sds = jax.ShapeDtypeStruct
    return pl.pallas_call(
        functools.partial(kernel, (rows, width, ff, share)),
        out_shape=(
            sds((1, rows, width), BF16),
            sds((1, rows, width), F32),
            sds((1, rows, width), F32),
            sds((blk, half), F32),
            sds((blk, half), F32),
            sds((blk, half), F32),
            sds((blk, half), F32),
            sds((blk, ff // 2), F32),
            sds((fblk, half), F32),
            sds((16, width), F32),
        ),
        in_specs=[ANY, ANY, VMEM, VMEM, VMEM, ANY] + [ANY] * 6 + [VMEM] * 13,
        out_specs=[VMEM] * 10,
        scratch_shapes=[scratch],
        compiler_params=pltpu.CompilerParams(
            collective_id=0, has_side_effects=True, vmem_limit_bytes=60 << 20
        ),
        cost_estimate=pl.CostEstimate(
            flops=6 * 10**9, bytes_accessed=16 * 10**6, transcendentals=10**6
        ),
    )(queries, latents, positions, vis_ok, msk_ok, dy, w_query, w_key, w_value, w_out, w_fc1, w_fc2, *vectors)


def finish_kernel(count, *refs):
    arrays, table = refs[:count], refs[count]
    outs, rows = refs[count + 1:2 * count + 1], refs[2 * count + 1:-1]
    sems = refs[-1]
    copies = [
        pltpu.make_async_copy(src, dst, sems.at[i]) for i, (src, dst) in enumerate(zip(arrays, outs))
    ]
    for copy in copies:
        copy.start()
    width = table.shape[1]
    parts = rows[0].shape[0] // width
    for k in range(parts):
        rows[0][k * width:(k + 1) * width] = table[k, :]
    for k, row in enumerate(rows[1:]):
        row[...] = table[parts + k, :]
    for copy in copies:
        copy.wait()


def finish(arrays, table, ff):
    count, width = len(arrays), table.shape[1]
    sds = jax.ShapeDtypeStruct
    vectors = table.shape[0] - ff // width
    ANY = pl.BlockSpec(memory_space=pl.ANY)
    VMEM = pl.BlockSpec(memory_space=pltpu.VMEM)
    return pl.pallas_call(
        functools.partial(finish_kernel, count),
        out_shape=tuple(sds(a.shape, a.dtype) for a in arrays)
        + (sds((ff,), F32),)
        + (sds((width,), F32),) * vectors,
        in_specs=[VMEM] * (count + 1),
        out_specs=[ANY] * count + [VMEM] * (1 + vectors),
        scratch_shapes=[pltpu.SemaphoreType.DMA((count,))],
    )(*arrays, table)


def per_device(
    queries, latents, positions, visible_valid, masked_valid,
    w_query, b_query, w_key, w_value, b_value, w_out, b_out, w_fc1, b_fc1, w_fc2, b_fc2,
    gain_query, shift_query, gain_keys, shift_keys, gain_mlp, shift_mlp, scale_attn, scale_mlp,
    out_grad,
):
    parts = lax.axis_size("dp")
    share = parts // GROUPS
    out = fused(
        share,
        (
            queries, latents, positions, visible_valid, masked_valid, out_grad,
            w_query, w_key, w_value, w_out, w_fc1, w_fc2,
            b_query, b_value, b_out, b_fc1, b_fc2,
            gain_query, shift_query, gain_keys, shift_keys, gain_mlp, shift_mlp, scale_attn, scale_mlp,
        ),
    )
    block_out, d_queries, d_latents, wq, wk, wv, wo, w1, w2, vec = out
    if share > 1:
        groups = [[n * share + i for i in range(share)] for n in range(GROUPS)]
        wq, wk, wv, wo, w1, w2 = (
            lax.psum_scatter(
                w, "dp", scatter_dimension=0, axis_index_groups=groups, tiled=True
            )
            for w in (wq, wk, wv, wo, w1, w2)
        )
        vec = lax.psum(vec, "dp", axis_index_groups=groups)
    arrays = (block_out, d_queries, d_latents, wq, wk, wv, wo, w1, w2)
    done = finish(arrays, vec, w_fc1.shape[1])
    block_out, d_queries, d_latents, wq, wk, wv, wo, w1, w2, b1 = done[:10]
    b2, sm, gm, hm, bo, sa, bq, bv, gq, hq, gk, hk = done[10:]
    return (
        block_out, d_queries, d_latents,
        wq, bq, wk, wv, bv, wo, bo, w1, b1, w2, b2,
        gq, hq, gk, hk, gm, hm, sa, sm,
    )


def solution(mesh):
    rows3 = P("dp", "qry", None)
    split = P("dp", "qry")
    full = P()
    return jax.shard_map(
        per_device,
        mesh=mesh,
        in_specs=(rows3, rows3, split, P("dp", None), P("dp", None)) + (full,) * 19 + (rows3,),
        out_specs=(
            rows3, rows3, rows3,
            split, full, split, split, full, split, full, split, full, split,
        ) + (full,) * 9,
        check_vma=False,
    )
```

time: 675 us -> 87.3 us (0.13)
  waiting for transfers between devices: 520 us -> 0 us
  Pallas kernels: 0 us -> 86.4 us
  matrix products: 53 us -> 0 us
  blocking collectives: 51 us -> 0 us
  other arithmetic: 19.6 us -> 0 us
  local copies, waits for them, and re-layouts: 14.7 us -> 0 us
  between operations: 15 us -> 0.68 us
    reduce_scatter x13 -> x0, waiting for transfers between devices: 520 us -> none  [the longest x1 115 us: per_device(): lax.psum_scatter(matrices[5], 'dp', scatter_dimension=0, tiled=True)]
    pallas_call x0 -> x2, Pallas kernels: none -> 86.4 us  [the longest x1 83.2 us: fused(): pl.pallas_call(functools.partial(kernel, (rows, width, ff, share)), out_s...]
    dot_general x24 -> x0, matrix products: 53 us -> none  [the longest x6 23.5 us: weight_grad(): jnp.einsum('bnd,bnf->df', left, right, preferred_element_type=jnp.float32)]
    psum x1 -> x0, blocking collectives: 42.2 us -> none  [per_device(): lax.psum((g_b_query, g_b_value, g_b_out, g_b_fc1, g_b_fc2, g_gain_query,...]
    reduce_sum x13 -> x0, other arithmetic: 10.6 us -> none  [the longest x4 4.24 us: layer_norm(): centre = x - jnp.mean(x, axis=-1, keepdims=True)]
    unnamed x165 -> x0, local copies, waits for them, and re-layouts: 9.12 us -> none
    all_gather x1 -> x0, blocking collectives: 8.81 us -> none  [per_device(): piece = lax.all_gather(hk, 'qry', axis=1, tiled=True)]
  transfers between devices with their start and end apart: 13 -> 0, of which waited for: 10 -> 0; matrix products, arithmetic and copies ran while one was open for 7% -> 0% of each run, Pallas kernels for 0% -> 0%
where the time goes in v1:
time: 87.3 us; the launch traced here: 87.1 us
  Pallas kernels  86.4 us (99%)
    pallas_call x1, Pallas kernels, fused(): pl.pallas_call(functools.partial(kernel, (rows, width, ff, share)), out_s...  83.2 us
    pallas_call x1, Pallas kernels, finish(): pl.pallas_call(functools.partial(finish_kernel, count), out_shape=tuple((...  3.2 us

profile of v1, /device:TPU:0, one launch (start us, length us, event | category | flops | bytes accessed | tf_op | source)
XLA Modules:
  0.0 87.1 jit_solution(9955266204934191021)
XLA Ops:
  0.7 83.2 %shard_map.408 = (bf16[1,64,768]{2,1,0:T(8,128)(2,1)}, f32[1,64,768]{2,1,0:T(8,128)}, f32[1,64,768]{2,1,0:T(8,128)}, f32[48,384]{1,0:T(8,128)}, f32[48,384]{1,0:...) custom-call(bf16[1,64,768]{2,1,0:T(8,128)(2,1)} %queries.1, ...), custom_call_target="tpu_custom_call" | custom-call | flops 6000000000 | bytes 16000000 | tf_op jit(solution)/shard_map/pallas_call | solution.py:591
  83.9 3.2 %shard_map.409 = (bf16[1,64,768]{2,1,0:T(8,128)(2,1)}, f32[1,64,768]{2,1,0:T(8,128)}, f32[1,64,768]{2,1,0:T(8,128)}, f32[48,384]{1,0:T(8,128)}, f32[48,384]{1,0:...) custom-call(bf16[1,64,768]{2,1,0:T(8,128)(2,1)} %get-tuple-element.5, ...), custom_call_target="tpu_custom_call" | custom-call | tf_op jit(solution)/shard_map/pallas_call | solution.py:642

commit v2 on v1

v2 whole, which is shorter than its diff:
```python
import functools
import math
import types

import jax
import jax.numpy as jnp
from jax import lax
from jax.experimental import pallas as pl
from jax.experimental.pallas import tpu as pltpu
from jax.sharding import PartitionSpec as P

HEAD_DIM = 64
MESH = pl.DeviceIdType.MESH
F32 = jnp.float32
BF16 = jnp.bfloat16
GROUPS = 16
Z_ORDER = (0, 2, 1, 3)


def dot(a, b):
    return lax.dot_general(a, b, (((1,), (0,)), ((), ())), preferred_element_type=F32)


def dot_t(a, b):
    return lax.dot_general(a, b, (((1,), (1,)), ((), ())), preferred_element_type=F32)


def col_sum(a):
    return jnp.sum(a, axis=0, keepdims=True)


def normalise(v):
    centre = v - jnp.mean(v, axis=-1, keepdims=True)
    spread = jnp.mean(centre * centre, axis=-1, keepdims=True)
    inv = lax.rsqrt(spread + 1e-06)
    return centre * inv, inv


def normalise_back(grad_hat, hat, inv):
    m1 = jnp.mean(grad_hat, axis=-1, keepdims=True)
    m2 = jnp.mean(grad_hat * hat, axis=-1, keepdims=True)
    return inv * (grad_hat - m1 - hat * m2)


def sinusoid(places, width):
    index = lax.broadcasted_iota(jnp.int32, (1, width), 1)
    half = index // 2
    freq = jnp.exp(-(2.0 * half.astype(F32) / width) * math.log(10000.0))
    odd = (index - 2 * half).astype(F32)
    angle = places * freq
    turns = jnp.floor(angle * (2.0 / math.pi) + 0.5)
    rest = angle - turns * 1.5703125
    rest = rest - turns * 4.8351287841796875e-4
    rest = rest - turns * 3.1385570764541626e-07
    sq = rest * rest
    sine = rest * (
        1.0 + sq * (-1.0 / 6 + sq * (1.0 / 120 + sq * (-1.0 / 5040 + sq * (1.0 / 362880))))
    )
    cosine = 1.0 + sq * (-0.5 + sq * (1.0 / 24 + sq * (-1.0 / 720 + sq * (1.0 / 40320))))
    quarter = turns + odd
    pairs = jnp.floor(quarter * 0.5)
    parity = quarter - 2.0 * pairs
    flips = pairs - 2.0 * jnp.floor(pairs * 0.5)
    value = jnp.where(parity > 0.5, cosine, sine)
    return jnp.where(flips > 0.5, -value, value)


def kernel(
    shape,
    queries, latents, positions, vis_ok, msk_ok, dy_in,
    w_query, w_key, w_value, w_out, w_fc1, w_fc2,
    b_query, b_value, b_out, b_fc1, b_fc2,
    gain_q, shift_q, gain_k, shift_k, gain_m, shift_m, scale_a, scale_m,
    out_block, out_dq, out_dl, out_wq, out_wk, out_wv, out_wo, out_w1, out_w2, out_vec,
    s,
):
    s = types.SimpleNamespace(**s)
    rows, width, ff, share = shape
    (b_query, b_value, b_out, b_fc1, b_fc2, gain_q, shift_q, gain_k, shift_k, gain_m, shift_m,
     scale_a, scale_m) = (
        ref[...].reshape(1, -1)
        for ref in (b_query, b_value, b_out, b_fc1, b_fc2, gain_q, shift_q, gain_k, shift_k, gain_m,
                    shift_m, scale_a, scale_m)
    )
    half = width // 2
    heads = half // HEAD_DIM
    blk = width // GROUPS
    fblk = ff // GROUPS
    hid = ff // 2
    nb = hid // half
    scale = 1.0 / math.sqrt(HEAD_DIM)

    x = lax.axis_index("qry")
    place = lax.axis_index("dp")
    n = place // share
    low = place - n * share
    z = n // 4
    y = (n // 2) % 2
    c = n % 2
    zs = (z, z + 1 - 2 * (z % 2), (z + 2) % 4, 3 - z)

    def dev(zz, yy, cc, xx):
        return (((zz * 2 + yy) * 2 + cc) * share + low, xx)

    PX = dev(z, y, c, 1 - x)
    PY = dev(z, 1 - y, c, x)
    PC = dev(z, y, 1 - c, x)
    PZ1 = dev(zs[1], y, c, x)
    PZ2 = dev(zs[2], y, c, x)

    counter = [0]
    sent = []

    def push(src, dst, peer, landing=None):
        i = counter[0]
        counter[0] += 1

        def describe(to):
            return pltpu.make_async_remote_copy(
                src_ref=src, dst_ref=to, send_sem=s.send.at[i], recv_sem=s.recv.at[i],
                device_id=peer, device_id_type=MESH,
            )

        copy = describe(dst)
        copy.start()
        sent.append(copy)
        arrival = copy if landing is None else describe(landing)
        return arrival.wait_recv

    loads = []

    def load(src, dst):
        copy = pltpu.make_async_copy(src, dst, s.load.at[len(loads)])
        copy.start()
        loads.append(copy)
        return copy.wait

    own = pl.ds(pl.multiple_of(x * rows, rows), rows)
    other = pl.ds(pl.multiple_of((1 - x) * rows, rows), rows)
    low_own = pl.ds(pl.multiple_of((2 + x) * rows, rows), rows)
    low_other = pl.ds(pl.multiple_of((3 - x) * rows, rows), rows)
    mine = pl.ds(pl.multiple_of(x * half, half), half)
    theirs = pl.ds(pl.multiple_of((1 - x) * half, half), half)
    units = pl.ds(pl.multiple_of(x * hid, hid), hid)
    load_q = load(queries.at[0], s.qraw.at[own])
    load_l = load(latents.at[0], s.lraw.at[own])
    load_dy = load(dy_in.at[0], s.dy.at[own])
    load_wk = load(w_key.at[:, mine], s.wk)
    load_wv = load(w_value.at[:, mine], s.wv)
    load_wq = load(w_query.at[:, mine], s.wq)
    load_w2 = load(w_fc2.at[units], s.w2)
    load_wo = load(w_out, s.wo)
    load_w1 = load(w_fc1.at[:, units], s.w1)

    barrier = pltpu.get_barrier_semaphore()
    peers = [PX, PY, PC, PZ1, PZ2]
    for peer in peers:
        pl.semaphore_signal(barrier, inc=1, device_id=peer, device_id_type=MESH)
    pl.semaphore_wait(barrier, len(peers))

    got_p = push(positions, s.ppos, PX)
    got_q = push(queries.at[0], s.qraw.at[own], PX, s.qraw.at[other])
    got_l = push(latents.at[0], s.lraw.at[own], PX, s.lraw.at[other])
    got_dy = push(dy_in.at[0], s.dy.at[own], PX, s.dy.at[other])

    eye = lax.broadcasted_iota(jnp.int32, (rows, rows), 0) == lax.broadcasted_iota(
        jnp.int32, (rows, rows), 1
    )

    def qry_half(pos_ref, at, low_at):
        row = jnp.broadcast_to(pos_ref[...].astype(F32), (rows, rows))
        places = jnp.sum(jnp.where(eye, row, 0.0), axis=1, keepdims=True)
        qin = s.qraw[at, :].astype(F32) + sinusoid(places, width)
        s.qin[at, :] = qin
        hat, inv = normalise(qin)
        s.hat[low_at, :] = hat
        hq = (hat * gain_q + shift_q).astype(BF16)
        hkq = (hat * gain_k + shift_k).astype(BF16)
        s.hq[at, :] = hq
        s.hk[low_at, :] = hkq
        return hat, inv, hq, hkq

    def lat_half(at):
        hat, inv = normalise(s.lraw[at, :].astype(F32))
        s.hat[at, :] = hat
        hkl = (hat * gain_k + shift_k).astype(BF16)
        s.hk[at, :] = hkl
        return hat, inv, hkl

    my_b_value = jnp.where(x == 0, b_value[:, :half], b_value[:, half:])
    my_b_query = jnp.where(x == 0, b_query[:, :half], b_query[:, half:])
    my_b_fc1 = jnp.where(x == 0, b_fc1[:, :hid], b_fc1[:, hid:])

    def project(hq, hkq, hkl, at, low_at):
        both = jnp.concatenate([hkl, hkq], axis=0)
        k = dot(both, s.wk[...]).astype(BF16)
        s.k[at, :] = k[:rows]
        s.k[low_at, :] = k[rows:]
        v = (dot(both, s.wv[...]) + my_b_value).astype(BF16)
        s.v[at, :] = v[:rows]
        s.v[low_at, :] = v[rows:]
        s.q[at, :] = (dot(hq, s.wq[...]) + my_b_query).astype(BF16)

    load_q()
    load_l()
    hat_q, inv_q, hq, hkq = qry_half(positions, own, low_own)
    hat_l, inv_l, hkl = lat_half(own)
    load_wk()
    load_wv()
    load_wq()
    project(hq, hkq, hkl, own, low_own)
    got_p()
    got_q()
    _, _, hq_o, hkq_o = qry_half(s.ppos, other, low_other)
    got_l()
    _, _, hkl_o = lat_half(other)
    project(hq_o, hkq_o, hkl_o, other, low_other)

    ok = jnp.concatenate([vis_ok[...], msk_ok[...]], axis=1) > 0
    lane = lax.broadcasted_iota(jnp.int32, (2 * rows, 2 * HEAD_DIM), 1)
    first = lane < HEAD_DIM

    def stack(pair):
        zero = jnp.zeros_like(pair)
        return jnp.concatenate([jnp.where(first, pair, zero), jnp.where(first, zero, pair)], axis=0)

    def unstack(both):
        return jnp.where(first, both[:2 * rows], both[2 * rows:])

    def lanes(pair):
        return slice(pair * 2 * HEAD_DIM, (pair + 1) * 2 * HEAD_DIM)

    for pair in range(heads // 2):
        raw = dot_t(stack(s.q[:, lanes(pair)]), s.k[:, lanes(pair)]) * scale
        scores = jnp.where(ok, raw, -1e30)
        peak = jnp.max(scores, axis=-1, keepdims=True)
        weight = jnp.exp(scores - peak)
        prob = weight * (1.0 / jnp.sum(weight, axis=-1, keepdims=True))
        s.prob[pair] = prob
        s.att[x, :, lanes(pair)] = unstack(dot(prob.astype(BF16), s.v[:, lanes(pair)])).astype(BF16)
    got_att = push(s.att.at[x], s.att.at[x], PX, s.att.at[1 - x])

    load_dy()
    got_dy()
    load_w2()
    dy = s.dy[...].astype(F32)
    d_mlp = (scale_m * dy).astype(BF16)
    s.dm[0] = d_mlp
    got_dm = push(s.dm.at[0], s.dm.at[1], PY)
    for b in range(nb):
        s.d_act[b] = dot_t(d_mlp, s.w2[b * half:(b + 1) * half, :])
    s.vec[0, 4:5, :] = col_sum((scale_m * s.dy[own, :].astype(F32)).astype(BF16).astype(F32))
    s.hq_t[...] = s.hq[...].T
    s.hk_t[...] = s.hk[...].T
    load_wo()
    got_att()

    branch = dot(s.att[0], s.wo[:half, :]) + dot(s.att[1], s.wo[half:, :]) + b_out
    s.branch[...] = branch
    resid = s.qin[...] + scale_a * branch
    s.resid[...] = resid
    hat_m, inv_m = normalise(resid)
    h_two = (hat_m * gain_m + shift_m).astype(BF16)

    def blocks(ref, cc, yy):
        return jnp.concatenate(
            [
                ref[pl.ds(pl.multiple_of(((zs[t] * 2 + yy) * 2 + cc) * blk, blk), blk), :]
                for t in Z_ORDER
            ],
            axis=0,
        )

    s.h2_t[...] = h_two.T
    for i, yy in enumerate((y, 1 - y)):
        s.h2_g[i, 0] = blocks(s.h2_t, c, yy)
        s.h2_g[i, 1] = blocks(s.h2_t, 1 - c, yy)
    got_h2 = push(s.h2_g.at[1], s.h2_r, PY)
    load_w1()
    mlp = jnp.zeros((2 * rows, width), F32)
    d_h2 = jnp.zeros((2 * rows, width), F32)
    s.vec[0, 0:4, :] = jnp.zeros((4, width), F32)
    got_dp = []
    for b in range(nb):
        cols = slice(b * half, (b + 1) * half)
        pre = dot(h_two, s.w1[:, cols]) + my_b_fc1[:, cols]
        cdf = 0.5 * (1.0 + lax.erf(pre * math.sqrt(0.5)))
        act = (pre * cdf).astype(BF16)
        slope = cdf + pre * (jnp.exp(-0.5 * pre * pre) * (1.0 / math.sqrt(2 * math.pi)))
        d_pre = (s.d_act[b] * slope).astype(BF16)
        s.act[b] = act
        s.dp[0, b] = d_pre
        got_dp.append(push(s.dp.at[0, b], s.dp.at[1, b], PY))
        d_h2 += dot_t(d_pre, s.w1[:, cols])
    s.dh2[0] = d_h2.astype(BF16)
    got_dh2 = push(s.dh2.at[0], s.dh2.at[1], PX)
    for b in range(nb):
        cols = slice(b * half, (b + 1) * half)
        mlp += dot(s.act[b], s.w2[cols, :])
        s.vec[0, pl.ds(2 * x + b // 2, 1), (b % 2) * half:(b % 2 + 1) * half] = col_sum(
            s.dp[0, b].astype(F32)
        )
        s.act_t[cols, :] = s.act[b].T
    for i, yy in enumerate((y, 1 - y)):
        for j, cc in enumerate((c, 1 - c)):
            for zz in range(2):
                at = pl.ds(pl.multiple_of((zz * 4 + yy * 2 + cc) * fblk, fblk), fblk)
                s.act_g[i, j, zz] = s.act_t[at, :]
    got_act = push(s.act_g.at[1], s.act_r, PY)
    s.mlp[...] = mlp
    s.mlp_s[...] = s.mlp[other, :].astype(BF16)
    got_mlp = push(s.mlp_s, s.mlp_r, PX)
    dy_own = s.dy[own, :].astype(F32)
    s.vec[0, 5:6, :] = col_sum(dy * mlp) + b_fc2 * col_sum(dy_own)
    s.vec[0, 6:7, :] = col_sum(d_h2 * hat_m)
    s.vec[0, 7:8, :] = col_sum(d_h2)

    got_c1, got_z1, got_w1 = [None] * nb, [None] * nb, [None] * nb

    def fc1_product(b):
        if b == 0:
            got_h2()
        got_dp[b]()
        right = s.dp[:, b].reshape(4 * rows, half)
        left = jnp.concatenate([s.h2_g[0], s.h2_r[...]], axis=-1)
        s.fc1_cs[b] = dot(left[1], right).astype(BF16)
        got_c1[b] = push(s.fc1_cs.at[b], s.fc1_cr.at[b], PC)
        s.fc1[b] = dot(left[0], right)

    def fc1_core(b):
        got_c1[b]()
        s.fc1[b] = s.fc1[b] + s.fc1_cr[b].astype(F32)
        s.fc1_zs[b] = s.fc1[b, 2 * blk:, :].astype(BF16)
        got_z1[b] = push(s.fc1_zs.at[b], s.fc1_zr.at[b], PZ1)

    def fc1_z(b):
        got_z1[b]()
        s.fc1_ws[b] = (s.fc1[b, blk:2 * blk, :] + s.fc1_zr[b, blk:, :].astype(F32)).astype(BF16)
        got_w1[b] = push(s.fc1_ws.at[b], s.fc1_wr.at[b], PZ2)

    def fc1_end(b):
        got_w1[b]()
        out_w1[:, b * half:(b + 1) * half] = (
            s.fc1[b, :blk, :] + s.fc1_zr[b, :blk, :].astype(F32) + s.fc1_wr[b].astype(F32)
        )

    got_c2, got_x2, got_z2, got_w2 = [None] * 2, [None] * 2, [None] * 2, [None]

    def fc2_product(zz):
        if zz == 0:
            got_dm()
            got_act()
        right = s.dm[...].reshape(4 * rows, width)
        for j in (1, 0):
            left = jnp.concatenate([s.act_g[0, j, zz], s.act_r[j, zz]], axis=-1)
            total = dot(left, right)
            if j:
                s.fc2_cs[zz] = total.astype(BF16)
                got_c2[zz] = push(s.fc2_cs.at[zz], s.fc2_cr.at[zz], PC)
            else:
                s.fc2[zz] = total

    def fc2_core(zz):
        got_c2[zz]()
        s.fc2[zz] = s.fc2[zz] + s.fc2_cr[zz].astype(F32)
        s.fc2_xs[zz] = s.fc2[zz, :, theirs].astype(BF16)
        got_x2[zz] = push(s.fc2_xs.at[zz], s.fc2_xr.at[zz], PX)
        s.fc2_all[2 * x + zz] = s.fc2[zz, :, mine]

    def fc2_swap():
        for zz in range(2):
            got_x2[zz]()
            s.fc2_all[2 * (1 - x) + zz] = s.fc2_xr[zz].astype(F32)
        for i, t in enumerate((3, 1)):
            s.fc2_zs[i] = s.fc2_all[zs[t]].astype(BF16)
            got_z2[i] = push(s.fc2_zs.at[i], s.fc2_zr.at[i], PZ1)

    def fc2_z():
        got_z2[0]()
        s.fc2_ws[...] = (s.fc2_all[zs[2]] + s.fc2_zr[0].astype(F32)).astype(BF16)
        got_w2[0] = push(s.fc2_ws, s.fc2_wr, PZ2)

    def fc2_end():
        got_z2[1]()
        got_w2[0]()
        out_w2[...] = s.fc2_all[zs[0]] + s.fc2_zr[1].astype(F32) + s.fc2_wr[...].astype(F32)

    yrows, zrows = 4 * blk, 2 * blk
    got_c, got_y, got_zsq, got_wsq = [None] * 4, [None] * 4, [None] * 4, [None] * 4

    def square(i, left_t, right):
        for leave in (1, 0):
            cc = 1 - c if leave else c
            left = jnp.concatenate([blocks(left_t, cc, y), blocks(left_t, cc, 1 - y)], axis=0)
            total = dot(left, right)
            if leave:
                s.sq_cs[i] = total.astype(BF16)
                got_c[i] = push(s.sq_cs.at[i], s.sq_cr.at[i], PC)
            else:
                s.sq[i] = total

    def square_core(i):
        got_c[i]()
        s.sq[i] = s.sq[i] + s.sq_cr[i].astype(F32)
        s.sq_ys[i] = s.sq[i, yrows:, :].astype(BF16)
        got_y[i] = push(s.sq_ys.at[i], s.sq_yr.at[i], PY)

    def square_y(i):
        got_y[i]()
        s.sq[i, :yrows, :] = s.sq[i, :yrows, :] + s.sq_yr[i].astype(F32)
        s.sq_zs[i] = s.sq[i, zrows:yrows, :].astype(BF16)
        got_zsq[i] = push(s.sq_zs.at[i], s.sq_zr.at[i], PZ1)

    def square_z(i):
        got_zsq[i]()
        s.sq_ws[i] = (s.sq[i, blk:zrows, :] + s.sq_zr[i, blk:, :].astype(F32)).astype(BF16)
        got_wsq[i] = push(s.sq_ws.at[i], s.sq_wr.at[i], PZ2)

    def square_end(i):
        got_wsq[i]()
        (out_wo, out_wv, out_wk, out_wq)[i][...] = (
            s.sq[i, :blk, :] + s.sq_zr[i, :blk, :].astype(F32) + s.sq_wr[i].astype(F32)
        )

    tables = (s.vec, s.vec2)
    landings = (s.vec_r, s.vec2_r)
    got_v = [None] * 2

    def vector_send(g, step, peer):
        got_v[g] = push(tables[g].at[step], landings[g].at[step], peer)

    def vector_add(g, step):
        got_v[g]()
        tables[g][step + 1] = tables[g][step] + landings[g][step]

    fc1_product(0)
    fc1_product(1)
    fc1_core(0)

    got_dh2()
    d_h2 = s.dh2[0].astype(F32) + s.dh2[1].astype(F32)
    d_resid = dy + normalise_back(d_h2 * gain_m, hat_m, inv_m)
    s.d_resid[...] = d_resid
    d_branch = (scale_a * d_resid).astype(BF16)
    s.dbr[...] = d_branch
    s.da[...] = dot_t(d_branch, s.wo[mine, :]).astype(BF16)

    for pair in range(heads // 2):
        q2 = stack(s.q[:, lanes(pair)])
        da2 = stack(s.da[:, lanes(pair)])
        prob = s.prob[pair]
        s.dv[:, lanes(pair)] = dot(prob.astype(BF16).T, da2).astype(BF16)
        d_prob = dot_t(da2, s.v[:, lanes(pair)])
        delta = jnp.sum(d_prob * prob, axis=-1, keepdims=True)
        ds = (prob * (d_prob - delta)).astype(BF16)
        s.dq[:, lanes(pair)] = (unstack(dot(ds, s.k[:, lanes(pair)])) * scale).astype(BF16)
        s.dk[:, lanes(pair)] = (dot(ds.T, q2) * scale).astype(BF16)
    fc1_core(1)

    square(1, s.hk_t, s.dv[...])
    square(2, s.hk_t, s.dk[...])
    square_core(1)
    square(3, s.hq_t, s.dq[...])
    square_core(2)
    s.att_t[mine, :] = s.att[x].T
    s.att_t[theirs, :] = s.att[1 - x].T
    square(0, s.att_t, s.dbr[:, mine])
    square_core(3)

    fc1_product(2)
    square_core(0)
    fc1_product(3)
    fc1_core(2)

    dhk = dot_t(s.dk[...], s.wk[...]) + dot_t(s.dv[...], s.wv[...])
    dhq = dot_t(s.dq[...], s.wq[...])
    s.dx[0] = dhk[:2 * rows] * gain_k
    s.dx[1] = dhk[2 * rows:] * gain_k + dhq * gain_q
    s.dx_s[...] = s.dx[:, other, :].astype(BF16)
    fc1_core(3)
    fc1_z(0)

    dbr_own = s.dbr[own, :].astype(F32)
    s.vec2[0, 0:1, :] = col_sum(dbr_own)
    s.vec2[0, 1:2, :] = col_sum(s.d_resid[own, :] * s.branch[own, :])
    s.vec2[0, 2:3, :] = jnp.zeros((1, width), F32)
    s.vec2[0, 3:4, :] = jnp.zeros((1, width), F32)
    s.vec2[0, 2:3, mine] = col_sum(s.dq[...].astype(F32))
    s.vec2[0, 3:4, mine] = col_sum(s.dv[...].astype(F32))
    hat_low = s.hat[2 * rows:, :]
    s.vec2[0, 4:5, :] = col_sum(dhq * hat_low)
    s.vec2[0, 5:6, :] = col_sum(dhq)
    s.vec2[0, 6:7, :] = col_sum(dhk * s.hat[...])
    s.vec2[0, 7:8, :] = col_sum(dhk)
    vector_send(0, 0, PC)
    vector_send(1, 0, PC)

    fc2_product(0)
    fc1_z(1)
    fc2_product(1)
    fc2_core(0)
    fc2_core(1)
    got_dx = push(s.dx_s, s.dx_r, PX)
    vector_add(0, 0)
    vector_send(0, 1, PX)
    vector_add(1, 0)
    vector_send(1, 1, PX)
    fc1_z(2)
    square_y(1)
    fc1_z(3)
    fc2_swap()

    got_mlp()
    mlp_own = s.mlp[own, :] + s.mlp_r[...].astype(F32) + b_fc2
    out_block[0] = (s.resid[own, :] + scale_m * mlp_own).astype(BF16)

    vector_add(0, 1)
    vector_send(0, 2, PY)
    vector_add(1, 1)
    vector_send(1, 2, PY)
    square_y(2)
    square_z(1)
    fc2_z()
    square_y(3)
    square_z(2)
    square_y(0)
    vector_add(0, 2)
    vector_send(0, 3, PZ1)
    vector_add(1, 2)
    vector_send(1, 3, PZ1)
    square_z(3)

    got_dx()
    dx_l = s.dx[0, own, :] + s.dx_r[0].astype(F32)
    dx_q = s.dx[1, own, :] + s.dx_r[1].astype(F32)
    out_dl[0] = normalise_back(dx_l, hat_l, inv_l)
    out_dq[0] = s.d_resid[own, :] + normalise_back(dx_q, hat_q, inv_q)

    for b in range(nb):
        fc1_end(b)
    square_z(0)
    vector_add(0, 3)
    vector_send(0, 4, PZ2)
    vector_add(1, 3)
    vector_send(1, 4, PZ2)
    fc2_end()
    square_end(1)
    square_end(2)
    square_end(3)
    square_end(0)
    for g in range(2):
        vector_add(g, 4)
        out_vec[g * 8:g * 8 + 8, :] = tables[g][5]
    for copy in sent:
        copy.wait_send()


def fused(share, args):
    (queries, latents, positions, vis_ok, msk_ok, dy, w_query, w_key, w_value, w_out, w_fc1, w_fc2) = args[:12]
    vectors = args[12:]
    _, rows, width = queries.shape
    ff = w_fc1.shape[1]
    half = width // 2
    blk, fblk, hid = width // GROUPS, ff // GROUPS, ff // 2
    nb = hid // half
    pairs = half // (2 * HEAD_DIM)
    vm = pltpu.VMEM
    scratch = dict(
        send=pltpu.SemaphoreType.DMA((96,)),
        recv=pltpu.SemaphoreType.DMA((96,)),
        load=pltpu.SemaphoreType.DMA((16,)),
        dy=vm((2 * rows, width), BF16),
        qraw=vm((2 * rows, width), BF16),
        lraw=vm((2 * rows, width), BF16),
        ppos=vm((1, rows), jnp.int32),
        w2=vm((hid, width), BF16),
        w1=vm((width, hid), BF16),
        wo=vm((width, width), BF16),
        wk=vm((width, half), BF16),
        wv=vm((width, half), BF16),
        wq=vm((width, half), BF16),
        qin=vm((2 * rows, width), F32),
        hat=vm((4 * rows, width), F32),
        hq=vm((2 * rows, width), BF16),
        hk=vm((4 * rows, width), BF16),
        hq_t=vm((width, 2 * rows), BF16),
        hk_t=vm((width, 4 * rows), BF16),
        att_t=vm((width, 2 * rows), BF16),
        h2_t=vm((width, 2 * rows), BF16),
        act_t=vm((hid, 2 * rows), BF16),
        q=vm((2 * rows, half), BF16),
        k=vm((4 * rows, half), BF16),
        v=vm((4 * rows, half), BF16),
        prob=vm((pairs, 4 * rows, 4 * rows), F32),
        att=vm((2, 2 * rows, half), BF16),
        branch=vm((2 * rows, width), F32),
        resid=vm((2 * rows, width), F32),
        d_resid=vm((2 * rows, width), F32),
        mlp=vm((2 * rows, width), F32),
        mlp_s=vm((rows, width), BF16),
        mlp_r=vm((rows, width), BF16),
        d_act=vm((nb, 2 * rows, half), F32),
        dm=vm((2, 2 * rows, width), BF16),
        h2_g=vm((2, 2, 4 * blk, 2 * rows), BF16),
        h2_r=vm((2, 4 * blk, 2 * rows), BF16),
        act=vm((nb, 2 * rows, half), BF16),
        act_g=vm((2, 2, 2, fblk, 2 * rows), BF16),
        act_r=vm((2, 2, fblk, 2 * rows), BF16),
        dp=vm((2, nb, 2 * rows, half), BF16),
        dh2=vm((2, 2 * rows, width), BF16),
        dbr=vm((2 * rows, width), BF16),
        da=vm((2 * rows, half), BF16),
        dq=vm((2 * rows, half), BF16),
        dk=vm((4 * rows, half), BF16),
        dv=vm((4 * rows, half), BF16),
        dx=vm((2, 2 * rows, width), F32),
        dx_s=vm((2, rows, width), BF16),
        dx_r=vm((2, rows, width), BF16),
        sq=vm((4, 8 * blk, half), F32),
        sq_cs=vm((4, 8 * blk, half), BF16),
        sq_cr=vm((4, 8 * blk, half), BF16),
        sq_ys=vm((4, 4 * blk, half), BF16),
        sq_yr=vm((4, 4 * blk, half), BF16),
        sq_zs=vm((4, 2 * blk, half), BF16),
        sq_zr=vm((4, 2 * blk, half), BF16),
        sq_ws=vm((4, blk, half), BF16),
        sq_wr=vm((4, blk, half), BF16),
        fc2=vm((2, fblk, width), F32),
        fc2_cs=vm((2, fblk, width), BF16),
        fc2_cr=vm((2, fblk, width), BF16),
        fc2_xs=vm((2, fblk, half), BF16),
        fc2_xr=vm((2, fblk, half), BF16),
        fc2_all=vm((4, fblk, half), F32),
        fc2_zs=vm((2, fblk, half), BF16),
        fc2_zr=vm((2, fblk, half), BF16),
        fc2_ws=vm((fblk, half), BF16),
        fc2_wr=vm((fblk, half), BF16),
        fc1=vm((nb, 4 * blk, half), F32),
        fc1_cs=vm((nb, 4 * blk, half), BF16),
        fc1_cr=vm((nb, 4 * blk, half), BF16),
        fc1_zs=vm((nb, 2 * blk, half), BF16),
        fc1_zr=vm((nb, 2 * blk, half), BF16),
        fc1_ws=vm((nb, blk, half), BF16),
        fc1_wr=vm((nb, blk, half), BF16),
        vec=vm((6, 8, width), F32),
        vec_r=vm((5, 8, width), F32),
        vec2=vm((6, 8, width), F32),
        vec2_r=vm((5, 8, width), F32),
    )
    ANY = pl.BlockSpec(memory_space=pl.ANY)
    VMEM = pl.BlockSpec(memory_space=pltpu.VMEM)
    sds = jax.ShapeDtypeStruct
    return pl.pallas_call(
        functools.partial(kernel, (rows, width, ff, share)),
        out_shape=(
            sds((1, rows, width), BF16),
            sds((1, rows, width), F32),
            sds((1, rows, width), F32),
            sds((blk, half), F32),
            sds((blk, half), F32),
            sds((blk, half), F32),
            sds((blk, half), F32),
            sds((blk, ff // 2), F32),
            sds((fblk, half), F32),
            sds((16, width), F32),
        ),
        in_specs=[ANY, ANY, VMEM, VMEM, VMEM, ANY] + [ANY] * 6 + [VMEM] * 13,
        out_specs=[VMEM] * 10,
        scratch_shapes=[scratch],
        compiler_params=pltpu.CompilerParams(
            collective_id=0, has_side_effects=True, vmem_limit_bytes=60 << 20
        ),
        cost_estimate=pl.CostEstimate(
            flops=6 * 10**9, bytes_accessed=16 * 10**6, transcendentals=10**6
        ),
    )(queries, latents, positions, vis_ok, msk_ok, dy, w_query, w_key, w_value, w_out, w_fc1, w_fc2, *vectors)


def finish_kernel(count, *refs):
    arrays, table = refs[:count], refs[count]
    outs, rows = refs[count + 1:2 * count + 1], refs[2 * count + 1:-1]
    sems = refs[-1]
    copies = [
        pltpu.make_async_copy(src, dst, sems.at[i]) for i, (src, dst) in enumerate(zip(arrays, outs))
    ]
    for copy in copies:
        copy.start()
    width = table.shape[1]
    parts = rows[0].shape[0] // width
    for k in range(parts):
        rows[0][k * width:(k + 1) * width] = table[k, :]
    for k, row in enumerate(rows[1:]):
        row[...] = table[parts + k, :]
    for copy in copies:
        copy.wait()


def finish(arrays, table, ff):
    count, width = len(arrays), table.shape[1]
    sds = jax.ShapeDtypeStruct
    vectors = table.shape[0] - ff // width
    ANY = pl.BlockSpec(memory_space=pl.ANY)
    VMEM = pl.BlockSpec(memory_space=pltpu.VMEM)
    return pl.pallas_call(
        functools.partial(finish_kernel, count),
        out_shape=tuple(sds(a.shape, a.dtype) for a in arrays)
        + (sds((ff,), F32),)
        + (sds((width,), F32),) * vectors,
        in_specs=[VMEM] * (count + 1),
        out_specs=[ANY] * count + [VMEM] * (1 + vectors),
        scratch_shapes=[pltpu.SemaphoreType.DMA((count,))],
    )(*arrays, table)


def per_device(
    queries, latents, positions, visible_valid, masked_valid,
    w_query, b_query, w_key, w_value, b_value, w_out, b_out, w_fc1, b_fc1, w_fc2, b_fc2,
    gain_query, shift_query, gain_keys, shift_keys, gain_mlp, shift_mlp, scale_attn, scale_mlp,
    out_grad,
):
    parts = lax.axis_size("dp")
    share = parts // GROUPS
    out = fused(
        share,
        (
            queries, latents, positions, visible_valid, masked_valid, out_grad,
            w_query, w_key, w_value, w_out, w_fc1, w_fc2,
            b_query, b_value, b_out, b_fc1, b_fc2,
            gain_query, shift_query, gain_keys, shift_keys, gain_mlp, shift_mlp, scale_attn, scale_mlp,
        ),
    )
    block_out, d_queries, d_latents, wq, wk, wv, wo, w1, w2, vec = out
    if share > 1:
        groups = [[n * share + i for i in range(share)] for n in range(GROUPS)]
        wq, wk, wv, wo, w1, w2 = (
            lax.psum_scatter(
                w, "dp", scatter_dimension=0, axis_index_groups=groups, tiled=True
            )
            for w in (wq, wk, wv, wo, w1, w2)
        )
        vec = lax.psum(vec, "dp", axis_index_groups=groups)
    arrays = (block_out, d_queries, d_latents, wq, wk, wv, wo, w1, w2)
    done = finish(arrays, vec, w_fc1.shape[1])
    block_out, d_queries, d_latents, wq, wk, wv, wo, w1, w2, b1 = done[:10]
    b2, sm, gm, hm, bo, sa, bq, bv, gq, hq, gk, hk = done[10:]
    return (
        block_out, d_queries, d_latents,
        wq, bq, wk, wv, bv, wo, bo, w1, b1, w2, b2,
        gq, hq, gk, hk, gm, hm, sa, sm,
    )


def solution(mesh):
    rows3 = P("dp", "qry", None)
    split = P("dp", "qry")
    full = P()
    return jax.shard_map(
        per_device,
        mesh=mesh,
        in_specs=(rows3, rows3, split, P("dp", None), P("dp", None)) + (full,) * 19 + (rows3,),
        out_specs=(
            rows3, rows3, rows3,
            split, full, split, split, full, split, full, split, full, split,
        ) + (full,) * 9,
        check_vma=False,
    )
```

time: 87.3 us -> 74.6 us (0.85)
  Pallas kernels: 86.4 us -> 73.7 us
    pallas_call x1, Pallas kernels: 83.2 us -> 70.5 us  [fused(): pl.pallas_call(functools.partial(kernel, (rows, width, ff, share)), out_s...]
where the time goes in v2:
time: 74.6 us; the launch traced here: 74.3 us
  Pallas kernels  73.7 us (99%)
    pallas_call x1, Pallas kernels, fused(): pl.pallas_call(functools.partial(kernel, (rows, width, ff, share)), out_s...  70.5 us
    pallas_call x1, Pallas kernels, finish(): pl.pallas_call(functools.partial(finish_kernel, count), out_shape=tuple((...  3.2 us

profile of v2, /device:TPU:0, one launch (start us, length us, event | category | flops | bytes accessed | tf_op | source)
XLA Modules:
  0.0 74.3 jit_solution(3951100963293837454)
XLA Ops:
  0.7 70.5 %shard_map.408 = (bf16[1,64,768]{2,1,0:T(8,128)(2,1)}, f32[1,64,768]{2,1,0:T(8,128)}, f32[1,64,768]{2,1,0:T(8,128)}, f32[48,384]{1,0:T(8,128)}, f32[48,384]{1,0:...) custom-call(bf16[1,64,768]{2,1,0:T(8,128)(2,1)} %queries.1, ...), custom_call_target="tpu_custom_call" | custom-call | flops 6000000000 | bytes 16000000 | tf_op jit(solution)/shard_map/pallas_call | solution.py:653
  71.1 3.2 %shard_map.409 = (bf16[1,64,768]{2,1,0:T(8,128)(2,1)}, f32[1,64,768]{2,1,0:T(8,128)}, f32[1,64,768]{2,1,0:T(8,128)}, f32[48,384]{1,0:T(8,128)}, f32[48,384]{1,0:...) custom-call(bf16[1,64,768]{2,1,0:T(8,128)(2,1)} %get-tuple-element.5, ...), custom_call_target="tpu_custom_call" | custom-call | tf_op jit(solution)/shard_map/pallas_call | solution.py:704

commit v3 on v2

--- a/solution.py
+++ b/solution.py
@@ -76,12 +76,6 @@
 ):
     s = types.SimpleNamespace(**s)
     rows, width, ff, share = shape
-    (b_query, b_value, b_out, b_fc1, b_fc2, gain_q, shift_q, gain_k, shift_k, gain_m, shift_m,
-     scale_a, scale_m) = (
-        ref[...].reshape(1, -1)
-        for ref in (b_query, b_value, b_out, b_fc1, b_fc2, gain_q, shift_q, gain_k, shift_k, gain_m,
-                    shift_m, scale_a, scale_m)
-    )
     half = width // 2
     heads = half // HEAD_DIM
     blk = width // GROUPS
@@ -107,6 +101,9 @@
     PC = dev(z, y, 1 - c, x)
     PZ1 = dev(zs[1], y, c, x)
     PZ2 = dev(zs[2], y, c, x)
+    PYZ1 = dev(zs[1], 1 - y, c, x)
+    z_low = z % 2
+    z_high = z // 2
 
     counter = [0]
     sent = []
@@ -126,6 +123,25 @@
         sent.append(copy)
         arrival = copy if landing is None else describe(landing)
         return arrival.wait_recv
+
+    barrier = pltpu.get_barrier_semaphore()
+
+    def tell(sem, peer):
+        pl.semaphore_signal(sem, inc=1, device_id=peer, device_id_type=MESH)
+
+    def tell_z(sem):
+        @pl.when(z > 0)
+        def _():
+            tell(sem, dev(z - 1, y, c, x))
+
+        @pl.when(z < 3)
+        def _():
+            tell(sem, dev(z + 1, y, c, x))
+
+    z_links = 2 - (z + 3) // 3 + (z + 1) // 2 - z // 3
+    for peer in (PX, PY, PC):
+        tell(barrier, peer)
+    tell_z(barrier)
 
     loads = []
 
@@ -142,30 +158,41 @@
     mine = pl.ds(pl.multiple_of(x * half, half), half)
     theirs = pl.ds(pl.multiple_of((1 - x) * half, half), half)
     units = pl.ds(pl.multiple_of(x * hid, hid), hid)
+
+    def row_of(ref, i):
+        wait = load(ref, s.rows.at[i])
+
+        def value():
+            wait()
+            return s.rows[i].reshape(1, width)
+
+        return value
+
     load_q = load(queries.at[0], s.qraw.at[own])
+    load_p = load(positions, s.pos)
     load_l = load(latents.at[0], s.lraw.at[own])
-    load_dy = load(dy_in.at[0], s.dy.at[own])
+    gain_q, shift_q, gain_k, shift_k = (
+        row_of(ref, i) for i, ref in enumerate((gain_q, shift_q, gain_k, shift_k))
+    )
     load_wk = load(w_key.at[:, mine], s.wk)
     load_wv = load(w_value.at[:, mine], s.wv)
     load_wq = load(w_query.at[:, mine], s.wq)
+    b_query, b_value, b_out, b_fc2, gain_m, shift_m, scale_a, scale_m = (
+        row_of(ref, 4 + i)
+        for i, ref in enumerate((b_query, b_value, b_out, b_fc2, gain_m, shift_m, scale_a, scale_m))
+    )
+    load_b1 = load(b_fc1, s.b_fc1)
+    load_ok = [load(vis_ok, s.ok.at[0]), load(msk_ok, s.ok.at[1])]
+    load_dy = load(dy_in.at[0], s.dy.at[0, own])
     load_w2 = load(w_fc2.at[units], s.w2)
     load_wo = load(w_out, s.wo)
     load_w1 = load(w_fc1.at[:, units], s.w1)
 
-    barrier = pltpu.get_barrier_semaphore()
-    peers = [PX, PY, PC, PZ1, PZ2]
-    for peer in peers:
-        pl.semaphore_signal(barrier, inc=1, device_id=peer, device_id_type=MESH)
-    pl.semaphore_wait(barrier, len(peers))
-
-    got_p = push(positions, s.ppos, PX)
-    got_q = push(queries.at[0], s.qraw.at[own], PX, s.qraw.at[other])
-    got_l = push(latents.at[0], s.lraw.at[own], PX, s.lraw.at[other])
-    got_dy = push(dy_in.at[0], s.dy.at[own], PX, s.dy.at[other])
-
     eye = lax.broadcasted_iota(jnp.int32, (rows, rows), 0) == lax.broadcasted_iota(
         jnp.int32, (rows, rows), 1
     )
+
+    gain_q, shift_q, gain_k, shift_k = gain_q(), shift_q(), gain_k(), shift_k()
 
     def qry_half(pos_ref, at, low_at):
         row = jnp.broadcast_to(pos_ref[...].astype(F32), (rows, rows))
@@ -187,10 +214,6 @@
         s.hk[at, :] = hkl
         return hat, inv, hkl
 
-    my_b_value = jnp.where(x == 0, b_value[:, :half], b_value[:, half:])
-    my_b_query = jnp.where(x == 0, b_query[:, :half], b_query[:, half:])
-    my_b_fc1 = jnp.where(x == 0, b_fc1[:, :hid], b_fc1[:, hid:])
-
     def project(hq, hkq, hkl, at, low_at):
         both = jnp.concatenate([hkl, hkq], axis=0)
         k = dot(both, s.wk[...]).astype(BF16)
@@ -202,21 +225,44 @@
         s.q[at, :] = (dot(hq, s.wq[...]) + my_b_query).astype(BF16)
 
     load_q()
+    load_p()
+    hat_q, inv_q, hq, hkq = qry_half(s.pos, own, low_own)
     load_l()
-    hat_q, inv_q, hq, hkq = qry_half(positions, own, low_own)
     hat_l, inv_l, hkl = lat_half(own)
+
+    pl.semaphore_wait(barrier, 3 + z_links)
+    got_p = push(positions, s.ppos, PX)
+    got_q = push(queries.at[0], s.qraw.at[own], PX, s.qraw.at[other])
+    got_l = push(latents.at[0], s.lraw.at[own], PX, s.lraw.at[other])
+    got_dy = push(dy_in.at[0], s.dy.at[0, own], PX, s.dy.at[0, other])
+    got_dy_y = push(dy_in.at[0], s.dy.at[1, own], PY)
+    got_dy_z = push(dy_in.at[0], s.dy.at[2, own], PZ1)
+    tell_z(s.ready)
+
     load_wk()
     load_wv()
     load_wq()
+    b_query, b_value, b_out, b_fc2, gain_m, shift_m, scale_a, scale_m = (
+        value() for value in (b_query, b_value, b_out, b_fc2, gain_m, shift_m, scale_a, scale_m)
+    )
+    load_b1()
+    my_b_value = jnp.where(x == 0, b_value[:, :half], b_value[:, half:])
+    my_b_query = jnp.where(x == 0, b_query[:, :half], b_query[:, half:])
+    b_fc1 = s.b_fc1[...].reshape(1, ff)
+    my_b_fc1 = jnp.where(x == 0, b_fc1[:, :hid], b_fc1[:, hid:])
     project(hq, hkq, hkl, own, low_own)
     got_p()
     got_q()
     _, _, hq_o, hkq_o = qry_half(s.ppos, other, low_other)
+    pl.semaphore_wait(s.ready, z_links)
+    got_dy_yz = push(dy_in.at[0], s.dy.at[3, own], PYZ1)
     got_l()
     _, _, hkl_o = lat_half(other)
     project(hq_o, hkq_o, hkl_o, other, low_other)
-
-    ok = jnp.concatenate([vis_ok[...], msk_ok[...]], axis=1) > 0
+    for wait in load_ok:
+        wait()
+
+    ok = jnp.concatenate([s.ok[0], s.ok[1]], axis=1) > 0
     lane = lax.broadcasted_iota(jnp.int32, (2 * rows, 2 * HEAD_DIM), 1)
     first = lane < HEAD_DIM
 
@@ -240,25 +286,25 @@
         s.att[x, :, lanes(pair)] = unstack(dot(prob.astype(BF16), s.v[:, lanes(pair)])).astype(BF16)
     got_att = push(s.att.at[x], s.att.at[x], PX, s.att.at[1 - x])
 
+    got_dy()
+    got_dy_y2 = push(s.dy.at[0, other], s.dy.at[1, other], PY)
+    got_dy_z2 = push(s.dy.at[0, other], s.dy.at[2, other], PZ1)
+    got_dy_yz2 = push(s.dy.at[0, other], s.dy.at[3, other], PYZ1)
+    s.hq_t[...] = s.hq[...].T
+    s.hk_t[...] = s.hk[...].T
     load_dy()
-    got_dy()
     load_w2()
-    dy = s.dy[...].astype(F32)
+    dy = s.dy[0].astype(F32)
     d_mlp = (scale_m * dy).astype(BF16)
     s.dm[0] = d_mlp
-    got_dm = push(s.dm.at[0], s.dm.at[1], PY)
     for b in range(nb):
         s.d_act[b] = dot_t(d_mlp, s.w2[b * half:(b + 1) * half, :])
-    s.vec[0, 4:5, :] = col_sum((scale_m * s.dy[own, :].astype(F32)).astype(BF16).astype(F32))
-    s.hq_t[...] = s.hq[...].T
-    s.hk_t[...] = s.hk[...].T
     load_wo()
+    s.branch[...] = dot(s.att[x], s.wo[mine, :]) + b_out
     got_att()
 
-    branch = dot(s.att[0], s.wo[:half, :]) + dot(s.att[1], s.wo[half:, :]) + b_out
-    s.branch[...] = branch
+    branch = s.branch[...] + dot(s.att[1 - x], s.wo[theirs, :])
     resid = s.qin[...] + scale_a * branch
-    s.resid[...] = resid
     hat_m, inv_m = normalise(resid)
     h_two = (hat_m * gain_m + shift_m).astype(BF16)
 
@@ -272,14 +318,11 @@
         )
 
     s.h2_t[...] = h_two.T
-    for i, yy in enumerate((y, 1 - y)):
-        s.h2_g[i, 0] = blocks(s.h2_t, c, yy)
-        s.h2_g[i, 1] = blocks(s.h2_t, 1 - c, yy)
+    s.h2_g[1, 0] = blocks(s.h2_t, c, 1 - y)
+    s.h2_g[1, 1] = blocks(s.h2_t, 1 - c, 1 - y)
     got_h2 = push(s.h2_g.at[1], s.h2_r, PY)
     load_w1()
-    mlp = jnp.zeros((2 * rows, width), F32)
     d_h2 = jnp.zeros((2 * rows, width), F32)
-    s.vec[0, 0:4, :] = jnp.zeros((4, width), F32)
     got_dp = []
     for b in range(nb):
         cols = slice(b * half, (b + 1) * half)
@@ -294,23 +337,36 @@
         d_h2 += dot_t(d_pre, s.w1[:, cols])
     s.dh2[0] = d_h2.astype(BF16)
     got_dh2 = push(s.dh2.at[0], s.dh2.at[1], PX)
+
+    for b in range(nb):
+        s.act_t[b * half:(b + 1) * half, :] = s.act[b].T
+    got_act = []
+    for i, (zz, yy) in enumerate(
+        ((z_low, y), (z_low, 1 - y), (1 - z_low, y), (1 - z_low, 1 - y))
+    ):
+        for j, cc in enumerate((c, 1 - c)):
+            at = pl.ds(pl.multiple_of((zz * 4 + yy * 2 + cc) * fblk, fblk), fblk)
+            s.act_s[i, j] = s.act_t[at, :]
+        if i:
+            got_act.append(push(s.act_s.at[i], s.act_r.at[i - 1], (PY, PZ1, PYZ1)[i - 1]))
+
+    s.branch[...] = branch
+    s.resid[...] = resid
+    s.h2_g[0, 0] = blocks(s.h2_t, c, y)
+    s.h2_g[0, 1] = blocks(s.h2_t, 1 - c, y)
+    mlp = jnp.zeros((2 * rows, width), F32)
+    s.vec[0, 0:4, :] = jnp.zeros((4, width), F32)
     for b in range(nb):
         cols = slice(b * half, (b + 1) * half)
         mlp += dot(s.act[b], s.w2[cols, :])
         s.vec[0, pl.ds(2 * x + b // 2, 1), (b % 2) * half:(b % 2 + 1) * half] = col_sum(
             s.dp[0, b].astype(F32)
         )
-        s.act_t[cols, :] = s.act[b].T
-    for i, yy in enumerate((y, 1 - y)):
-        for j, cc in enumerate((c, 1 - c)):
-            for zz in range(2):
-                at = pl.ds(pl.multiple_of((zz * 4 + yy * 2 + cc) * fblk, fblk), fblk)
-                s.act_g[i, j, zz] = s.act_t[at, :]
-    got_act = push(s.act_g.at[1], s.act_r, PY)
     s.mlp[...] = mlp
     s.mlp_s[...] = s.mlp[other, :].astype(BF16)
     got_mlp = push(s.mlp_s, s.mlp_r, PX)
-    dy_own = s.dy[own, :].astype(F32)
+    dy_own = s.dy[0, own, :].astype(F32)
+    s.vec[0, 4:5, :] = col_sum(s.dm[0, own, :].astype(F32))
     s.vec[0, 5:6, :] = col_sum(dy * mlp) + b_fc2 * col_sum(dy_own)
     s.vec[0, 6:7, :] = col_sum(d_h2 * hat_m)
     s.vec[0, 7:8, :] = col_sum(d_h2)
@@ -344,49 +400,42 @@
             s.fc1[b, :blk, :] + s.fc1_zr[b, :blk, :].astype(F32) + s.fc1_wr[b].astype(F32)
         )
 
-    got_c2, got_x2, got_z2, got_w2 = [None] * 2, [None] * 2, [None] * 2, [None]
-
-    def fc2_product(zz):
-        if zz == 0:
-            got_dm()
-            got_act()
-        right = s.dm[...].reshape(4 * rows, width)
+    got_c2, got_x2, got_w2 = [None], [None], [None]
+
+    def fc2_product():
+        for got in [got_dy_y, got_dy_z, got_dy_yz, got_dy_y2, got_dy_z2, got_dy_yz2] + got_act:
+            got()
+        for g in range(1, 4):
+            s.dm[g] = (scale_m * s.dy[g].astype(F32)).astype(BF16)
+        right = s.dm[...].reshape(8 * rows, width)
         for j in (1, 0):
-            left = jnp.concatenate([s.act_g[0, j, zz], s.act_r[j, zz]], axis=-1)
+            left = jnp.concatenate([s.act_s[0, j]] + [s.act_r[g, j] for g in range(3)], axis=-1)
             total = dot(left, right)
             if j:
-                s.fc2_cs[zz] = total.astype(BF16)
-                got_c2[zz] = push(s.fc2_cs.at[zz], s.fc2_cr.at[zz], PC)
+                s.fc2_cs[...] = total.astype(BF16)
+                got_c2[0] = push(s.fc2_cs, s.fc2_cr, PC)
             else:
-                s.fc2[zz] = total
-
-    def fc2_core(zz):
-        got_c2[zz]()
-        s.fc2[zz] = s.fc2[zz] + s.fc2_cr[zz].astype(F32)
-        s.fc2_xs[zz] = s.fc2[zz, :, theirs].astype(BF16)
-        got_x2[zz] = push(s.fc2_xs.at[zz], s.fc2_xr.at[zz], PX)
-        s.fc2_all[2 * x + zz] = s.fc2[zz, :, mine]
+                s.fc2[...] = total
+
+    def fc2_core():
+        got_c2[0]()
+        s.fc2[...] = s.fc2[...] + s.fc2_cr[...].astype(F32)
+        s.fc2_xs[...] = s.fc2[:, theirs].astype(BF16)
+        got_x2[0] = push(s.fc2_xs, s.fc2_xr, PX)
+        s.fc2_all[x] = s.fc2[:, mine]
 
     def fc2_swap():
-        for zz in range(2):
-            got_x2[zz]()
-            s.fc2_all[2 * (1 - x) + zz] = s.fc2_xr[zz].astype(F32)
-        for i, t in enumerate((3, 1)):
-            s.fc2_zs[i] = s.fc2_all[zs[t]].astype(BF16)
-            got_z2[i] = push(s.fc2_zs.at[i], s.fc2_zr.at[i], PZ1)
-
-    def fc2_z():
-        got_z2[0]()
-        s.fc2_ws[...] = (s.fc2_all[zs[2]] + s.fc2_zr[0].astype(F32)).astype(BF16)
+        got_x2[0]()
+        s.fc2_all[1 - x] = s.fc2_xr[...].astype(F32)
+        s.fc2_ws[...] = s.fc2_all[1 - z_high].astype(BF16)
         got_w2[0] = push(s.fc2_ws, s.fc2_wr, PZ2)
 
     def fc2_end():
-        got_z2[1]()
         got_w2[0]()
-        out_w2[...] = s.fc2_all[zs[0]] + s.fc2_zr[1].astype(F32) + s.fc2_wr[...].astype(F32)
+        out_w2[...] = s.fc2_all[z_high] + s.fc2_wr[...].astype(F32)
 
     yrows, zrows = 4 * blk, 2 * blk
-    got_c, got_y, got_zsq, got_wsq = [None] * 4, [None] * 4, [None] * 4, [None] * 4
+    got_c, got_y, got_yr, got_zsq, got_wsq = ([None] * 4 for _ in range(5))
 
     def square(i, left_t, right):
         for leave in (1, 0):
@@ -402,24 +451,31 @@
     def square_core(i):
         got_c[i]()
         s.sq[i] = s.sq[i] + s.sq_cr[i].astype(F32)
-        s.sq_ys[i] = s.sq[i, yrows:, :].astype(BF16)
-        got_y[i] = push(s.sq_ys.at[i], s.sq_yr.at[i], PY)
+        s.sq_ys[i, 1] = s.sq[i, yrows + zrows:, :].astype(BF16)
+        got_y[i] = push(s.sq_ys.at[i, 1], s.sq_yr.at[i, 1], PY)
+
+    def square_core_rest(i):
+        s.sq_ys[i, 0] = s.sq[i, yrows:yrows + zrows, :].astype(BF16)
+        got_yr[i] = push(s.sq_ys.at[i, 0], s.sq_yr.at[i, 0], PY)
 
     def square_y(i):
         got_y[i]()
-        s.sq[i, :yrows, :] = s.sq[i, :yrows, :] + s.sq_yr[i].astype(F32)
-        s.sq_zs[i] = s.sq[i, zrows:yrows, :].astype(BF16)
+        s.sq_zs[i] = (s.sq[i, zrows:yrows, :] + s.sq_yr[i, 1].astype(F32)).astype(BF16)
         got_zsq[i] = push(s.sq_zs.at[i], s.sq_zr.at[i], PZ1)
 
     def square_z(i):
+        got_yr[i]()
         got_zsq[i]()
-        s.sq_ws[i] = (s.sq[i, blk:zrows, :] + s.sq_zr[i, blk:, :].astype(F32)).astype(BF16)
+        s.sq[i, :zrows, :] = (
+            s.sq[i, :zrows, :] + s.sq_yr[i, 0].astype(F32) + s.sq_zr[i].astype(F32)
+        )
+        s.sq_ws[i] = s.sq[i, blk:zrows, :].astype(BF16)
         got_wsq[i] = push(s.sq_ws.at[i], s.sq_wr.at[i], PZ2)
 
     def square_end(i):
         got_wsq[i]()
         (out_wo, out_wv, out_wk, out_wq)[i][...] = (
-            s.sq[i, :blk, :] + s.sq_zr[i, :blk, :].astype(F32) + s.sq_wr[i].astype(F32)
+            s.sq[i, :blk, :] + s.sq_wr[i].astype(F32)
         )
 
     tables = (s.vec, s.vec2)
@@ -433,124 +489,144 @@
         got_v[g]()
         tables[g][step + 1] = tables[g][step] + landings[g][step]
 
+    live = types.SimpleNamespace()
+
+    def d_resid():
+        got_dh2()
+        d_h2 = s.dh2[0].astype(F32) + s.dh2[1].astype(F32)
+        d_resid = dy + normalise_back(d_h2 * gain_m, hat_m, inv_m)
+        s.d_resid[...] = d_resid
+        d_branch = (scale_a * d_resid).astype(BF16)
+        s.dbr[...] = d_branch
+        s.da[...] = dot_t(d_branch, s.wo[mine, :]).astype(BF16)
+
+    def attention_back():
+        for pair in range(heads // 2):
+            q2 = stack(s.q[:, lanes(pair)])
+            da2 = stack(s.da[:, lanes(pair)])
+            prob = s.prob[pair]
+            s.dv[:, lanes(pair)] = dot(prob.astype(BF16).T, da2).astype(BF16)
+            d_prob = dot_t(da2, s.v[:, lanes(pair)])
+            delta = jnp.sum(d_prob * prob, axis=-1, keepdims=True)
+            ds = (prob * (d_prob - delta)).astype(BF16)
+            s.dq[:, lanes(pair)] = (unstack(dot(ds, s.k[:, lanes(pair)])) * scale).astype(BF16)
+            s.dk[:, lanes(pair)] = (dot(ds.T, q2) * scale).astype(BF16)
+
+    def square_product(i):
+        if i == 0:
+            s.att_t[mine, :] = s.att[x].T
+            s.att_t[theirs, :] = s.att[1 - x].T
+            square(0, s.att_t, s.dbr[:, mine])
+        elif i < 3:
+            square(i, s.hk_t, (s.dv, s.dk)[i - 1][...])
+        else:
+            square(3, s.hq_t, s.dq[...])
+
+    def norms_back():
+        dhk = dot_t(s.dk[...], s.wk[...]) + dot_t(s.dv[...], s.wv[...])
+        dhq = dot_t(s.dq[...], s.wq[...])
+        s.dx[0] = dhk[:2 * rows] * gain_k
+        s.dx[1] = dhk[2 * rows:] * gain_k + dhq * gain_q
+        s.dx_s[...] = s.dx[:, other, :].astype(BF16)
+        s.vec2[0, 0:1, :] = col_sum(s.dbr[own, :].astype(F32))
+        s.vec2[0, 1:2, :] = col_sum(s.d_resid[own, :] * s.branch[own, :])
+        s.vec2[0, 2:3, :] = jnp.zeros((1, width), F32)
+        s.vec2[0, 3:4, :] = jnp.zeros((1, width), F32)
+        s.vec2[0, 2:3, mine] = col_sum(s.dq[...].astype(F32))
+        s.vec2[0, 3:4, mine] = col_sum(s.dv[...].astype(F32))
+        s.vec2[0, 4:5, :] = col_sum(dhq * s.hat[2 * rows:, :])
+        s.vec2[0, 5:6, :] = col_sum(dhq)
+        s.vec2[0, 6:7, :] = col_sum(dhk * s.hat[...])
+        s.vec2[0, 7:8, :] = col_sum(dhk)
+
+    def norms_send():
+        live.got_dx = push(s.dx_s, s.dx_r, PX)
+
+    def norms_end():
+        live.got_dx()
+        dx_l = s.dx[0, own, :] + s.dx_r[0].astype(F32)
+        dx_q = s.dx[1, own, :] + s.dx_r[1].astype(F32)
+        out_dl[0] = normalise_back(dx_l, hat_l, inv_l)
+        out_dq[0] = s.d_resid[own, :] + normalise_back(dx_q, hat_q, inv_q)
+
+    def block_end():
+        got_mlp()
+        mlp_own = s.mlp[own, :] + s.mlp_r[...].astype(F32) + b_fc2
+        out_block[0] = (s.resid[own, :] + scale_m * mlp_own).astype(BF16)
+
+    routes = (PZ2, PZ1, PY, PX, PC)
+
+    def vector(g, step):
+        if step:
+            vector_add(g, step - 1)
+        if step < 5:
+            vector_send(g, step, routes[step])
+        else:
+            out_vec[g * 8:g * 8 + 8, :] = tables[g][5]
+
+    V, K, Q, O = 1, 2, 3, 0
+    vector(0, 0)
     fc1_product(0)
+    d_resid()
+    fc1_core(0)
+    attention_back()
     fc1_product(1)
-    fc1_core(0)
-
-    got_dh2()
-    d_h2 = s.dh2[0].astype(F32) + s.dh2[1].astype(F32)
-    d_resid = dy + normalise_back(d_h2 * gain_m, hat_m, inv_m)
-    s.d_resid[...] = d_resid
-    d_branch = (scale_a * d_resid).astype(BF16)
-    s.dbr[...] = d_branch
-    s.da[...] = dot_t(d_branch, s.wo[mine, :]).astype(BF16)
-
-    for pair in range(heads // 2):
-        q2 = stack(s.q[:, lanes(pair)])
-        da2 = stack(s.da[:, lanes(pair)])
-        prob = s.prob[pair]
-        s.dv[:, lanes(pair)] = dot(prob.astype(BF16).T, da2).astype(BF16)
-        d_prob = dot_t(da2, s.v[:, lanes(pair)])
-        delta = jnp.sum(d_prob * prob, axis=-1, keepdims=True)
-        ds = (prob * (d_prob - delta)).astype(BF16)
-        s.dq[:, lanes(pair)] = (unstack(dot(ds, s.k[:, lanes(pair)])) * scale).astype(BF16)
-        s.dk[:, lanes(pair)] = (dot(ds.T, q2) * scale).astype(BF16)
+    norms_back()
+    vector(0, 1)
+    fc1_product(2)
+    square_product(V)
     fc1_core(1)
-
-    square(1, s.hk_t, s.dv[...])
-    square(2, s.hk_t, s.dk[...])
-    square_core(1)
-    square(3, s.hq_t, s.dq[...])
-    square_core(2)
-    s.att_t[mine, :] = s.att[x].T
-    s.att_t[theirs, :] = s.att[1 - x].T
-    square(0, s.att_t, s.dbr[:, mine])
-    square_core(3)
-
-    fc1_product(2)
-    square_core(0)
+    square_product(O)
+    fc1_core(2)
+    block_end()
+    square_core(V)
+    vector(1, 0)
     fc1_product(3)
-    fc1_core(2)
-
-    dhk = dot_t(s.dk[...], s.wk[...]) + dot_t(s.dv[...], s.wv[...])
-    dhq = dot_t(s.dq[...], s.wq[...])
-    s.dx[0] = dhk[:2 * rows] * gain_k
-    s.dx[1] = dhk[2 * rows:] * gain_k + dhq * gain_q
-    s.dx_s[...] = s.dx[:, other, :].astype(BF16)
+    square_product(K)
+    square_core(O)
     fc1_core(3)
+    square_product(Q)
     fc1_z(0)
-
-    dbr_own = s.dbr[own, :].astype(F32)
-    s.vec2[0, 0:1, :] = col_sum(dbr_own)
-    s.vec2[0, 1:2, :] = col_sum(s.d_resid[own, :] * s.branch[own, :])
-    s.vec2[0, 2:3, :] = jnp.zeros((1, width), F32)
-    s.vec2[0, 3:4, :] = jnp.zeros((1, width), F32)
-    s.vec2[0, 2:3, mine] = col_sum(s.dq[...].astype(F32))
-    s.vec2[0, 3:4, mine] = col_sum(s.dv[...].astype(F32))
-    hat_low = s.hat[2 * rows:, :]
-    s.vec2[0, 4:5, :] = col_sum(dhq * hat_low)
-    s.vec2[0, 5:6, :] = col_sum(dhq)
-    s.vec2[0, 6:7, :] = col_sum(dhk * s.hat[...])
-    s.vec2[0, 7:8, :] = col_sum(dhk)
-    vector_send(0, 0, PC)
-    vector_send(1, 0, PC)
-
-    fc2_product(0)
+    square_core_rest(V)
+    square_core_rest(O)
     fc1_z(1)
-    fc2_product(1)
-    fc2_core(0)
-    fc2_core(1)
-    got_dx = push(s.dx_s, s.dx_r, PX)
-    vector_add(0, 0)
-    vector_send(0, 1, PX)
-    vector_add(1, 0)
-    vector_send(1, 1, PX)
     fc1_z(2)
-    square_y(1)
+    fc2_product()
+    square_y(V)
+    square_core(K)
+    square_y(O)
+    fc2_core()
+    square_core(Q)
+    square_core_rest(K)
+    vector(1, 1)
     fc1_z(3)
+    square_z(V)
+    square_z(O)
+    vector(1, 2)
+    square_y(K)
     fc2_swap()
-
-    got_mlp()
-    mlp_own = s.mlp[own, :] + s.mlp_r[...].astype(F32) + b_fc2
-    out_block[0] = (s.resid[own, :] + scale_m * mlp_own).astype(BF16)
-
-    vector_add(0, 1)
-    vector_send(0, 2, PY)
-    vector_add(1, 1)
-    vector_send(1, 2, PY)
-    square_y(2)
-    square_z(1)
-    fc2_z()
-    square_y(3)
-    square_z(2)
-    square_y(0)
-    vector_add(0, 2)
-    vector_send(0, 3, PZ1)
-    vector_add(1, 2)
-    vector_send(1, 3, PZ1)
-    square_z(3)
-
-    got_dx()
-    dx_l = s.dx[0, own, :] + s.dx_r[0].astype(F32)
-    dx_q = s.dx[1, own, :] + s.dx_r[1].astype(F32)
-    out_dl[0] = normalise_back(dx_l, hat_l, inv_l)
-    out_dq[0] = s.d_resid[own, :] + normalise_back(dx_q, hat_q, inv_q)
-
-    for b in range(nb):
-        fc1_end(b)
-    square_z(0)
-    vector_add(0, 3)
-    vector_send(0, 4, PZ2)
-    vector_add(1, 3)
-    vector_send(1, 4, PZ2)
+    square_core_rest(Q)
+    norms_send()
+    vector(0, 2)
+    vector(1, 3)
+    fc1_end(3)
+    square_y(Q)
+    vector(0, 3)
+    fc1_end(2)
+    square_z(K)
+    norms_end()
+    vector(1, 4)
+    square_z(Q)
+    vector(1, 5)
+    square_end(V)
+    fc1_end(1)
+    square_end(K)
     fc2_end()
-    square_end(1)
-    square_end(2)
-    square_end(3)
-    square_end(0)
-    for g in range(2):
-        vector_add(g, 4)
-        out_vec[g * 8:g * 8 + 8, :] = tables[g][5]
+    square_end(O)
+    fc1_end(0)
+    vector(0, 4)
+    vector(0, 5)
+    square_end(Q)
     for copy in sent:
         copy.wait_send()
 
@@ -568,8 +644,13 @@
     scratch = dict(
         send=pltpu.SemaphoreType.DMA((96,)),
         recv=pltpu.SemaphoreType.DMA((96,)),
-        load=pltpu.SemaphoreType.DMA((16,)),
-        dy=vm((2 * rows, width), BF16),
+        load=pltpu.SemaphoreType.DMA((32,)),
+        ready=pltpu.SemaphoreType.REGULAR,
+        rows=vm((12, width), F32),
+        b_fc1=vm((ff,), F32),
+        ok=vm((2, 1, 2 * rows), jnp.int32),
+        pos=vm((1, rows), jnp.int32),
+        dy=vm((4, 2 * rows, width), BF16),
         qraw=vm((2 * rows, width), BF16),
         lraw=vm((2 * rows, width), BF16),
         ppos=vm((1, rows), jnp.int32),
@@ -600,12 +681,12 @@
         mlp_s=vm((rows, width), BF16),
         mlp_r=vm((rows, width), BF16),
         d_act=vm((nb, 2 * rows, half), F32),
-        dm=vm((2, 2 * rows, width), BF16),
+        dm=vm((4, 2 * rows, width), BF16),
         h2_g=vm((2, 2, 4 * blk, 2 * rows), BF16),
         h2_r=vm((2, 4 * blk, 2 * rows), BF16),
         act=vm((nb, 2 * rows, half), BF16),
-        act_g=vm((2, 2, 2, fblk, 2 * rows), BF16),
-        act_r=vm((2, 2, fblk, 2 * rows), BF16),
+        act_s=vm((4, 2, fblk, 2 * rows), BF16),
+        act_r=vm((3, 2, fblk, 2 * rows), BF16),
         dp=vm((2, nb, 2 * rows, half), BF16),
         dh2=vm((2, 2 * rows, width), BF16),
         dbr=vm((2 * rows, width), BF16),
@@ -619,20 +700,18 @@
         sq=vm((4, 8 * blk, half), F32),
         sq_cs=vm((4, 8 * blk, half), BF16),
         sq_cr=vm((4, 8 * blk, half), BF16),
-        sq_ys=vm((4, 4 * blk, half), BF16),
-        sq_yr=vm((4, 4 * blk, half), BF16),
+        sq_ys=vm((4, 2, 2 * blk, half), BF16),
+        sq_yr=vm((4, 2, 2 * blk, half), BF16),
         sq_zs=vm((4, 2 * blk, half), BF16),
         sq_zr=vm((4, 2 * blk, half), BF16),
         sq_ws=vm((4, blk, half), BF16),
         sq_wr=vm((4, blk, half), BF16),
-        fc2=vm((2, fblk, width), F32),
-        fc2_cs=vm((2, fblk, width), BF16),
-        fc2_cr=vm((2, fblk, width), BF16),
-        fc2_xs=vm((2, fblk, half), BF16),
-        fc2_xr=vm((2, fblk, half), BF16),
-        fc2_all=vm((4, fblk, half), F32),
-        fc2_zs=vm((2, fblk, half), BF16),
-        fc2_zr=vm((2, fblk, half), BF16),
+        fc2=vm((fblk, width), F32),
+        fc2_cs=vm((fblk, width), BF16),
+        fc2_cr=vm((fblk, width), BF16),
+        fc2_xs=vm((fblk, half), BF16),
+        fc2_xr=vm((fblk, half), BF16),
+        fc2_all=vm((2, fblk, half), F32),
         fc2_ws=vm((fblk, half), BF16),
         fc2_wr=vm((fblk, half), BF16),
         fc1=vm((nb, 4 * blk, half), F32),
@@ -653,18 +732,18 @@
     return pl.pallas_call(
         functools.partial(kernel, (rows, width, ff, share)),
         out_shape=(
-            sds((1, rows, width), BF16),
-            sds((1, rows, width), F32),
-            sds((1, rows, width), F32),
-            sds((blk, half), F32),
-            sds((blk, half), F32),
-            sds((blk, half), F32),
-            sds((blk, half), F32),
-            sds((blk, ff // 2), F32),
-            sds((fblk, half), F32),
-            sds((16, width), F32),
+            vm((1, rows, width), BF16),
+            vm((1, rows, width), F32),
+            vm((1, rows, width), F32),
+            vm((blk, half), F32),
+            vm((blk, half), F32),
+            vm((blk, half), F32),
+            vm((blk, half), F32),
+            vm((blk, ff // 2), F32),
+            vm((fblk, half), F32),
+            vm((16, width), F32),
         ),
-        in_specs=[ANY, ANY, VMEM, VMEM, VMEM, ANY] + [ANY] * 6 + [VMEM] * 13,
+        in_specs=[ANY] * 25,
         out_specs=[VMEM] * 10,
         scratch_shapes=[scratch],
         compiler_params=pltpu.CompilerParams(
@@ -695,7 +774,10 @@
         copy.wait()
 
 
-def finish(arrays, table, ff):
+def finish(arrays, table, ff, share):
+    if share == 1:
+        arrays = tuple(pltpu.with_memory_space_constraint(a, pltpu.VMEM) for a in arrays)
+        table = pltpu.with_memory_space_constraint(table, pltpu.VMEM)
     count, width = len(arrays), table.shape[1]
     sds = jax.ShapeDtypeStruct
     vectors = table.shape[0] - ff // width
@@ -740,7 +822,7 @@
         )
         vec = lax.psum(vec, "dp", axis_index_groups=groups)
     arrays = (block_out, d_queries, d_latents, wq, wk, wv, wo, w1, w2)
-    done = finish(arrays, vec, w_fc1.shape[1])
+    done = finish(arrays, vec, w_fc1.shape[1], share)
     block_out, d_queries, d_latents, wq, wk, wv, wo, w1, w2, b1 = done[:10]
     b2, sm, gm, hm, bo, sa, bq, bv, gq, hq, gk, hk = done[10:]
     return (

time: 74.6 us -> 63.9 us (0.86)
  Pallas kernels: 73.7 us -> 63 us
    pallas_call x1, Pallas kernels: 70.5 us -> 61.2 us  [fused(): pl.pallas_call(functools.partial(kernel, (rows, width, ff, share)), out_s...]
    pallas_call x1, Pallas kernels: 3.2 us -> 1.83 us  [finish(): pl.pallas_call(functools.partial(finish_kernel, count), out_shape=tuple((...]
where the time goes in v3:
time: 63.9 us; the launch traced here: 63.7 us
  Pallas kernels  63 us (99%)
  between operations  0.68 us (1%)
    pallas_call x1, Pallas kernels, fused(): pl.pallas_call(functools.partial(kernel, (rows, width, ff, share)), out_s...  61.2 us
    pallas_call x1, Pallas kernels, finish(): pl.pallas_call(functools.partial(finish_kernel, count), out_shape=tuple((...  1.83 us

profile of v3, /device:TPU:0, one launch (start us, length us, event | category | flops | bytes accessed | tf_op | source)
XLA Modules:
  0.0 63.7 jit_solution(1292074843690181756)
XLA Ops:
  0.7 61.2 %shard_map.408 = (bf16[1,64,768]{2,1,0:T(8,128)(2,1)S(1)}, f32[1,64,768]{2,1,0:T(8,128)S(1)}, f32[1,64,768]{2,1,0:T(8,128)S(1)}, f32[48,384]{1,0:T(8,128)S(1)}, ...) custom-call(bf16[1,64,768]{2,1,0:T(8,128)(2,1)} %queries.1, ...), custom_call_target="tpu_custom_call" | custom-call | flops 6000000000 | bytes 16000000 | tf_op jit(solution)/shard_map/pallas_call | solution.py:732
  61.9 1.8 %shard_map.409 = (bf16[1,64,768]{2,1,0:T(8,128)(2,1)}, f32[1,64,768]{2,1,0:T(8,128)}, f32[1,64,768]{2,1,0:T(8,128)}, f32[48,384]{1,0:T(8,128)}, f32[48,384]{1,0:...) custom-call(bf16[1,64,768]{2,1,0:T(8,128)(2,1)S(1)} %get-tuple-eleme, ...), custom_call_target="tpu_custom_call" | custom-call | tf_op jit(solution)/shard_map/pallas_call | solution.py:786

commit v4 on v3

--- a/solution.py
+++ b/solution.py
@@ -15,6 +15,8 @@
 BF16 = jnp.bfloat16
 GROUPS = 16
 Z_ORDER = (0, 2, 1, 3)
+Z2_FIRST = (0, 1)
+Z_FIRST = (3, 0)
 
 
 def dot(a, b):
@@ -77,7 +79,7 @@
     s = types.SimpleNamespace(**s)
     rows, width, ff, share = shape
     half = width // 2
-    heads = half // HEAD_DIM
+    pairs = half // (2 * HEAD_DIM)
     blk = width // GROUPS
     fblk = ff // GROUPS
     hid = ff // 2
@@ -101,7 +103,6 @@
     PC = dev(z, y, 1 - c, x)
     PZ1 = dev(zs[1], y, c, x)
     PZ2 = dev(zs[2], y, c, x)
-    PYZ1 = dev(zs[1], 1 - y, c, x)
     z_low = z % 2
     z_high = z // 2
 
@@ -157,7 +158,6 @@
     low_other = pl.ds(pl.multiple_of((3 - x) * rows, rows), rows)
     mine = pl.ds(pl.multiple_of(x * half, half), half)
     theirs = pl.ds(pl.multiple_of((1 - x) * half, half), half)
-    units = pl.ds(pl.multiple_of(x * hid, hid), hid)
 
     def row_of(ref, i):
         wait = load(ref, s.rows.at[i])
@@ -174,9 +174,9 @@
     gain_q, shift_q, gain_k, shift_k = (
         row_of(ref, i) for i, ref in enumerate((gain_q, shift_q, gain_k, shift_k))
     )
-    load_wk = load(w_key.at[:, mine], s.wk)
-    load_wv = load(w_value.at[:, mine], s.wv)
-    load_wq = load(w_query.at[:, mine], s.wq)
+    load_wk = load(w_key, s.wk)
+    load_wv = load(w_value, s.wv)
+    load_wq = load(w_query, s.wq)
     b_query, b_value, b_out, b_fc2, gain_m, shift_m, scale_a, scale_m = (
         row_of(ref, 4 + i)
         for i, ref in enumerate((b_query, b_value, b_out, b_fc2, gain_m, shift_m, scale_a, scale_m))
@@ -184,9 +184,9 @@
     load_b1 = load(b_fc1, s.b_fc1)
     load_ok = [load(vis_ok, s.ok.at[0]), load(msk_ok, s.ok.at[1])]
     load_dy = load(dy_in.at[0], s.dy.at[0, own])
-    load_w2 = load(w_fc2.at[units], s.w2)
+    load_w2 = load(w_fc2, s.w2)
     load_wo = load(w_out, s.wo)
-    load_w1 = load(w_fc1.at[:, units], s.w1)
+    load_w1 = load(w_fc1, s.w1)
 
     eye = lax.broadcasted_iota(jnp.int32, (rows, rows), 0) == lax.broadcasted_iota(
         jnp.int32, (rows, rows), 1
@@ -219,10 +219,10 @@
         k = dot(both, s.wk[...]).astype(BF16)
         s.k[at, :] = k[:rows]
         s.k[low_at, :] = k[rows:]
-        v = (dot(both, s.wv[...]) + my_b_value).astype(BF16)
+        v = (dot(both, s.wv[...]) + b_value).astype(BF16)
         s.v[at, :] = v[:rows]
         s.v[low_at, :] = v[rows:]
-        s.q[at, :] = (dot(hq, s.wq[...]) + my_b_query).astype(BF16)
+        s.q[at, :] = (dot(hq, s.wq[...]) + b_query).astype(BF16)
 
     load_q()
     load_p()
@@ -235,8 +235,7 @@
     got_q = push(queries.at[0], s.qraw.at[own], PX, s.qraw.at[other])
     got_l = push(latents.at[0], s.lraw.at[own], PX, s.lraw.at[other])
     got_dy = push(dy_in.at[0], s.dy.at[0, own], PX, s.dy.at[0, other])
-    got_dy_y = push(dy_in.at[0], s.dy.at[1, own], PY)
-    got_dy_z = push(dy_in.at[0], s.dy.at[2, own], PZ1)
+    got_dy_z = push(dy_in.at[0], s.dy.at[1, own], PZ1)
     tell_z(s.ready)
 
     load_wk()
@@ -246,16 +245,24 @@
         value() for value in (b_query, b_value, b_out, b_fc2, gain_m, shift_m, scale_a, scale_m)
     )
     load_b1()
-    my_b_value = jnp.where(x == 0, b_value[:, :half], b_value[:, half:])
-    my_b_query = jnp.where(x == 0, b_query[:, :half], b_query[:, half:])
     b_fc1 = s.b_fc1[...].reshape(1, ff)
-    my_b_fc1 = jnp.where(x == 0, b_fc1[:, :hid], b_fc1[:, hid:])
+    halves_b_fc1 = [
+        jnp.where(x == k, b_fc1[:, :hid], b_fc1[:, hid:]) for k in range(2)
+    ]
     project(hq, hkq, hkl, own, low_own)
+
+    def act_back(at):
+        d_mlp = (scale_m * s.dy[0, at, :].astype(F32)).astype(BF16)
+        s.dm[0, at, :] = d_mlp
+        for b in range(2 * nb):
+            s.d_act[b, at, :] = dot_t(d_mlp, s.w2[b * half:(b + 1) * half, :])
+
+    load_dy()
+    load_w2()
+    act_back(own)
     got_p()
     got_q()
     _, _, hq_o, hkq_o = qry_half(s.ppos, other, low_other)
-    pl.semaphore_wait(s.ready, z_links)
-    got_dy_yz = push(dy_in.at[0], s.dy.at[3, own], PYZ1)
     got_l()
     _, _, hkl_o = lat_half(other)
     project(hq_o, hkq_o, hkl_o, other, low_other)
@@ -273,37 +280,20 @@
     def unstack(both):
         return jnp.where(first, both[:2 * rows], both[2 * rows:])
 
-    def lanes(pair):
-        return slice(pair * 2 * HEAD_DIM, (pair + 1) * 2 * HEAD_DIM)
-
-    for pair in range(heads // 2):
-        raw = dot_t(stack(s.q[:, lanes(pair)]), s.k[:, lanes(pair)]) * scale
+    for pair in range(2 * pairs):
+        at = slice(pair * 2 * HEAD_DIM, (pair + 1) * 2 * HEAD_DIM)
+        raw = dot_t(stack(s.q[:, at]), s.k[:, at]) * scale
         scores = jnp.where(ok, raw, -1e30)
         peak = jnp.max(scores, axis=-1, keepdims=True)
         weight = jnp.exp(scores - peak)
         prob = weight * (1.0 / jnp.sum(weight, axis=-1, keepdims=True))
         s.prob[pair] = prob
-        s.att[x, :, lanes(pair)] = unstack(dot(prob.astype(BF16), s.v[:, lanes(pair)])).astype(BF16)
-    got_att = push(s.att.at[x], s.att.at[x], PX, s.att.at[1 - x])
+        s.att[:, at] = unstack(dot(prob.astype(BF16), s.v[:, at])).astype(BF16)
 
     got_dy()
-    got_dy_y2 = push(s.dy.at[0, other], s.dy.at[1, other], PY)
-    got_dy_z2 = push(s.dy.at[0, other], s.dy.at[2, other], PZ1)
-    got_dy_yz2 = push(s.dy.at[0, other], s.dy.at[3, other], PYZ1)
-    s.hq_t[...] = s.hq[...].T
-    s.hk_t[...] = s.hk[...].T
-    load_dy()
-    load_w2()
-    dy = s.dy[0].astype(F32)
-    d_mlp = (scale_m * dy).astype(BF16)
-    s.dm[0] = d_mlp
-    for b in range(nb):
-        s.d_act[b] = dot_t(d_mlp, s.w2[b * half:(b + 1) * half, :])
+    got_dy_z2 = push(s.dy.at[0, other], s.dy.at[1, other], PZ1)
     load_wo()
-    s.branch[...] = dot(s.att[x], s.wo[mine, :]) + b_out
-    got_att()
-
-    branch = s.branch[...] + dot(s.att[1 - x], s.wo[theirs, :])
+    branch = dot(s.att[...], s.wo[...]) + b_out
     resid = s.qin[...] + scale_a * branch
     hat_m, inv_m = normalise(resid)
     h_two = (hat_m * gain_m + shift_m).astype(BF16)
@@ -321,55 +311,31 @@
     s.h2_g[1, 0] = blocks(s.h2_t, c, 1 - y)
     s.h2_g[1, 1] = blocks(s.h2_t, 1 - c, 1 - y)
     got_h2 = push(s.h2_g.at[1], s.h2_r, PY)
+    act_back(other)
     load_w1()
-    d_h2 = jnp.zeros((2 * rows, width), F32)
+
+    def hidden(first_block, b, bias):
+        at = pl.ds(pl.multiple_of((first_block + b) * half, half), half)
+        pre = dot(h_two, s.w1[:, at]) + bias[:, b * half:(b + 1) * half]
+        cdf = 0.5 * (1.0 + lax.erf(pre * math.sqrt(0.5)))
+        slope = cdf + pre * (jnp.exp(-0.5 * pre * pre) * (1.0 / math.sqrt(2 * math.pi)))
+        s.act[first_block + b] = (pre * cdf).astype(BF16)
+        s.dp[first_block + b] = (s.d_act[first_block + b] * slope).astype(BF16)
+
     got_dp = []
     for b in range(nb):
-        cols = slice(b * half, (b + 1) * half)
-        pre = dot(h_two, s.w1[:, cols]) + my_b_fc1[:, cols]
-        cdf = 0.5 * (1.0 + lax.erf(pre * math.sqrt(0.5)))
-        act = (pre * cdf).astype(BF16)
-        slope = cdf + pre * (jnp.exp(-0.5 * pre * pre) * (1.0 / math.sqrt(2 * math.pi)))
-        d_pre = (s.d_act[b] * slope).astype(BF16)
-        s.act[b] = act
-        s.dp[0, b] = d_pre
-        got_dp.append(push(s.dp.at[0, b], s.dp.at[1, b], PY))
-        d_h2 += dot_t(d_pre, s.w1[:, cols])
-    s.dh2[0] = d_h2.astype(BF16)
-    got_dh2 = push(s.dh2.at[0], s.dh2.at[1], PX)
+        hidden(x * nb, b, halves_b_fc1[0])
+        got_dp.append(push(s.dp.at[x * nb + b], s.dp_r.at[b], PY))
 
     for b in range(nb):
-        s.act_t[b * half:(b + 1) * half, :] = s.act[b].T
-    got_act = []
-    for i, (zz, yy) in enumerate(
-        ((z_low, y), (z_low, 1 - y), (1 - z_low, y), (1 - z_low, 1 - y))
-    ):
-        for j, cc in enumerate((c, 1 - c)):
-            at = pl.ds(pl.multiple_of((zz * 4 + yy * 2 + cc) * fblk, fblk), fblk)
-            s.act_s[i, j] = s.act_t[at, :]
-        if i:
-            got_act.append(push(s.act_s.at[i], s.act_r.at[i - 1], (PY, PZ1, PYZ1)[i - 1]))
-
-    s.branch[...] = branch
-    s.resid[...] = resid
+        zz, at = divmod(b * half, hid // 2)
+        s.act_t[zz, at:at + half, :] = s.act[x * nb + b].T
+    got_act = push(s.act_t.at[1 - z_low], s.act_r, PZ1)
     s.h2_g[0, 0] = blocks(s.h2_t, c, y)
     s.h2_g[0, 1] = blocks(s.h2_t, 1 - c, y)
-    mlp = jnp.zeros((2 * rows, width), F32)
-    s.vec[0, 0:4, :] = jnp.zeros((4, width), F32)
-    for b in range(nb):
-        cols = slice(b * half, (b + 1) * half)
-        mlp += dot(s.act[b], s.w2[cols, :])
-        s.vec[0, pl.ds(2 * x + b // 2, 1), (b % 2) * half:(b % 2 + 1) * half] = col_sum(
-            s.dp[0, b].astype(F32)
-        )
-    s.mlp[...] = mlp
-    s.mlp_s[...] = s.mlp[other, :].astype(BF16)
-    got_mlp = push(s.mlp_s, s.mlp_r, PX)
-    dy_own = s.dy[0, own, :].astype(F32)
-    s.vec[0, 4:5, :] = col_sum(s.dm[0, own, :].astype(F32))
-    s.vec[0, 5:6, :] = col_sum(dy * mlp) + b_fc2 * col_sum(dy_own)
-    s.vec[0, 6:7, :] = col_sum(d_h2 * hat_m)
-    s.vec[0, 7:8, :] = col_sum(d_h2)
+    s.hq_t[...] = s.hq[...].T
+    s.hk_t[...] = s.hk[...].T
+    s.att_t[...] = s.att[...].T
 
     got_c1, got_z1, got_w1 = [None] * nb, [None] * nb, [None] * nb
 
@@ -377,22 +343,29 @@
         if b == 0:
             got_h2()
         got_dp[b]()
-        right = s.dp[:, b].reshape(4 * rows, half)
+        right = jnp.concatenate([s.dp[x * nb + b], s.dp_r[b]], axis=0)
         left = jnp.concatenate([s.h2_g[0], s.h2_r[...]], axis=-1)
         s.fc1_cs[b] = dot(left[1], right).astype(BF16)
         got_c1[b] = push(s.fc1_cs.at[b], s.fc1_cr.at[b], PC)
         s.fc1[b] = dot(left[0], right)
 
+    def fc1_rows(b):
+        kept, leaving = ((0, 2), (1, 3)) if b in Z2_FIRST else ((0, 1), (2, 3))
+        return [[slice(k * blk, (k + 1) * blk) for k in side] for side in (kept, leaving)]
+
     def fc1_core(b):
         got_c1[b]()
         s.fc1[b] = s.fc1[b] + s.fc1_cr[b].astype(F32)
-        s.fc1_zs[b] = s.fc1[b, 2 * blk:, :].astype(BF16)
-        got_z1[b] = push(s.fc1_zs.at[b], s.fc1_zr.at[b], PZ1)
+        for k, at in enumerate(fc1_rows(b)[1]):
+            s.fc1_zs[b, k * blk:(k + 1) * blk, :] = s.fc1[b, at, :].astype(BF16)
+        got_z1[b] = push(s.fc1_zs.at[b], s.fc1_zr.at[b], PZ2 if b in Z2_FIRST else PZ1)
 
     def fc1_z(b):
         got_z1[b]()
-        s.fc1_ws[b] = (s.fc1[b, blk:2 * blk, :] + s.fc1_zr[b, blk:, :].astype(F32)).astype(BF16)
-        got_w1[b] = push(s.fc1_ws.at[b], s.fc1_wr.at[b], PZ2)
+        s.fc1_ws[b] = (
+            s.fc1[b, fc1_rows(b)[0][1], :] + s.fc1_zr[b, blk:, :].astype(F32)
+        ).astype(BF16)
+        got_w1[b] = push(s.fc1_ws.at[b], s.fc1_wr.at[b], PZ1 if b in Z2_FIRST else PZ2)
 
     def fc1_end(b):
         got_w1[b]()
@@ -400,39 +373,61 @@
             s.fc1[b, :blk, :] + s.fc1_zr[b, :blk, :].astype(F32) + s.fc1_wr[b].astype(F32)
         )
 
-    got_c2, got_x2, got_w2 = [None], [None], [None]
-
-    def fc2_product():
-        for got in [got_dy_y, got_dy_z, got_dy_yz, got_dy_y2, got_dy_z2, got_dy_yz2] + got_act:
-            got()
-        for g in range(1, 4):
-            s.dm[g] = (scale_m * s.dy[g].astype(F32)).astype(BF16)
-        right = s.dm[...].reshape(8 * rows, width)
-        for j in (1, 0):
-            left = jnp.concatenate([s.act_s[0, j]] + [s.act_r[g, j] for g in range(3)], axis=-1)
-            total = dot(left, right)
-            if j:
-                s.fc2_cs[...] = total.astype(BF16)
-                got_c2[0] = push(s.fc2_cs, s.fc2_cr, PC)
-            else:
-                s.fc2[...] = total
-
-    def fc2_core():
-        got_c2[0]()
-        s.fc2[...] = s.fc2[...] + s.fc2_cr[...].astype(F32)
-        s.fc2_xs[...] = s.fc2[:, theirs].astype(BF16)
-        got_x2[0] = push(s.fc2_xs, s.fc2_xr, PX)
-        s.fc2_all[x] = s.fc2[:, mine]
-
-    def fc2_swap():
-        got_x2[0]()
-        s.fc2_all[1 - x] = s.fc2_xr[...].astype(F32)
-        s.fc2_ws[...] = s.fc2_all[1 - z_high].astype(BF16)
-        got_w2[0] = push(s.fc2_ws, s.fc2_wr, PZ2)
-
-    def fc2_end():
-        got_w2[0]()
-        out_w2[...] = s.fc2_all[z_high] + s.fc2_wr[...].astype(F32)
+    live = types.SimpleNamespace()
+    hb = fblk // 2
+    got_c2, got_x2, got_y2, got_w2 = ([None] * 2 for _ in range(4))
+
+    def fc2_side(cc, k):
+        left = jnp.concatenate(
+            [
+                jnp.concatenate([s.act_t[z_low, at, :], s.act_r[at, :]], axis=-1)
+                for at in (
+                    pl.ds(pl.multiple_of((yy * 2 + cc) * fblk + k * hb, hb), hb)
+                    for yy in (y, 1 - y)
+                )
+            ],
+            axis=0,
+        )
+        return dot(left, s.dm[...].reshape(4 * rows, width))
+
+    def fc2_product(k):
+        if got_c2 == [None, None]:
+            for got in (got_dy_z, got_dy_z2, got_act):
+                got()
+            s.dm[1] = (scale_m * s.dy[1].astype(F32)).astype(BF16)
+        s.fc2_cs[k] = fc2_side(1 - c, k).astype(BF16)
+        got_c2[k] = push(s.fc2_cs.at[k], s.fc2_cr.at[k], PC)
+
+    def fc2_rest(k):
+        s.fc2[k] = fc2_side(c, k)
+
+    def fc2_core(k):
+        got_c2[k]()
+        s.fc2[k] = s.fc2[k] + s.fc2_cr[k].astype(F32)
+        s.fc2_xs[k] = s.fc2[k, :, theirs].astype(BF16)
+        got_x2[k] = push(s.fc2_xs.at[k], s.fc2_xr.at[k], PX)
+        s.fc2_all[k, x] = s.fc2[k, :, mine]
+
+    def fc2_swap(k):
+        got_x2[k]()
+        s.fc2_all[k, 1 - x] = s.fc2_xr[k].astype(F32)
+        s.fc2_ys[k] = s.fc2_all[k, :, hb:, :].astype(BF16)
+        got_y2[k] = push(s.fc2_ys.at[k], s.fc2_yr.at[k], PY)
+
+    def fc2_y(k):
+        got_y2[k]()
+        s.fc2_ws[k] = (
+            s.fc2_all[k, 1 - z_high, :hb, :] + s.fc2_yr[k, 1 - z_high].astype(F32)
+        ).astype(BF16)
+        got_w2[k] = push(s.fc2_ws.at[k], s.fc2_wr.at[k], PZ2)
+
+    def fc2_end(k):
+        got_w2[k]()
+        out_w2[k * hb:(k + 1) * hb, :] = (
+            s.fc2_all[k, z_high, :hb, :]
+            + s.fc2_yr[k, z_high].astype(F32)
+            + s.fc2_wr[k].astype(F32)
+        )
 
     yrows, zrows = 4 * blk, 2 * blk
     got_c, got_y, got_yr, got_zsq, got_wsq = ([None] * 4 for _ in range(5))
@@ -451,23 +446,36 @@
     def square_core(i):
         got_c[i]()
         s.sq[i] = s.sq[i] + s.sq_cr[i].astype(F32)
-        s.sq_ys[i, 1] = s.sq[i, yrows + zrows:, :].astype(BF16)
-        got_y[i] = push(s.sq_ys.at[i, 1], s.sq_yr.at[i, 1], PY)
+        if i in Z_FIRST:
+            for k in range(2):
+                s.sq_zs[i, k] = s.sq[i, k * yrows + zrows:(k + 1) * yrows, :].astype(BF16)
+            got_zsq[i] = push(s.sq_zs.at[i], s.sq_zr.at[i], PZ1)
+        else:
+            s.sq_ys[i, 1] = s.sq[i, yrows + zrows:, :].astype(BF16)
+            got_y[i] = push(s.sq_ys.at[i, 1], s.sq_yr.at[i, 1], PY)
 
     def square_core_rest(i):
         s.sq_ys[i, 0] = s.sq[i, yrows:yrows + zrows, :].astype(BF16)
         got_yr[i] = push(s.sq_ys.at[i, 0], s.sq_yr.at[i, 0], PY)
 
     def square_y(i):
-        got_y[i]()
-        s.sq_zs[i] = (s.sq[i, zrows:yrows, :] + s.sq_yr[i, 1].astype(F32)).astype(BF16)
-        got_zsq[i] = push(s.sq_zs.at[i], s.sq_zr.at[i], PZ1)
+        if i in Z_FIRST:
+            got_zsq[i]()
+            s.sq_ys[i, 0] = (
+                s.sq[i, yrows:yrows + zrows, :] + s.sq_zr[i, 1].astype(F32)
+            ).astype(BF16)
+            got_yr[i] = push(s.sq_ys.at[i, 0], s.sq_yr.at[i, 0], PY)
+        else:
+            got_y[i]()
+            s.sq_zs[i, 0] = (s.sq[i, zrows:yrows, :] + s.sq_yr[i, 1].astype(F32)).astype(BF16)
+            got_zsq[i] = push(s.sq_zs.at[i, 0], s.sq_zr.at[i, 0], PZ1)
 
     def square_z(i):
         got_yr[i]()
-        got_zsq[i]()
+        if i not in Z_FIRST:
+            got_zsq[i]()
         s.sq[i, :zrows, :] = (
-            s.sq[i, :zrows, :] + s.sq_yr[i, 0].astype(F32) + s.sq_zr[i].astype(F32)
+            s.sq[i, :zrows, :] + s.sq_yr[i, 0].astype(F32) + s.sq_zr[i, 0].astype(F32)
         )
         s.sq_ws[i] = s.sq[i, blk:zrows, :].astype(BF16)
         got_wsq[i] = push(s.sq_ws.at[i], s.sq_wr.at[i], PZ2)
@@ -489,144 +497,163 @@
         got_v[g]()
         tables[g][step + 1] = tables[g][step] + landings[g][step]
 
-    live = types.SimpleNamespace()
+    def hidden_others():
+        for b in range(nb):
+            hidden((1 - x) * nb, b, halves_b_fc1[1])
+        s.branch[...] = branch
+        s.resid[...] = resid
 
     def d_resid():
-        got_dh2()
-        d_h2 = s.dh2[0].astype(F32) + s.dh2[1].astype(F32)
-        d_resid = dy + normalise_back(d_h2 * gain_m, hat_m, inv_m)
+        d_h2 = jnp.zeros((width, 2 * rows), F32)
+        for b in range(2 * nb):
+            d_h2 += dot(s.w1[:, b * half:(b + 1) * half], s.dp[b].T)
+        d_h2 = d_h2.T
+        s.vec[0, 6:7, :] = col_sum(d_h2 * hat_m)
+        s.vec[0, 7:8, :] = col_sum(d_h2)
+        d_resid = s.dy[0].astype(F32) + normalise_back(d_h2 * gain_m, hat_m, inv_m)
         s.d_resid[...] = d_resid
-        d_branch = (scale_a * d_resid).astype(BF16)
-        s.dbr[...] = d_branch
-        s.da[...] = dot_t(d_branch, s.wo[mine, :]).astype(BF16)
-
-    def attention_back():
-        for pair in range(heads // 2):
-            q2 = stack(s.q[:, lanes(pair)])
-            da2 = stack(s.da[:, lanes(pair)])
+        s.dbr[...] = (scale_a * d_resid).astype(BF16)
+
+    def mlp_sums():
+        mlp = jnp.zeros((2 * rows, width), F32) + b_fc2
+        for b in range(2 * nb):
+            mlp += dot(s.act[b], s.w2[b * half:(b + 1) * half, :])
+            s.vec[0, b // 2:b // 2 + 1, (b % 2) * half:(b % 2 + 1) * half] = col_sum(
+                s.dp[b].astype(F32)
+            )
+        s.mlp[...] = mlp
+        s.vec[0, 4:5, :] = col_sum(s.dm[0].astype(F32))
+        s.vec[0, 5:6, :] = col_sum(s.dy[0].astype(F32) * mlp)
+
+    def block_end():
+        out_block[0] = (s.resid[own, :] + scale_m * s.mlp[own, :]).astype(BF16)
+
+    def heads_back(xx, cols):
+        s.da[:, cols] = dot(s.wo[cols, :], s.dbr[...].T).T.astype(BF16)
+        for p in range(pairs):
+            pair = xx * pairs + p
+            at = pl.ds(pl.multiple_of(pair * 2 * HEAD_DIM, 2 * HEAD_DIM), 2 * HEAD_DIM)
+            q2 = stack(s.q[:, at])
+            da2 = stack(s.da[:, at])
             prob = s.prob[pair]
-            s.dv[:, lanes(pair)] = dot(prob.astype(BF16).T, da2).astype(BF16)
-            d_prob = dot_t(da2, s.v[:, lanes(pair)])
+            s.dv[:, at] = dot(prob.astype(BF16).T, da2).astype(BF16)
+            d_prob = dot_t(da2, s.v[:, at])
             delta = jnp.sum(d_prob * prob, axis=-1, keepdims=True)
             ds = (prob * (d_prob - delta)).astype(BF16)
-            s.dq[:, lanes(pair)] = (unstack(dot(ds, s.k[:, lanes(pair)])) * scale).astype(BF16)
-            s.dk[:, lanes(pair)] = (dot(ds.T, q2) * scale).astype(BF16)
+            s.dq[:, at] = (unstack(dot(ds, s.k[:, at])) * scale).astype(BF16)
+            s.dk[:, at] = (dot(ds.T, q2) * scale).astype(BF16)
+
+    def attention_back():
+        heads_back(x, mine)
+
+    def attention_back_others():
+        heads_back(1 - x, theirs)
 
     def square_product(i):
-        if i == 0:
-            s.att_t[mine, :] = s.att[x].T
-            s.att_t[theirs, :] = s.att[1 - x].T
-            square(0, s.att_t, s.dbr[:, mine])
-        elif i < 3:
-            square(i, s.hk_t, (s.dv, s.dk)[i - 1][...])
-        else:
-            square(3, s.hq_t, s.dq[...])
+        square(
+            i,
+            (s.att_t, s.hk_t, s.hk_t, s.hq_t)[i],
+            (s.dbr, s.dv, s.dk, s.dq)[i][:, mine],
+        )
 
     def norms_back():
         dhk = dot_t(s.dk[...], s.wk[...]) + dot_t(s.dv[...], s.wv[...])
         dhq = dot_t(s.dq[...], s.wq[...])
         s.dx[0] = dhk[:2 * rows] * gain_k
         s.dx[1] = dhk[2 * rows:] * gain_k + dhq * gain_q
-        s.dx_s[...] = s.dx[:, other, :].astype(BF16)
-        s.vec2[0, 0:1, :] = col_sum(s.dbr[own, :].astype(F32))
-        s.vec2[0, 1:2, :] = col_sum(s.d_resid[own, :] * s.branch[own, :])
-        s.vec2[0, 2:3, :] = jnp.zeros((1, width), F32)
-        s.vec2[0, 3:4, :] = jnp.zeros((1, width), F32)
-        s.vec2[0, 2:3, mine] = col_sum(s.dq[...].astype(F32))
-        s.vec2[0, 3:4, mine] = col_sum(s.dv[...].astype(F32))
+        s.vec2[0, 0:1, :] = col_sum(s.dbr[...].astype(F32))
+        s.vec2[0, 1:2, :] = col_sum(s.d_resid[...] * s.branch[...])
+        s.vec2[0, 2:3, :] = col_sum(s.dq[...].astype(F32))
+        s.vec2[0, 3:4, :] = col_sum(s.dv[...].astype(F32))
         s.vec2[0, 4:5, :] = col_sum(dhq * s.hat[2 * rows:, :])
         s.vec2[0, 5:6, :] = col_sum(dhq)
         s.vec2[0, 6:7, :] = col_sum(dhk * s.hat[...])
         s.vec2[0, 7:8, :] = col_sum(dhk)
 
-    def norms_send():
-        live.got_dx = push(s.dx_s, s.dx_r, PX)
-
     def norms_end():
-        live.got_dx()
-        dx_l = s.dx[0, own, :] + s.dx_r[0].astype(F32)
-        dx_q = s.dx[1, own, :] + s.dx_r[1].astype(F32)
-        out_dl[0] = normalise_back(dx_l, hat_l, inv_l)
-        out_dq[0] = s.d_resid[own, :] + normalise_back(dx_q, hat_q, inv_q)
-
-    def block_end():
-        got_mlp()
-        mlp_own = s.mlp[own, :] + s.mlp_r[...].astype(F32) + b_fc2
-        out_block[0] = (s.resid[own, :] + scale_m * mlp_own).astype(BF16)
-
-    routes = (PZ2, PZ1, PY, PX, PC)
+        out_dl[0] = normalise_back(s.dx[0, own, :], hat_l, inv_l)
+        out_dq[0] = s.d_resid[own, :] + normalise_back(s.dx[1, own, :], hat_q, inv_q)
+
+    routes = (PZ2, PZ1, PY, PC)
 
     def vector(g, step):
         if step:
             vector_add(g, step - 1)
-        if step < 5:
+        if step < 4:
             vector_send(g, step, routes[step])
         else:
-            out_vec[g * 8:g * 8 + 8, :] = tables[g][5]
-
+            out_vec[g * 8:g * 8 + 8, :] = tables[g][4]
+
+    pl.semaphore_wait(s.ready, z_links)
     V, K, Q, O = 1, 2, 3, 0
+    hidden_others()
+    d_resid()
+    square_product(O)
+    attention_back()
+    fc1_product(0)
+    square_core(O)
+    square_product(V)
+    attention_back_others()
+    fc1_core(0)
+    fc1_product(1)
+    square_product(K)
+    fc2_product(1)
+    square_core(V)
+    fc1_core(1)
+    norms_back()
+    fc1_product(2)
+    square_core(K)
+    fc2_product(0)
+    fc2_rest(1)
+    fc2_core(1)
+    fc2_rest(0)
+    square_y(O)
+    fc1_core(2)
+    norms_end()
+    mlp_sums()
     vector(0, 0)
-    fc1_product(0)
-    d_resid()
-    fc1_core(0)
-    attention_back()
-    fc1_product(1)
-    norms_back()
+    square_core_rest(V)
+    square_y(V)
+    fc1_product(3)
+    square_core_rest(K)
+    fc2_core(0)
+    square_y(K)
+    vector(1, 0)
+    fc1_z(2)
+    fc2_swap(1)
+    square_product(Q)
+    square_z(O)
+    square_z(V)
     vector(0, 1)
-    fc1_product(2)
-    square_product(V)
-    fc1_core(1)
-    square_product(O)
-    fc1_core(2)
+    fc2_swap(0)
+    square_core(Q)
+    square_z(K)
+    fc1_core(3)
+    fc2_y(1)
+    vector(1, 1)
+    fc2_y(0)
+    square_y(Q)
+    fc1_z(3)
+    square_end(O)
+    square_z(Q)
+    fc1_z(1)
+    vector(0, 2)
+    vector(1, 2)
+    fc1_end(2)
+    fc1_z(0)
+    fc2_end(0)
     block_end()
-    square_core(V)
-    vector(1, 0)
-    fc1_product(3)
-    square_product(K)
-    square_core(O)
-    fc1_core(3)
-    square_product(Q)
-    fc1_z(0)
-    square_core_rest(V)
-    square_core_rest(O)
-    fc1_z(1)
-    fc1_z(2)
-    fc2_product()
-    square_y(V)
-    square_core(K)
-    square_y(O)
-    fc2_core()
-    square_core(Q)
-    square_core_rest(K)
-    vector(1, 1)
-    fc1_z(3)
-    square_z(V)
-    square_z(O)
-    vector(1, 2)
-    square_y(K)
-    fc2_swap()
-    square_core_rest(Q)
-    norms_send()
-    vector(0, 2)
+    square_end(K)
+    square_end(V)
+    vector(0, 3)
+    fc1_end(3)
     vector(1, 3)
-    fc1_end(3)
-    square_y(Q)
-    vector(0, 3)
-    fc1_end(2)
-    square_z(K)
-    norms_end()
+    fc2_end(1)
+    fc1_end(1)
+    vector(0, 4)
     vector(1, 4)
-    square_z(Q)
-    vector(1, 5)
-    square_end(V)
-    fc1_end(1)
-    square_end(K)
-    fc2_end()
-    square_end(O)
+    square_end(Q)
     fc1_end(0)
-    vector(0, 4)
-    vector(0, 5)
-    square_end(Q)
     for copy in sent:
         copy.wait_send()
 
@@ -650,16 +677,16 @@
         b_fc1=vm((ff,), F32),
         ok=vm((2, 1, 2 * rows), jnp.int32),
         pos=vm((1, rows), jnp.int32),
-        dy=vm((4, 2 * rows, width), BF16),
+        dy=vm((2, 2 * rows, width), BF16),
         qraw=vm((2 * rows, width), BF16),
         lraw=vm((2 * rows, width), BF16),
         ppos=vm((1, rows), jnp.int32),
-        w2=vm((hid, width), BF16),
-        w1=vm((width, hid), BF16),
+        w2=vm((ff, width), BF16),
+        w1=vm((width, ff), BF16),
         wo=vm((width, width), BF16),
-        wk=vm((width, half), BF16),
-        wv=vm((width, half), BF16),
-        wq=vm((width, half), BF16),
+        wk=vm((width, width), BF16),
+        wv=vm((width, width), BF16),
+        wq=vm((width, width), BF16),
         qin=vm((2 * rows, width), F32),
         hat=vm((4 * rows, width), F32),
         hq=vm((2 * rows, width), BF16),
@@ -668,52 +695,49 @@
         hk_t=vm((width, 4 * rows), BF16),
         att_t=vm((width, 2 * rows), BF16),
         h2_t=vm((width, 2 * rows), BF16),
-        act_t=vm((hid, 2 * rows), BF16),
-        q=vm((2 * rows, half), BF16),
-        k=vm((4 * rows, half), BF16),
-        v=vm((4 * rows, half), BF16),
-        prob=vm((pairs, 4 * rows, 4 * rows), F32),
-        att=vm((2, 2 * rows, half), BF16),
+        act_t=vm((2, hid // 2, 2 * rows), BF16),
+        q=vm((2 * rows, width), BF16),
+        k=vm((4 * rows, width), BF16),
+        v=vm((4 * rows, width), BF16),
+        prob=vm((2 * pairs, 4 * rows, 4 * rows), F32),
+        att=vm((2 * rows, width), BF16),
         branch=vm((2 * rows, width), F32),
         resid=vm((2 * rows, width), F32),
         d_resid=vm((2 * rows, width), F32),
         mlp=vm((2 * rows, width), F32),
-        mlp_s=vm((rows, width), BF16),
-        mlp_r=vm((rows, width), BF16),
-        d_act=vm((nb, 2 * rows, half), F32),
-        dm=vm((4, 2 * rows, width), BF16),
+        d_act=vm((2 * nb, 2 * rows, half), F32),
+        dm=vm((2, 2 * rows, width), BF16),
         h2_g=vm((2, 2, 4 * blk, 2 * rows), BF16),
         h2_r=vm((2, 4 * blk, 2 * rows), BF16),
-        act=vm((nb, 2 * rows, half), BF16),
-        act_s=vm((4, 2, fblk, 2 * rows), BF16),
-        act_r=vm((3, 2, fblk, 2 * rows), BF16),
-        dp=vm((2, nb, 2 * rows, half), BF16),
-        dh2=vm((2, 2 * rows, width), BF16),
+        act=vm((2 * nb, 2 * rows, half), BF16),
+        act_r=vm((hid // 2, 2 * rows), BF16),
+        dp=vm((2 * nb, 2 * rows, half), BF16),
+        dp_r=vm((nb, 2 * rows, half), BF16),
         dbr=vm((2 * rows, width), BF16),
-        da=vm((2 * rows, half), BF16),
-        dq=vm((2 * rows, half), BF16),
-        dk=vm((4 * rows, half), BF16),
-        dv=vm((4 * rows, half), BF16),
+        da=vm((2 * rows, width), BF16),
+        dq=vm((2 * rows, width), BF16),
+        dk=vm((4 * rows, width), BF16),
+        dv=vm((4 * rows, width), BF16),
         dx=vm((2, 2 * rows, width), F32),
-        dx_s=vm((2, rows, width), BF16),
-        dx_r=vm((2, rows, width), BF16),
         sq=vm((4, 8 * blk, half), F32),
         sq_cs=vm((4, 8 * blk, half), BF16),
         sq_cr=vm((4, 8 * blk, half), BF16),
         sq_ys=vm((4, 2, 2 * blk, half), BF16),
         sq_yr=vm((4, 2, 2 * blk, half), BF16),
-        sq_zs=vm((4, 2 * blk, half), BF16),
-        sq_zr=vm((4, 2 * blk, half), BF16),
+        sq_zs=vm((4, 2, 2 * blk, half), BF16),
+        sq_zr=vm((4, 2, 2 * blk, half), BF16),
         sq_ws=vm((4, blk, half), BF16),
         sq_wr=vm((4, blk, half), BF16),
-        fc2=vm((fblk, width), F32),
-        fc2_cs=vm((fblk, width), BF16),
-        fc2_cr=vm((fblk, width), BF16),
-        fc2_xs=vm((fblk, half), BF16),
-        fc2_xr=vm((fblk, half), BF16),
-        fc2_all=vm((2, fblk, half), F32),
-        fc2_ws=vm((fblk, half), BF16),
-        fc2_wr=vm((fblk, half), BF16),
+        fc2=vm((2, fblk, width), F32),
+        fc2_cs=vm((2, fblk, width), BF16),
+        fc2_cr=vm((2, fblk, width), BF16),
+        fc2_xs=vm((2, fblk, half), BF16),
+        fc2_xr=vm((2, fblk, half), BF16),
+        fc2_all=vm((2, 2, fblk, half), F32),
+        fc2_ys=vm((2, 2, fblk // 2, half), BF16),
+        fc2_yr=vm((2, 2, fblk // 2, half), BF16),
+        fc2_ws=vm((2, fblk // 2, half), BF16),
+        fc2_wr=vm((2, fblk // 2, half), BF16),
         fc1=vm((nb, 4 * blk, half), F32),
         fc1_cs=vm((nb, 4 * blk, half), BF16),
         fc1_cr=vm((nb, 4 * blk, half), BF16),
@@ -721,10 +745,10 @@
         fc1_zr=vm((nb, 2 * blk, half), BF16),
         fc1_ws=vm((nb, blk, half), BF16),
         fc1_wr=vm((nb, blk, half), BF16),
-        vec=vm((6, 8, width), F32),
-        vec_r=vm((5, 8, width), F32),
-        vec2=vm((6, 8, width), F32),
-        vec2_r=vm((5, 8, width), F32),
+        vec=vm((5, 8, width), F32),
+        vec_r=vm((4, 8, width), F32),
+        vec2=vm((5, 8, width), F32),
+        vec2_r=vm((4, 8, width), F32),
     )
     ANY = pl.BlockSpec(memory_space=pl.ANY)
     VMEM = pl.BlockSpec(memory_space=pltpu.VMEM)

time: 63.9 us -> 59.3 us (0.928); the launches traced: 63.7 us -> 58.3 us
  Pallas kernels: 63 us -> 57.5 us
    pallas_call x1, Pallas kernels: 61.2 us -> 55.6 us  [fused(): pl.pallas_call(functools.partial(kernel, (rows, width, ff, share)), out_s...]
where the time goes in v4:
time: 59.3 us; the launch traced here: 58.3 us
  Pallas kernels  57.5 us (97%)
  between operations  0.84 us (1%)
    pallas_call x1, Pallas kernels, fused(): pl.pallas_call(functools.partial(kernel, (rows, width, ff, share)), out_s...  55.6 us
    pallas_call x1, Pallas kernels, finish(): pl.pallas_call(functools.partial(finish_kernel, count), out_shape=tuple((...  1.83 us

profile of v4, /device:TPU:0, one launch (start us, length us, event | category | flops | bytes accessed | tf_op | source)
XLA Modules:
  0.0 58.3 jit_solution(1350129415133208002)
XLA Ops:
  0.7 55.6 %shard_map.408 = (bf16[1,64,768]{2,1,0:T(8,128)(2,1)S(1)}, f32[1,64,768]{2,1,0:T(8,128)S(1)}, f32[1,64,768]{2,1,0:T(8,128)S(1)}, f32[48,384]{1,0:T(8,128)S(1)}, ...) custom-call(bf16[1,64,768]{2,1,0:T(8,128)(2,1)} %queries.1, ...), custom_call_target="tpu_custom_call" | custom-call | flops 6000000000 | bytes 16000000 | tf_op jit(solution)/shard_map/pallas_call | solution.py:756
  56.3 1.8 %shard_map.409 = (bf16[1,64,768]{2,1,0:T(8,128)(2,1)}, f32[1,64,768]{2,1,0:T(8,128)}, f32[1,64,768]{2,1,0:T(8,128)}, f32[48,384]{1,0:T(8,128)}, f32[48,384]{1,0:...) custom-call(bf16[1,64,768]{2,1,0:T(8,128)(2,1)S(1)} %get-tuple-eleme, ...), custom_call_target="tpu_custom_call" | custom-call | tf_op jit(solution)/shard_map/pallas_call | solution.py:810

commit v5 on v4

--- a/solution.py
+++ b/solution.py
@@ -214,14 +214,11 @@
         s.hk[at, :] = hkl
         return hat, inv, hkl
 
-    def project(hq, hkq, hkl, at, low_at):
-        both = jnp.concatenate([hkl, hkq], axis=0)
-        k = dot(both, s.wk[...]).astype(BF16)
-        s.k[at, :] = k[:rows]
-        s.k[low_at, :] = k[rows:]
-        v = (dot(both, s.wv[...]) + b_value).astype(BF16)
-        s.v[at, :] = v[:rows]
-        s.v[low_at, :] = v[rows:]
+    def project(hk, at):
+        s.k[at, :] = dot(hk, s.wk[...]).astype(BF16)
+        s.v[at, :] = (dot(hk, s.wv[...]) + b_value).astype(BF16)
+
+    def project_query(hq, at):
         s.q[at, :] = (dot(hq, s.wq[...]) + b_query).astype(BF16)
 
     load_q()
@@ -249,7 +246,9 @@
     halves_b_fc1 = [
         jnp.where(x == k, b_fc1[:, :hid], b_fc1[:, hid:]) for k in range(2)
     ]
-    project(hq, hkq, hkl, own, low_own)
+    project(hkl, own)
+    project(hkq, low_own)
+    project_query(hq, own)
 
     def act_back(at):
         d_mlp = (scale_m * s.dy[0, at, :].astype(F32)).astype(BF16)
@@ -263,9 +262,11 @@
     got_p()
     got_q()
     _, _, hq_o, hkq_o = qry_half(s.ppos, other, low_other)
+    project(hkq_o, low_other)
+    project_query(hq_o, other)
     got_l()
     _, _, hkl_o = lat_half(other)
-    project(hq_o, hkq_o, hkl_o, other, low_other)
+    project(hkl_o, other)
     for wait in load_ok:
         wait()
 
@@ -327,10 +328,13 @@
         hidden(x * nb, b, halves_b_fc1[0])
         got_dp.append(push(s.dp.at[x * nb + b], s.dp_r.at[b], PY))
 
-    for b in range(nb):
-        zz, at = divmod(b * half, hid // 2)
-        s.act_t[zz, at:at + half, :] = s.act[x * nb + b].T
+    def turn(zz):
+        for k in range(nb // 2):
+            s.act_t[zz, k * half:(k + 1) * half, :] = s.act[x * nb + zz * (nb // 2) + k].T
+
+    turn(1 - z_low)
     got_act = push(s.act_t.at[1 - z_low], s.act_r, PZ1)
+    turn(z_low)
     s.h2_g[0, 0] = blocks(s.h2_t, c, y)
     s.h2_g[0, 1] = blocks(s.h2_t, 1 - c, y)
     s.hq_t[...] = s.hq[...].T
@@ -485,17 +489,6 @@
         (out_wo, out_wv, out_wk, out_wq)[i][...] = (
             s.sq[i, :blk, :] + s.sq_wr[i].astype(F32)
         )
-
-    tables = (s.vec, s.vec2)
-    landings = (s.vec_r, s.vec2_r)
-    got_v = [None] * 2
-
-    def vector_send(g, step, peer):
-        got_v[g] = push(tables[g].at[step], landings[g].at[step], peer)
-
-    def vector_add(g, step):
-        got_v[g]()
-        tables[g][step + 1] = tables[g][step] + landings[g][step]
 
     def hidden_others():
         for b in range(nb):
@@ -575,14 +568,23 @@
         out_dq[0] = s.d_resid[own, :] + normalise_back(s.dx[1, own, :], hat_q, inv_q)
 
     routes = (PZ2, PZ1, PY, PC)
+    got_v = [None] * 2
 
     def vector(g, step):
-        if step:
-            vector_add(g, step - 1)
+        if step == 0:
+            s.part[g, 0] = (s.vec, s.vec2)[g][0, :, mine]
+        else:
+            got_v[g]()
+            if step < 5:
+                s.part[g, step] = s.part[g, step - 1] + s.part_r[g, step - 1]
+        at = slice(g * 8, g * 8 + 8)
         if step < 4:
-            vector_send(g, step, routes[step])
+            got_v[g] = push(s.part.at[g, step], s.part_r.at[g, step], routes[step])
+        elif step == 4:
+            out_vec[at, mine] = s.part[g, 4]
+            got_v[g] = push(s.part.at[g, 4], s.part_r.at[g, 4], PX)
         else:
-            out_vec[g * 8:g * 8 + 8, :] = tables[g][4]
+            out_vec[at, theirs] = s.part_r[g, 4]
 
     pl.semaphore_wait(s.ready, z_links)
     V, K, Q, O = 1, 2, 3, 0
@@ -590,70 +592,72 @@
     d_resid()
     square_product(O)
     attention_back()
+    square_product(V)
+    square_core(O)
     fc1_product(0)
-    square_core(O)
-    square_product(V)
     attention_back_others()
+    fc1_product(1)
+    square_core(V)
     fc1_core(0)
-    fc1_product(1)
+    fc2_product(1)
+    mlp_sums()
+    fc1_product(2)
+    fc2_rest(1)
+    vector(0, 0)
+    fc2_core(1)
     square_product(K)
-    fc2_product(1)
-    square_core(V)
+    fc1_core(2)
+    fc2_product(0)
+    square_y(O)
+    fc2_rest(0)
     fc1_core(1)
+    fc1_product(3)
+    square_core(K)
     norms_back()
-    fc1_product(2)
-    square_core(K)
-    fc2_product(0)
-    fc2_rest(1)
-    fc2_core(1)
-    fc2_rest(0)
-    square_y(O)
-    fc1_core(2)
+    square_core_rest(V)
+    vector(1, 0)
+    fc1_core(3)
+    fc2_core(0)
+    square_y(V)
+    vector(0, 1)
+    square_z(O)
+    fc1_z(2)
+    square_product(Q)
+    fc2_swap(1)
+    fc1_z(3)
+    block_end()
+    vector(1, 1)
+    square_core(Q)
+    fc2_swap(0)
+    square_z(V)
+    square_core_rest(K)
     norms_end()
-    mlp_sums()
-    vector(0, 0)
-    square_core_rest(V)
-    square_y(V)
-    fc1_product(3)
-    square_core_rest(K)
-    fc2_core(0)
     square_y(K)
-    vector(1, 0)
-    fc1_z(2)
-    fc2_swap(1)
-    square_product(Q)
-    square_z(O)
-    square_z(V)
-    vector(0, 1)
-    fc2_swap(0)
-    square_core(Q)
+    fc2_y(1)
+    fc2_y(0)
+    vector(1, 2)
+    square_y(Q)
+    fc1_z(0)
+    vector(0, 2)
     square_z(K)
-    fc1_core(3)
-    fc2_y(1)
-    vector(1, 1)
-    fc2_y(0)
-    square_y(Q)
-    fc1_z(3)
+    vector(1, 3)
+    square_z(Q)
+    vector(0, 3)
+    vector(1, 4)
     square_end(O)
-    square_z(Q)
     fc1_z(1)
-    vector(0, 2)
-    vector(1, 2)
     fc1_end(2)
-    fc1_z(0)
+    fc2_end(1)
+    vector(0, 4)
+    fc1_end(3)
+    fc1_end(1)
+    square_end(V)
+    square_end(K)
+    vector(0, 5)
     fc2_end(0)
-    block_end()
-    square_end(K)
-    square_end(V)
-    vector(0, 3)
-    fc1_end(3)
-    vector(1, 3)
-    fc2_end(1)
-    fc1_end(1)
-    vector(0, 4)
-    vector(1, 4)
+    vector(1, 5)
+    fc1_end(0)
     square_end(Q)
-    fc1_end(0)
     for copy in sent:
         copy.wait_send()
 
@@ -745,10 +749,10 @@
         fc1_zr=vm((nb, 2 * blk, half), BF16),
         fc1_ws=vm((nb, blk, half), BF16),
         fc1_wr=vm((nb, blk, half), BF16),
-        vec=vm((5, 8, width), F32),
-        vec_r=vm((4, 8, width), F32),
-        vec2=vm((5, 8, width), F32),
-        vec2_r=vm((4, 8, width), F32),
+        part=vm((2, 5, 8, half), F32),
+        part_r=vm((2, 5, 8, half), F32),
+        vec=vm((1, 8, width), F32),
+        vec2=vm((1, 8, width), F32),
     )
     ANY = pl.BlockSpec(memory_space=pl.ANY)
     VMEM = pl.BlockSpec(memory_space=pltpu.VMEM)

time: 59.3 us -> 57.8 us (0.975); the launches traced: 58.3 us -> 57.6 us
  Pallas kernels: 57.5 us -> 56.8 us
    pallas_call x1, Pallas kernels: 55.6 us -> 54.9 us  [fused(): pl.pallas_call(functools.partial(kernel, (rows, width, ff, share)), out_s...]
where the time goes in v5:
time: 57.8 us; the launch traced here: 57.6 us
  Pallas kernels  56.8 us (98%)
  between operations  0.84 us (1%)
    pallas_call x1, Pallas kernels, fused(): pl.pallas_call(functools.partial(kernel, (rows, width, ff, share)), out_s...  54.9 us
    pallas_call x1, Pallas kernels, finish(): pl.pallas_call(functools.partial(finish_kernel, count), out_shape=tuple((...  1.83 us

profile of v5, /device:TPU:0, one launch (start us, length us, event | category | flops | bytes accessed | tf_op | source)
XLA Modules:
  0.0 57.6 jit_solution(13255636442952065922)
XLA Ops:
  0.7 54.9 %shard_map.408 = (bf16[1,64,768]{2,1,0:T(8,128)(2,1)S(1)}, f32[1,64,768]{2,1,0:T(8,128)S(1)}, f32[1,64,768]{2,1,0:T(8,128)S(1)}, f32[48,384]{1,0:T(8,128)S(1)}, ...) custom-call(bf16[1,64,768]{2,1,0:T(8,128)(2,1)} %queries.1, ...), custom_call_target="tpu_custom_call" | custom-call | flops 6000000000 | bytes 16000000 | tf_op jit(solution)/shard_map/pallas_call | solution.py:760
  55.6 1.8 %shard_map.409 = (bf16[1,64,768]{2,1,0:T(8,128)(2,1)}, f32[1,64,768]{2,1,0:T(8,128)}, f32[1,64,768]{2,1,0:T(8,128)}, f32[48,384]{1,0:T(8,128)}, f32[48,384]{1,0:...) custom-call(bf16[1,64,768]{2,1,0:T(8,128)(2,1)S(1)} %get-tuple-eleme, ...), custom_call_target="tpu_custom_call" | custom-call | tf_op jit(solution)/shard_map/pallas_call | solution.py:814

commit v6 on v5

--- a/solution.py
+++ b/solution.py
@@ -250,15 +250,18 @@
     project(hkq, low_own)
     project_query(hq, own)
 
-    def act_back(at):
-        d_mlp = (scale_m * s.dy[0, at, :].astype(F32)).astype(BF16)
-        s.dm[0, at, :] = d_mlp
-        for b in range(2 * nb):
-            s.d_act[b, at, :] = dot_t(d_mlp, s.w2[b * half:(b + 1) * half, :])
+    def act_back(at, first_block, blocks):
+        for b in range(blocks):
+            units = pl.ds(pl.multiple_of((first_block + b) * half, half), half)
+            s.d_act[first_block + b, at, :] = dot_t(s.dm[0, at, :], s.w2[units, :])
+
+    def d_mlp(at):
+        s.dm[0, at, :] = (scale_m * s.dy[0, at, :].astype(F32)).astype(BF16)
 
     load_dy()
     load_w2()
-    act_back(own)
+    d_mlp(own)
+    act_back(own, 0, 2 * nb)
     got_p()
     got_q()
     _, _, hq_o, hkq_o = qry_half(s.ppos, other, low_other)
@@ -312,7 +315,8 @@
     s.h2_g[1, 0] = blocks(s.h2_t, c, 1 - y)
     s.h2_g[1, 1] = blocks(s.h2_t, 1 - c, 1 - y)
     got_h2 = push(s.h2_g.at[1], s.h2_r, PY)
-    act_back(other)
+    d_mlp(other)
+    act_back(other, x * nb, nb)
     load_w1()
 
     def hidden(first_block, b, bias):
@@ -335,17 +339,14 @@
     turn(1 - z_low)
     got_act = push(s.act_t.at[1 - z_low], s.act_r, PZ1)
     turn(z_low)
-    s.h2_g[0, 0] = blocks(s.h2_t, c, y)
-    s.h2_g[0, 1] = blocks(s.h2_t, 1 - c, y)
-    s.hq_t[...] = s.hq[...].T
-    s.hk_t[...] = s.hk[...].T
-    s.att_t[...] = s.att[...].T
 
     got_c1, got_z1, got_w1 = [None] * nb, [None] * nb, [None] * nb
 
     def fc1_product(b):
         if b == 0:
             got_h2()
+            s.h2_g[0, 0] = blocks(s.h2_t, c, y)
+            s.h2_g[0, 1] = blocks(s.h2_t, 1 - c, y)
         got_dp[b]()
         right = jnp.concatenate([s.dp[x * nb + b], s.dp_r[b]], axis=0)
         left = jnp.concatenate([s.h2_g[0], s.h2_r[...]], axis=-1)
@@ -491,6 +492,7 @@
         )
 
     def hidden_others():
+        act_back(other, (1 - x) * nb, nb)
         for b in range(nb):
             hidden((1 - x) * nb, b, halves_b_fc1[1])
         s.branch[...] = branch
@@ -542,7 +544,14 @@
     def attention_back_others():
         heads_back(1 - x, theirs)
 
+    turned = set()
+
     def square_product(i):
+        kind = (0, 1, 1, 2)[i]
+        if kind not in turned:
+            turned.add(kind)
+            left, left_t = ((s.att, s.att_t), (s.hk, s.hk_t), (s.hq, s.hq_t))[kind]
+            left_t[...] = left[...].T
         square(
             i,
             (s.att_t, s.hk_t, s.hk_t, s.hq_t)[i],

time: 57.8 us -> 57.5 us (level)
  no operation moved by 1% of the time
where the time goes in v6:
time: 57.5 us; the launch traced here: 57.3 us
  Pallas kernels  56.5 us (98%)
  between operations  0.84 us (1%)
    pallas_call x1, Pallas kernels, fused(): pl.pallas_call(functools.partial(kernel, (rows, width, ff, share)), out_s...  54.7 us
    pallas_call x1, Pallas kernels, finish(): pl.pallas_call(functools.partial(finish_kernel, count), out_shape=tuple((...  1.83 us

profile of v6, /device:TPU:0, one launch (start us, length us, event | category | flops | bytes accessed | tf_op | source)
XLA Modules:
  0.0 57.3 jit_solution(6648637977948228667)
XLA Ops:
  0.7 54.7 %shard_map.408 = (bf16[1,64,768]{2,1,0:T(8,128)(2,1)S(1)}, f32[1,64,768]{2,1,0:T(8,128)S(1)}, f32[1,64,768]{2,1,0:T(8,128)S(1)}, f32[48,384]{1,0:T(8,128)S(1)}, ...) custom-call(bf16[1,64,768]{2,1,0:T(8,128)(2,1)} %queries.1, ...), custom_call_target="tpu_custom_call" | custom-call | flops 6000000000 | bytes 16000000 | tf_op jit(solution)/shard_map/pallas_call | solution.py:769
  55.4 1.8 %shard_map.409 = (bf16[1,64,768]{2,1,0:T(8,128)(2,1)}, f32[1,64,768]{2,1,0:T(8,128)}, f32[1,64,768]{2,1,0:T(8,128)}, f32[48,384]{1,0:T(8,128)}, f32[48,384]{1,0:...) custom-call(bf16[1,64,768]{2,1,0:T(8,128)(2,1)S(1)} %get-tuple-eleme, ...), custom_call_target="tpu_custom_call" | custom-call | tf_op jit(solution)/shard_map/pallas_call | solution.py:823

commit v7 on v6

--- a/solution.py
+++ b/solution.py
@@ -286,7 +286,7 @@
 
     for pair in range(2 * pairs):
         at = slice(pair * 2 * HEAD_DIM, (pair + 1) * 2 * HEAD_DIM)
-        raw = dot_t(stack(s.q[:, at]), s.k[:, at]) * scale
+        raw = dot_t(stack(s.q[:, at] * scale), s.k[:, at])
         scores = jnp.where(ok, raw, -1e30)
         peak = jnp.max(scores, axis=-1, keepdims=True)
         weight = jnp.exp(scores - peak)
@@ -605,11 +605,11 @@
     square_core(O)
     fc1_product(0)
     attention_back_others()
-    fc1_product(1)
     square_core(V)
     fc1_core(0)
     fc2_product(1)
     mlp_sums()
+    fc1_product(1)
     fc1_product(2)
     fc2_rest(1)
     vector(0, 0)
@@ -625,8 +625,8 @@
     norms_back()
     square_core_rest(V)
     vector(1, 0)
+    fc2_core(0)
     fc1_core(3)
-    fc2_core(0)
     square_y(V)
     vector(0, 1)
     square_z(O)
@@ -651,12 +651,12 @@
     square_z(K)
     vector(1, 3)
     square_z(Q)
-    vector(0, 3)
     vector(1, 4)
     square_end(O)
     fc1_z(1)
     fc1_end(2)
     fc2_end(1)
+    vector(0, 3)
     vector(0, 4)
     fc1_end(3)
     fc1_end(1)

time: 57.5 us -> 57.6 us (level)
  no operation moved by 1% of the time
where the time goes in v7:
time: 57.6 us; the launch traced here: 57.4 us
  Pallas kernels  56.6 us (98%)
  between operations  0.84 us (1%)
    pallas_call x1, Pallas kernels, fused(): pl.pallas_call(functools.partial(kernel, (rows, width, ff, share)), out_s...  54.8 us
    pallas_call x1, Pallas kernels, finish(): pl.pallas_call(functools.partial(finish_kernel, count), out_shape=tuple((...  1.83 us

profile of v7, /device:TPU:0, one launch (start us, length us, event | category | flops | bytes accessed | tf_op | source)
XLA Modules:
  0.0 57.4 jit_solution(10550606772029450906)
XLA Ops:
  0.7 54.8 %shard_map.408 = (bf16[1,64,768]{2,1,0:T(8,128)(2,1)S(1)}, f32[1,64,768]{2,1,0:T(8,128)S(1)}, f32[1,64,768]{2,1,0:T(8,128)S(1)}, f32[48,384]{1,0:T(8,128)S(1)}, ...) custom-call(bf16[1,64,768]{2,1,0:T(8,128)(2,1)} %queries.1, ...), custom_call_target="tpu_custom_call" | custom-call | flops 6000000000 | bytes 16000000 | tf_op jit(solution)/shard_map/pallas_call | solution.py:769
  55.5 1.8 %shard_map.409 = (bf16[1,64,768]{2,1,0:T(8,128)(2,1)}, f32[1,64,768]{2,1,0:T(8,128)}, f32[1,64,768]{2,1,0:T(8,128)}, f32[48,384]{1,0:T(8,128)}, f32[48,384]{1,0:...) custom-call(bf16[1,64,768]{2,1,0:T(8,128)(2,1)S(1)} %get-tuple-eleme, ...), custom_call_target="tpu_custom_call" | custom-call | tf_op jit(solution)/shard_map/pallas_call | solution.py:823
